TPU v7x, 128 devices: a whole 4x4x4 slice. The times are simulated.
128 devices in a mesh: dp: 8 (over y, z_lo), tok: 16 (over x, z_hi, core).
Axes of the slice: x: 4, y: 4, z: 4 (z_hi: 2, z_lo: 2; z = z_hi * 2 + z_lo), core: 2. Of those that a mesh axis runs over, the one named last changes fastest.
Arguments:
- embeddings: bfloat16 [2560, 1024, 256], P('dp', 'tok'), may hold values from -6 to 6
- projection: bfloat16 [1024, 32], P('tok'), may hold values from -0.01171875 to 0.01171875
- mlp_weight: bfloat16 [32768, 1024], P('tok'), may hold values from -0.03125 to 0.03125
- mlp_bias: float32 [1024], replicated, may hold values from -1 to 1
- upstream: bfloat16 [2560, 1024], P('dp'), may hold values from -24 to 24
Outputs:
- grad_embeddings: bfloat16 [2560, 1024, 256], P('dp', 'tok')
- grad_weight: float32 [32768, 1024], P(('tok', 'dp'))
- grad_projection: float32 [1024, 32], P('tok')
- grad_bias: float32 [1024], replicated
All inputs are finite; a program needn't handle non-finite values.
Results may differ from a plain program's by a relative error of at most 0.034.
Values may be sent and summed in bfloat16 or wider, within the bound.
No kernel may reach another device: no remote copies, remote signals or barrier semaphores. Data moves between devices by JAX's collectives and lax.ppermute only.
A program may use at most 192 MiB of HBM per device.

v0:
```python
import jax
import jax.numpy as jnp
from jax import lax
from jax.sharding import PartitionSpec as P


def silu_grad(value):
    sig = jax.nn.sigmoid(value)
    return sig * (1.0 + value * (1.0 - sig))


def per_device(embeddings, projection, mlp_weight, mlp_bias, upstream):
    examples, tokens, width = embeddings.shape
    rank = projection.shape[1]
    comp_part = jnp.einsum(
        "tk,etd->ekd", projection, embeddings, preferred_element_type=jnp.float32
    )
    compressed = lax.psum(comp_part.astype(jnp.bfloat16), "tok")
    field = jnp.einsum(
        "etd,ekd->etk", embeddings, compressed, preferred_element_type=jnp.float32
    ).astype(jnp.bfloat16)
    flat = field.reshape(examples, tokens * rank)
    hidden_part = jnp.dot(flat, mlp_weight, preferred_element_type=jnp.float32)
    pre = lax.psum(hidden_part.astype(jnp.bfloat16), "tok").astype(jnp.float32) + mlp_bias
    grad_pre = (upstream.astype(jnp.float32) * silu_grad(pre)).astype(jnp.bfloat16)
    dflat = lax.dot_general(
        grad_pre, mlp_weight, (((1,), (1,)), ((), ())), preferred_element_type=jnp.float32
    ).astype(jnp.bfloat16)
    dfield = dflat.reshape(examples, tokens, rank)
    dcomp_part = jnp.einsum("etk,etd->ekd", dfield, embeddings, preferred_element_type=jnp.float32)
    dcomp = lax.psum(dcomp_part.astype(jnp.bfloat16), "tok")
    grad_x = jnp.einsum("etk,ekd->etd", dfield, compressed, preferred_element_type=jnp.float32)
    grad_x = grad_x + jnp.einsum(
        "tk,ekd->etd", projection, dcomp, preferred_element_type=jnp.float32
    )
    proj_local = jnp.einsum("etd,ekd->tk", embeddings, dcomp, preferred_element_type=jnp.float32)
    bias_local = jnp.sum(grad_pre.astype(jnp.float32), axis=0)
    grad_w = lax.psum_scatter(
        lax.dot_general(
            flat, grad_pre, (((0,), (0,)), ((), ())), preferred_element_type=jnp.float32
        ).astype(jnp.bfloat16),
        "dp",
        scatter_dimension=0,
        tiled=True,
    ).astype(jnp.float32)
    grad_p, grad_b = lax.psum((proj_local, bias_local), "dp")
    return (grad_x.astype(jnp.bfloat16), grad_w, grad_p, grad_b)


def solution(mesh):
    in_specs = (P("dp", "tok", None), P("tok", None), P("tok", None), P(), P("dp", None))
    out_specs = (P("dp", "tok", None), P(("tok", "dp"), None), P("tok", None), P())
    return jax.shard_map(
        per_device, mesh=mesh, in_specs=in_specs, out_specs=out_specs, check_vma=False
    )
```

profile of v0, /device:TPU:4, one launch (start us, length us, event | category | flops | bytes accessed | tf_op | source)
XLA Modules:
  0.0 615.8 jit_solution(6736574161487299365)
XLA Ops:
  7.2 0.0 copy-start
  7.2 0.0 all-reduce.5.cloned.1.call-start
  7.2 0.6 copy-done
  7.9 7.9 %convert_bitcast_fusion = bf16[320,32,256]{2,1,0:T(8,128)(2,1)} fusion(bf16[320,64,256]{2,1,0:T(8,128)(2,1)} %param.5, bf16[64,32]{0,1:T(8,128)(2,1)S(1)} %copy-done), kind=kOutput, calls=%fused_computation.2 | convolution fusion | flops 338165760 | bytes 15732736 | tf_op jit(solution)/shard_map/tk,etd->ekd/dot_general | solution.py:15
  15.8 0.0 all-reduce.5.cloned.1.call-update
  15.8 0.0 all-reduce.7.cloned.1.call-start
  15.8 152.0 %all-reduce.5.cloned.1.call-done = bf16[320,32,256]{2,1,0:T(8,128)(2,1)} async-done(((bf16[320,32,256]{2,1,0:T(8,128)(2,1)}), bf16[320,32,256]{2,1,0:T(8,128)(2,1)}) %all-reduce.5.cloned.1.call-update) | async-done | bytes 5242896 | tf_op jit(solution)/shard_map/psum | solution.py:18
  167.9 8.4 %convert_bitcast_fusion.1 = bf16[320,64,32]{1,2,0:T(8,128)(2,1)S(1)} fusion(bf16[320,32,256]{2,1,0:T(8,128)(2,1)} %all-reduce.5.cloned.1.call-done, bf16[320,64,256]{2,1,0:T(8,128)(2,1)} %param.5), kind=kOutput, calls=%fused_computation.6 | convolution fusion | flops 336199680 | bytes 17039360 | tf_op jit(solution)/shard_map/etd,ekd->etk/dot_general | solution.py:19
  176.3 5.7 copy.11
  182.0 0.0 copy-start.1
  182.0 5.1 convolution_convert_fusion.3
  187.1 0.0 all-reduce.7.cloned.1.call-update
  187.1 0.2 all-reduce.9.cloned.1.call-start
  187.4 137.2 %all-reduce.7.cloned.1.call-done = bf16[320,1024]{1,0:T(8,128)(2,1)} async-done(((bf16[320,1024]{1,0:T(8,128)(2,1)}), bf16[320,1024]{1,0:T(8,128)(2,1)}) %all-reduce.7.cloned.1.call-update) | async-done | bytes 655376 | tf_op jit(solution)/shard_map/psum | solution.py:24
  324.6 0.0 copy-done.1
  324.6 0.0 copy-done.2
  324.6 1.7 convert_reduce_fusion
  326.3 3.8 convolution_convert_fusion.2
  330.1 1.6 copy.12
  331.7 6.7 %copy.13 = bf16[320,64,32]{1,2,0:T(8,128)(2,1)S(1)} copy(bf16[320,64,32]{0,2,1:T(8,128)(2,1)} %bitcast.35) | data formatting | bytes 2621440 | tf_op jit(solution)/shard_map/reshape | solution.py:29
  338.3 8.0 %convolution_convert_fusion.1 = bf16[320,32,256]{2,1,0:T(8,128)(2,1)} fusion(bf16[320,64,32]{1,2,0:T(8,128)(2,1)S(1)} %copy.13, bf16[320,64,256]{2,1,0:T(8,128)(2,1)} %param.5), kind=kOutput, calls=%fused_computation.4 | convolution fusion | flops 338165760 | bytes 17039360 | tf_op jit(solution)/shard_map/etk,etd->ekd/dot_general | solution.py:30
  346.3 0.0 all-reduce.9.cloned.1.call-update
  346.4 0.0 reduce-scatter.2.cloned.1.call-start
  346.4 5.7 convolution_convert_fusion
  352.1 0.0 reduce-scatter.2.cloned.1.call-update
  352.2 154.2 %all-reduce.9.cloned.1.call-done = bf16[320,32,256]{2,1,0:T(8,128)(2,1)} async-done(((bf16[320,32,256]{2,1,0:T(8,128)(2,1)}), bf16[320,32,256]{2,1,0:T(8,128)(2,1)}) %all-reduce.9.cloned.1.call-update) | async-done | bytes 5242896 | tf_op jit(solution)/shard_map/psum | solution.py:31
  506.4 8.4 %convolution_bitcast_fusion = f32[64,32]{0,1:T(8,128)S(1)} fusion(bf16[320,32,256]{2,1,0:T(8,128)(2,1)} %all-reduce.9.cloned.1.call-done, bf16[320,64,256]{2,1,0:T(8,128)(2,1)} %param.5), kind=kOutput, calls=%fused_computation.10 | convolution fusion | flops 335544320 | bytes 15736832 | tf_op jit(solution)/shard_map/etd,ekd->tk/dot_general | solution.py:36
  514.8 35.6 %all-reduce = (f32[64,32]{0,1:T(8,128)}, f32[1024]{0:T(1024)}) all-reduce(f32[64,32]{0,1:T(8,128)S(1)} %convolution_bitcast_fusion, f32[1024]{0:T(1024)S(1)} %get-tuple-element.6), channel_id=1, replica_groups=mesh['dp'=8,'tok'=16] {'dp'}, use_global_device_ids=true, to_apply=%region_4.0 | all-reduce | flops 3072 | bytes 24576 | tf_op jit(solution)/shard_map/psum | solution.py:46
  550.4 12.5 %fusion.1 = f32[320,256,64]{1,2,0:T(8,128)} fusion(bf16[320,32,256]{2,1,0:T(8,128)(2,1)} %all-reduce.9.cloned.1.call-done, bf16[64,32]{0,1:T(8,128)(2,1)S(1)} %copy-done), kind=kOutput, calls=%fused_computation.11 | convolution fusion | flops 335544320 | bytes 26218496 | tf_op jit(solution)/shard_map/tk,ekd->etd/dot_general | solution.py:33
  562.9 14.6 %fusion = bf16[320,64,256]{2,1,0:T(8,128)(2,1)} fusion(f32[320,256,64]{1,2,0:T(8,128)} %fusion.1, bf16[320,64,32]{1,2,0:T(8,128)(2,1)S(1)} %copy.13, bf16[320,32,256]{2,1,0:T(8,128)(2,1)} %all-reduce.5.cloned.1.call-done), kind=kOutput, calls=%fused_computation.1 | convolution fusion | flops 346030080 | bytes 38010880 | tf_op jit(solution)/shard_map/etk,ekd->etd/dot_general | solution.py:32
  577.5 29.7 %reduce-scatter.2.cloned.1.call-done = bf16[256,1024]{1,0:T(8,128)(2,1)} async-done(((bf16[2048,1024]{1,0:T(8,128)(2,1)}), bf16[256,1024]{1,0:T(8,128)(2,1)}) %reduce-scatter.2.cloned.1.call-update) | async-done | bytes 524304 | tf_op jit(solution)/shard_map/reduce_scatter | solution.py:38
  607.2 2.1 convert_element_type.54
  (1 shorter events, 0.0 us)
Async XLA Ops:
  7.2 0.7 copy-start
  7.2 160.7 %all-reduce.5.cloned.1.call-start = ((), (), s32[]{:S(2)}) async-start(), calls=%async_computation.1 | async-start | bytes 10485760 | tf_op jit(solution)/shard_map/psum | solution.py:18
  15.8 308.8 %all-reduce.7.cloned.1.call-start = ((), (), s32[]{:S(2)}) async-start(), calls=%async_computation.2 | async-start | bytes 1310720 | tf_op jit(solution)/shard_map/psum | solution.py:24
  182.0 142.6 %copy-start.1 = (bf16[320,1024]{1,0:T(8,128)(2,1)S(1)}, bf16[320,1024]{1,0:T(8,128)(2,1)}, u32[]{:S(2)}) copy-start(bf16[320,1024]{1,0:T(8,128)(2,1)} %param.9) | copy-start | bytes 1966084
  182.0 142.6 %copy-start.2 = (f32[1024]{0:T(1024)S(1)}, f32[1024]{0:T(1024)}, u32[]{:S(2)}) copy-start(f32[1024]{0:T(1024)} %param.8) | copy-start | bytes 12292
  187.1 319.3 %all-reduce.9.cloned.1.call-start = ((), (), s32[]{:S(2)}) async-start(), calls=%async_computation.3 | async-start | bytes 10485760 | tf_op jit(solution)/shard_map/psum | solution.py:31
  346.4 260.8 %reduce-scatter.2.cloned.1.call-start = ((), (), s32[]{:S(2)}) async-start(), calls=%async_computation.4 | async-start | bytes 4718592 | tf_op jit(solution)/shard_map/reduce_scatter | solution.py:38
Sparse Core Ops, SparseCore 0:
  15.9 151.9 all-reduce.4
  187.3 137.2 all-reduce.6
  346.5 159.8 all-reduce.8
  508.8 98.3 reduce-scatter.1
where the time goes:
time: 618 us; the launch traced here: 616 us
  waiting for transfers between devices  473 us (77%)
  matrix products  74.3 us (12%)
  blocking collectives  35.6 us (6%)
  local copies, waits for them, and re-layouts  14.6 us (2%)
  between operations  13.8 us (2%)
    psum x1, waiting for transfers between devices, per_device(): dcomp = lax.psum(dcomp_part.astype(jnp.bfloat16), 'tok')  154 us
    psum x1, waiting for transfers between devices, per_device(): compressed = lax.psum(comp_part.astype(jnp.bfloat16), 'tok')  152 us
    psum x1, waiting for transfers between devices, per_device(): lax.psum(hidden_part.astype(jnp.bfloat16), 'tok').astype(jnp.float32)  137 us
    psum x1, blocking collectives, per_device(): grad_p, grad_b = lax.psum((proj_local, bias_local), 'dp')  35.6 us
    reduce_scatter x1, waiting for transfers between devices, per_device(): lax.psum_scatter(lax.dot_general(flat, grad_pre, (((0,), (0,)), ((), ()))...  29.7 us
    dot_general x1, matrix products, per_device(): jnp.einsum('etk,ekd->etd', dfield, compressed, preferred_element_type=jnp...  14.6 us
    dot_general x1, matrix products, per_device(): jnp.einsum('tk,ekd->etd', projection, dcomp, preferred_element_type=jnp.f...  12.5 us
  transfers between devices with their start and end apart: 4, of which 4 were waited for; matrix products, arithmetic and copies ran while one was open for 7% of the time, Pallas kernels for 0%

commit v1 on v0

v1 whole, which is shorter than its diff:
```python
import jax, jax.numpy as jnp
from jax import lax
from jax.experimental import pallas as pl
from jax.experimental.pallas import tpu as pltpu
from jax.sharding import PartitionSpec as P
f32=jnp.float32; bf=jnp.bfloat16
EB=16
T,K,D,H=64,32,256,1024
VM=pltpu.CompilerParams(vmem_limit_bytes=32*1024*1024)
def whole(shape): return pl.BlockSpec(shape, lambda i,*_: (0,)*len(shape))
def xspec(): return pl.BlockSpec((EB,T,D), lambda i,tbl,blk: (blk[0]+i,0,0))

def k1_body(tbl, blk, x, pt4, out):
    i=pl.program_id(0)
    for g in range(EB//4):
        r=jnp.dot(pt4[...], x[4*g:4*g+4].reshape(4*T,D), preferred_element_type=f32).astype(bf)
        for j in range(4):
            out[tbl[i*EB+4*g+j]]=r[K*j:K*j+K]
def k1(x,pt4,tbl,blk):
    n=tbl.shape[0]
    return pl.pallas_call(k1_body, out_shape=jax.ShapeDtypeStruct((n,K,D),bf),
        grid_spec=pltpu.PrefetchScalarGridSpec(num_scalar_prefetch=2, grid=(n//EB,),
            in_specs=[xspec(), whole((4*K,4*T))], out_specs=whole((n,K,D))),
        compiler_params=VM, name="compress")(tbl,blk,x,pt4)

def k2_body(tbl, blk, perm, x, comp, flat, flatp, sc):
    i=pl.program_id(0)
    for e in range(EB):
        c=comp[tbl[i*EB+e]]
        c4=jnp.concatenate([c]*4,axis=0)
        sc[T*e:T*e+T,:]=lax.dot_general(x[e],c4,(((1,),(1,)),((),())),preferred_element_type=f32)
    lane=lax.broadcasted_iota(jnp.int32,(EB,128),1)>>5
    for g in range(T//4):
        acc=sc[pl.ds(4*g,EB,stride=T),:]
        for j in range(1,4):
            acc=jnp.where(lane==j, sc[pl.ds(4*g+j,EB,stride=T),:], acc)
        flat[:,128*g:128*g+128]=acc.astype(bf)
    for j in range(8):
        flatp[:,256*j:256*j+256]=flat[:,pl.ds(pl.multiple_of(perm[j]*256,256),256)]
def k2(x,comp,tbl,blk,perm):
    n=tbl.shape[0]
    fs=pl.BlockSpec((EB,T*K), lambda i,*_: (i,0))
    return pl.pallas_call(k2_body, out_shape=[jax.ShapeDtypeStruct((n,T*K),bf)]*2,
        grid_spec=pltpu.PrefetchScalarGridSpec(num_scalar_prefetch=3, grid=(n//EB,),
            in_specs=[pl.BlockSpec((EB,T,D), lambda i,tbl,blk,perm: (blk[0]+i,0,0)), whole((n,K,D))], out_specs=[fs,fs],
            scratch_shapes=[pltpu.VMEM((EB*T,128),f32)]),
        compiler_params=VM, name="field")(tbl,blk,perm,x,comp)

def expand(df, sc):
    lane=lax.broadcasted_iota(jnp.int32,(EB,128),1)>>5
    for g in range(T//4):
        v=df[:,128*g:128*g+128].astype(f32)
        for j in range(4):
            sc[pl.ds(4*g+j,EB,stride=T),:]=jnp.where(lane==j,v,0.0)

def k3_body(tbl, blk, x, df, out, sc):
    i=pl.program_id(0)
    expand(df,sc)
    for e in range(EB):
        s=sc[T*e:T*e+T,:].astype(bf)
        r=lax.dot_general(s,x[e],(((0,),(0,)),((),())),preferred_element_type=f32)
        out[tbl[i*EB+e]]=(r[:K]+r[K:2*K]+r[2*K:3*K]+r[3*K:]).astype(bf)
def k3(x,df,tbl,blk):
    n=tbl.shape[0]
    return pl.pallas_call(k3_body, out_shape=jax.ShapeDtypeStruct((n,K,D),bf),
        grid_spec=pltpu.PrefetchScalarGridSpec(num_scalar_prefetch=2, grid=(n//EB,),
            in_specs=[xspec(), pl.BlockSpec((EB,T*K), lambda i,*_: (i,0))], out_specs=whole((n,K,D)),
            scratch_shapes=[pltpu.VMEM((EB*T,128),f32)]),
        compiler_params=VM, name="grad_compress")(tbl,blk,x,df)

def k4_body(tbl, blk, df, comp, dcomp, pexp, gx_in, gx, sc):
    i=pl.program_id(0)
    expand(df,sc)
    p=pexp[...]
    for e in range(EB):
        s=jnp.concatenate([sc[T*e:T*e+T,:].astype(bf),p],axis=1)
        c=comp[tbl[i*EB+e]]; d=dcomp[tbl[i*EB+e]]
        w=jnp.concatenate([c]*4+[d]*4,axis=0)
        gx[e]=jnp.dot(s,w,preferred_element_type=f32).astype(bf)
def k4(df,comp,dcomp,pexp,gx,shape,tbl,blk):
    n=tbl.shape[0]
    in_specs=[pl.BlockSpec((EB,T*K), lambda i,*_: (i,0)), whole((n,K,D)), whole((n,K,D)), whole((T,128))]
    args=[df,comp,dcomp,pexp]
    body=k4_body; alias={}
    if gx is None:
        def body(tbl, blk, df, comp, dcomp, pexp, gx, sc): k4_body(tbl,blk,df,comp,dcomp,pexp,None,gx,sc)
    else:
        in_specs.append(pl.BlockSpec(memory_space=pl.ANY)); args.append(gx); alias={6:0}
    return pl.pallas_call(body, out_shape=jax.ShapeDtypeStruct(shape,bf),
        grid_spec=pltpu.PrefetchScalarGridSpec(num_scalar_prefetch=2, grid=(n//EB,),
            in_specs=in_specs, out_specs=xspec(),
            scratch_shapes=[pltpu.VMEM((EB*T,128),f32)]),
        input_output_aliases=alias,
        compiler_params=VM, name="grad_tokens")(tbl,blk,*args)

def k5_body(tbl, blk, x, dcomp, gp):
    i=pl.program_id(0)
    @pl.when(i==0)
    def _(): gp[...]=jnp.zeros_like(gp)
    acc=gp[...]
    for e in range(EB):
        acc=acc+lax.dot_general(dcomp[tbl[i*EB+e]],x[e],(((1,),(1,)),((),())),preferred_element_type=f32)
    gp[...]=acc
def k5(x,dcomp,tbl,blk):
    n=tbl.shape[0]
    return pl.pallas_call(k5_body, out_shape=jax.ShapeDtypeStruct((K,T),f32),
        grid_spec=pltpu.PrefetchScalarGridSpec(num_scalar_prefetch=2, grid=(n//EB,),
            in_specs=[xspec(), whole((n,K,D))], out_specs=whole((K,T))),
        compiler_params=VM, name="grad_projection")(tbl,blk,x,dcomp)


NCH = 2
ORDERS = (("ABZ", "BAZ"), ("ABZ", "BAZ"))
DP_ORDERS = ("ABZ", "BAZ")


def tok_bits(i):
    x = i // 4
    g = x ^ (x >> 1)
    return {"A": g & 1, "B": g >> 1, "Z": (i >> 1) & 1}


def tok_flip(i, d):
    x = i // 4
    return {"A": (x ^ 1) * 4 + i % 4, "B": (3 - x) * 4 + i % 4, "Z": i ^ 2, "C": i ^ 1}[d]


def dp_bits(i):
    y = i // 2
    g = y ^ (y >> 1)
    return {"A": g & 1, "B": g >> 1, "Z": i & 1}


def dp_flip(i, d):
    y = i // 2
    return {"A": (y ^ 1) * 2 + i % 2, "B": (3 - y) * 2 + i % 2, "Z": i ^ 1}[d]


def place(bits, order):
    return bits[order[0]] * 4 + bits[order[1]] * 2 + bits[order[2]]


def tok_swap(x, step, orders):
    if step == "C":
        pairs = [(i, tok_flip(i, "C")) for i in range(16)]
    else:
        pairs = [(i, tok_flip(i, orders[i & 1][step])) for i in range(16)]
    return lax.ppermute(x, "tok", pairs)


def dp_swap(x, step):
    pairs = []
    for d in range(8):
        for t in range(16):
            pairs.append((d * 16 + t, dp_flip(d, DP_ORDERS[t & 1][step]) * 16 + t))
    return lax.ppermute(x, ("dp", "tok"), pairs)


def add(a, b, dtype=jnp.bfloat16):
    return (a.astype(jnp.float32) + b.astype(jnp.float32)).astype(dtype)


def reduce_scatter(x, got, swap):
    for step in range(3):
        h = x.shape[0] // 2
        if got is None:
            keep, send = x[:h], x[h:]
        else:
            keep, send = add(x[:h], got[:h]), add(x[h:], got[h:])
        got = swap(send, step)
        x = keep
    return x, got


def all_gather(x, swap):
    for step in (2, 1, 0):
        x = jnp.concatenate([x, swap(x, step)], axis=0)
    return x


def all_sum(x, swap):
    for step in range(3):
        x = add(x, swap(x, step), x.dtype)
    return x


def silu_grad(value):
    sig = jax.nn.sigmoid(value)
    return sig * (1.0 + value * (1.0 - sig))


def per_device(embeddings, projection, mlp_weight, mlp_bias, upstream):
    examples = embeddings.shape[0]
    half = examples // NCH // 2
    part = half // 8
    tok = lax.axis_index("tok")
    dp = lax.axis_index("dp")
    core = tok & 1
    bits = tok_bits(tok)
    dbits = dp_bits(dp)
    own = jnp.where(core == 0, place(dbits, DP_ORDERS[0]), place(dbits, DP_ORDERS[1]))
    owners = []
    for order in DP_ORDERS:
        table = [0] * 8
        for d in range(8):
            table[place(dp_bits(d), order)] = d
        owners.append(table)
    owners = jnp.asarray(owners, jnp.int32)[core]
    perm = owners[own ^ jnp.arange(8)].astype(jnp.int32)

    pt4 = jnp.kron(jnp.eye(4, dtype=bf), projection.T)
    lanes = (jnp.arange(128)[None] // K) == (jnp.arange(T)[:, None] % 4)
    pexp = jnp.where(lanes, jnp.tile(projection, (1, 4)), 0).astype(bf)

    e = jnp.arange(half, dtype=jnp.int32)
    tables, blocks, swaps = [], [], []
    for c in range(NCH):
        orders = ORDERS[c]
        tabs = [((e // part) ^ place(bits, orders[h])) * part + e % part for h in range(2)]
        tables.append((jnp.where(core == 0, tabs[0], tabs[1]), jnp.where(core == 0, tabs[1], tabs[0])))
        first = c * 2 * half // EB
        blocks.append(((first + core * (half // EB)).reshape(1), (first + (1 - core) * (half // EB)).reshape(1)))
        swaps.append(lambda x, step, orders=orders: tok_swap(x, step, orders))

    def total(c, kernel):
        other = kernel(1)
        got = swaps[c](other, "C")
        mine = kernel(0)
        x = all_gather(add(*reduce_scatter(mine, got, swaps[c])), swaps[c])
        return x, swaps[c](x, "C")

    comp, dcomp, flat, flatp, gpre = [], [], [], [], []
    for c in range(NCH):
        with jax.named_scope("compressed"):
            comp.append(total(c, lambda h: k1(embeddings, pt4, tables[c][h], blocks[c][h])))
    for c in range(NCH):
        with jax.named_scope("pre"):
            fl, flp, hp = [None, None], [None, None], [None, None]
            for h in (0, 1):
                fl[h], flp[h] = k2(embeddings, comp[c][h], tables[c][h], blocks[c][h], perm)
                hp[h] = jnp.dot(fl[h], mlp_weight, preferred_element_type=f32).astype(bf)
            x = add(hp[0], swaps[c](hp[1], "C"))
            x = all_sum(x, swaps[c])
            pre = [x, swaps[c](x, "C")]
            up = upstream.reshape(NCH, 2, half, H)[c]
            gp = []
            for h in (0, 1):
                u = lax.dynamic_index_in_dim(up, core if h == 0 else 1 - core, 0, keepdims=False)
                gp.append((u.astype(f32) * silu_grad(pre[h].astype(f32) + mlp_bias)).astype(bf))
            flat.append(fl)
            flatp.append(flp)
            gpre.append(gp)
    dflat = []
    for c in range(NCH):
        with jax.named_scope("grad_compressed"):
            df = [
                lax.dot_general(g, mlp_weight, (((1,), (1,)), ((), ())), preferred_element_type=f32).astype(bf)
                for g in gpre[c]
            ]
            dflat.append(df)
            dcomp.append(total(c, lambda h: k3(embeddings, df[h], tables[c][h], blocks[c][h])))
    with jax.named_scope("grad_weight"):
        rows = jnp.concatenate([f for fs in flatp for f in fs], axis=0)
        cols = jnp.concatenate([g for gs in gpre for g in gs], axis=0)
        gw = lax.dot_general(rows, cols, (((0,), (0,)), ((), ())), preferred_element_type=f32).astype(bf)
        a, b = reduce_scatter(gw, None, dp_swap)
        grad_w = a.astype(f32) + b.astype(f32)
        bias = jnp.sum(cols.astype(f32), axis=0)
    with jax.named_scope("grad_projection"):
        gp = sum(k5(embeddings, dcomp[c][h], tables[c][h], blocks[c][h]) for c in range(NCH) for h in (0, 1))
        both = jnp.concatenate([gp.reshape(T * K // 128, 128), bias.reshape(H // 128, 128)], axis=0)
        both = all_sum(both, dp_swap)
        grad_p = both[: T * K // 128].reshape(K, T).T
        grad_b = both[T * K // 128 :].reshape(H)
    with jax.named_scope("grad_embeddings"):
        gx = None
        for c in range(NCH):
            for h in (0, 1):
                gx = k4(dflat[c][h], comp[c][h], dcomp[c][h], pexp, gx, embeddings.shape, tables[c][h], blocks[c][h])
    return gx, grad_w, grad_p, grad_b


def solution(mesh):
    in_specs = (P("dp", "tok", None), P("tok", None), P("tok", None), P(), P("dp", None))
    out_specs = (P("dp", "tok", None), P(("tok", "dp"), None), P("tok", None), P())
    return jax.shard_map(
        per_device, mesh=mesh, in_specs=in_specs, out_specs=out_specs, check_vma=False
    )
```

time: 618 us -> 319 us (0.52)
  waiting for transfers between devices: 473 us -> 82.9 us
  starting transfers between devices: 0.35 us -> 91.7 us
  Pallas kernels: 0 us -> 73.1 us
  matrix products: 74.3 us -> 13.6 us
  blocking collectives: 35.6 us -> 0 us
  local copies, waits for them, and re-layouts: 14.6 us -> 34.3 us
  other arithmetic: 3.85 us -> 17 us
  between operations: 13.8 us -> 1.83 us
    psum x3 -> x0, waiting for transfers between devices: 444 us -> none  [the longest x1 154 us: per_device(): dcomp = lax.psum(dcomp_part.astype(jnp.bfloat16), 'tok')]
    ppermute x0 -> x48, starting transfers between devices: none -> 91.7 us  [the longest x42 81.5 us: tok_swap(): return lax.ppermute(x, 'tok', pairs)]
    ppermute x0 -> x48, waiting for transfers between devices: none -> 82.9 us  [the longest x42 71.5 us: tok_swap(): return lax.ppermute(x, 'tok', pairs)]
    pallas_call x0 -> x20, Pallas kernels: none -> 73.1 us  [the longest x4 22.7 us: k4(): pl.pallas_call(body, out_shape=jax.ShapeDtypeStruct(shape, bf), grid_spec...]
    dot_general x9, matrix products: 74.3 us -> 13.6 us  [the longest x4 7.8 us: per_device(): lax.dot_general(g, mlp_weight, (((1,), (1,)), ((), ())), preferred_elemen...]
    psum x1 -> x0, blocking collectives: 35.6 us -> none  [per_device(): grad_p, grad_b = lax.psum((proj_local, bias_local), 'dp')]
    reduce_scatter x1 -> x0, waiting for transfers between devices: 29.7 us -> none  [per_device(): lax.psum_scatter(lax.dot_general(flat, grad_pre, (((0,), (0,)), ((), ()))...]
    unnamed x6 -> x102, local copies, waits for them, and re-layouts: 0.66 us -> 30.1 us
  transfers between devices with their start and end apart: 4 -> 48, of which waited for: 4 -> 24; matrix products, arithmetic and copies ran while one was open for 7% -> 10% of each run, Pallas kernels for 0% -> 23%
where the time goes in v1:
time: 319 us; the launch traced here: 314 us
  starting transfers between devices  91.7 us (29%)
  waiting for transfers between devices  82.9 us (26%)
  Pallas kernels  73.1 us (23%)
  local copies, waits for them, and re-layouts  34.3 us (11%)
  other arithmetic  17 us (5%)
  matrix products  13.6 us (4%)
    ppermute x42, starting transfers between devices, tok_swap(): return lax.ppermute(x, 'tok', pairs)  81.5 us
    ppermute x42, waiting for transfers between devices, tok_swap(): return lax.ppermute(x, 'tok', pairs)  71.5 us
    unnamed x102, local copies, waits for them, and re-layouts  30.1 us
    pallas_call x4, Pallas kernels, k4(): pl.pallas_call(body, out_shape=jax.ShapeDtypeStruct(shape, bf), grid_spec...  22.7 us
    pallas_call x4, Pallas kernels, k2(): pl.pallas_call(k2_body, out_shape=[jax.ShapeDtypeStruct((n, T * K), bf)]...  18.7 us
    pallas_call x4, Pallas kernels, k3(): pl.pallas_call(k3_body, out_shape=jax.ShapeDtypeStruct((n, K, D), bf), gr...  16.8 us
    ppermute x6, waiting for transfers between devices, dp_swap(): return lax.ppermute(x, ('dp', 'tok'), pairs)  11.4 us
    ppermute x6, starting transfers between devices, dp_swap(): return lax.ppermute(x, ('dp', 'tok'), pairs)  10.2 us
  transfers between devices with their start and end apart: 48, of which 24 were waited for; matrix products, arithmetic and copies ran while one was open for 10% of the time, Pallas kernels for 23%

profile of v1, /device:TPU:4, one launch (start us, length us, event | category | flops | bytes accessed | tf_op | source)
XLA Modules:
  0.0 314.5 jit_solution(4609525321922711916)
XLA Ops:
  1.7 4.0 %copy-done = bf16[320,64,256]{2,1,0:T(8,128)(2,1)S(1)} copy-done((bf16[320,64,256]{2,1,0:T(8,128)(2,1)S(1)}, bf16[320,64,256]{2,1,0:T(8,128)(2,1)}, u32[]{:S(2)}) %copy-start) | copy-done | bytes 10485784
  7.6 4.0 %copy-done.1 = bf16[320,64,256]{2,1,0:T(8,128)(2,1)S(1)} copy-done((bf16[320,64,256]{2,1,0:T(8,128)(2,1)S(1)}, bf16[320,64,256]{2,1,0:T(8,128)(2,1)}, u32[]{:S(2)}) %copy-start.1) | copy-done | bytes 10485784
  14.0 4.0 %copy-done.2 = bf16[320,64,256]{2,1,0:T(8,128)(2,1)S(1)} copy-done((bf16[320,64,256]{2,1,0:T(8,128)(2,1)S(1)}, bf16[320,64,256]{2,1,0:T(8,128)(2,1)}, u32[]{:S(2)}) %copy-start.2) | copy-done | bytes 10485784
  23.0 4.0 %copy-done.3 = bf16[320,64,256]{2,1,0:T(8,128)(2,1)S(1)} copy-done((bf16[320,64,256]{2,1,0:T(8,128)(2,1)S(1)}, bf16[320,64,256]{2,1,0:T(8,128)(2,1)}, u32[]{:S(2)}) %copy-start.3) | copy-done | bytes 10485784
  35.2 7.8 %collective-permute-done.23 = bf16[20,32,256]{2,1,0:T(8,128)(2,1)S(1)} collective-permute-done((bf16[20,32,256]{2,1,0:T(8,128)(2,1)S(1)}, bf16[20,32,256]{2,1,0:T(8,128)(2,1)S(1)}, u32[]{:S(2)}, u32[]{:S(2)}) %collective-permute-start.23) | collective-permute-done | bytes 327712 | tf_op jit(solution)/shard_map/compressed/ppermute | solution.py:148
  43.0 3.9 %collective-permute-start.24 = (bf16[10,32,256]{2,1,0:T(8,128)(2,1)S(1)}, bf16[10,32,256]{2,1,0:T(8,128)(2,1)S(1)}, u32[]{:S(2)}, u32[]{:S(2)}) collective-permute-start(bf16[10,32,256]{2,1,0:T(8,128)(2,1)S(1)} %add_convert_fusion.27), channel_id=1, source_target_pairs={{0,2},{1,3},{2,0},{3,1},{4,6},{5,7},{6,4},{7,5},{8,10},{9,11},{10,... | collective-permute-start | bytes 491528 | tf_op jit(solution)/shard_map/compressed/ppermute | solution.py:148
  51.8 3.9 %collective-permute-start.25 = (bf16[10,32,256]{2,1,0:T(8,128)(2,1)S(1)}, bf16[10,32,256]{2,1,0:T(8,128)(2,1)S(1)}, u32[]{:S(2)}, u32[]{:S(2)}) collective-permute-start(bf16[10,32,256]{2,1,0:T(8,128)(2,1)S(1)} %add_convert_fusion.26), channel_id=1, source_target_pairs={{0,2},{1,3},{2,0},{3,1},{4,6},{5,7},{6,4},{7,5},{8,10},{9,11},{10,... | collective-permute-start | bytes 491528 | tf_op jit(solution)/shard_map/compressed/ppermute | solution.py:148
  56.2 4.2 %collective-permute-done.25 = bf16[10,32,256]{2,1,0:T(8,128)(2,1)S(1)} collective-permute-done((bf16[10,32,256]{2,1,0:T(8,128)(2,1)S(1)}, bf16[10,32,256]{2,1,0:T(8,128)(2,1)S(1)}, u32[]{:S(2)}, u32[]{:S(2)}) %collective-permute-start.25) | collective-permute-done | bytes 163872 | tf_op jit(solution)/shard_map/compressed/ppermute | solution.py:148
  71.0 3.9 %collective-permute-start.27 = (bf16[40,32,256]{2,1,0:T(8,128)(2,1)S(1)}, bf16[40,32,256]{2,1,0:T(8,128)(2,1)S(1)}, u32[]{:S(2)}, u32[]{:S(2)}) collective-permute-start(bf16[40,32,256]{2,1,0:T(8,128)(2,1)S(1)} %pad_maximum_fusion.6), channel_id=1, source_target_pairs={{0,4},{1,13},{2,6},{3,15},{4,0},{5,9},{6,2},{7,11},{8,12},{9,5},{1... | collective-permute-start | bytes 1966088 | tf_op jit(solution)/shard_map/compressed/ppermute | solution.py:148
  74.9 6.6 %collective-permute-done.5 = bf16[20,32,256]{2,1,0:T(8,128)(2,1)S(1)} collective-permute-done((bf16[20,32,256]{2,1,0:T(8,128)(2,1)S(1)}, bf16[20,32,256]{2,1,0:T(8,128)(2,1)S(1)}, u32[]{:S(2)}, u32[]{:S(2)}) %collective-permute-start.5) | collective-permute-done | bytes 327712 | tf_op jit(solution)/shard_map/compressed/ppermute | solution.py:148
  84.5 8.3 %collective-permute-done.6 = bf16[40,32,256]{2,1,0:T(8,128)(2,1)S(1)} collective-permute-done((bf16[40,32,256]{2,1,0:T(8,128)(2,1)S(1)}, bf16[40,32,256]{2,1,0:T(8,128)(2,1)S(1)}, u32[]{:S(2)}, u32[]{:S(2)}) %collective-permute-start.6) | collective-permute-done | bytes 655392 | tf_op jit(solution)/shard_map/compressed/ppermute | solution.py:148
  95.6 4.0 %copy-done.4 = bf16[320,64,256]{2,1,0:T(8,128)(2,1)S(1)} copy-done((bf16[320,64,256]{2,1,0:T(8,128)(2,1)S(1)}, bf16[320,64,256]{2,1,0:T(8,128)(2,1)}, u32[]{:S(2)}) %copy-start.4) | copy-done | bytes 10485784
  99.6 3.9 %field.4 = (bf16[80,2048]{1,0:T(8,128)(2,1)S(1)}, bf16[80,2048]{1,0:T(8,128)(2,1)S(1)}) custom-call(s32[80]{0:T(128)S(1)} %broadcast_select_fusion.tbl, s32[1]{0:T(128)} %bitcast.3.blk, s32[8]{0:T(128)S(1)} %gather_fusion, bf16[320,64,256]{2,1,0:T(8,128)(2,1)S(1)} %copy-done.4, bf16[80,32,256]{2,1,0:T(8,128)(2,1)S(1)} %pad_maximum_fusion.comp), custom_call_target="tpu_custom_call" | custom-call | tf_op jit(solution)/shard_map/pre/field/pallas_call | solution.py:43
  104.3 3.9 %field.6 = (bf16[80,2048]{1,0:T(8,128)(2,1)S(1)}, bf16[80,2048]{1,0:T(8,128)(2,1)S(1)}) custom-call(s32[80]{0:T(128)S(1)} %broadcast_select_fusion.tbl, s32[1]{0:T(128)} %bitcast.12.blk, s32[8]{0:T(128)S(1)} %gather_fusion, bf16[320,64,256]{2,1,0:T(8,128)(2,1)S(1)} %copy-done.4, bf16[80,32,256]{2,1,0:T(8,128)(2,1)S(1)} %pad_maximum_fusion.2.comp), custom_call_target="tpu_custom_call" | custom-call | tf_op jit(solution)/shard_map/pre/field/pallas_call | solution.py:43
  109.0 5.6 %field.7 = (bf16[80,2048]{1,0:T(8,128)(2,1)S(1)}, bf16[80,2048]{1,0:T(8,128)(2,1)S(1)}) custom-call(s32[80]{0:T(128)S(1)} %broadcast_select_fusion.1.tbl, s32[1]{0:T(128)} %bitcast.9.blk, s32[8]{0:T(128)S(1)} %gather_fusion, bf16[320,64,256]{2,1,0:T(8,128)(2,1)S(1)} %bitcast.45, bf16[80,32,256]{2,1,0:T(8,128)(2,1)} %collective-permute-done.28.comp), custom_call_target="tpu_custom_call" | custom-call | tf_op jit(solution)/shard_map/pre/field/pallas_call | solution.py:43
  116.0 5.3 %field.5 = (bf16[80,2048]{1,0:T(8,128)(2,1)S(1)}, bf16[80,2048]{1,0:T(8,128)(2,1)S(1)}) custom-call(s32[80]{0:T(128)S(1)} %broadcast_select_fusion.1.tbl, s32[1]{0:T(128)} %bitcast.blk, s32[8]{0:T(128)S(1)} %gather_fusion, bf16[320,64,256]{2,1,0:T(8,128)(2,1)S(1)} %bitcast.45, bf16[80,32,256]{2,1,0:T(8,128)(2,1)} %collective-permute-done.7.comp), custom_call_target="tpu_custom_call" | custom-call | tf_op jit(solution)/shard_map/pre/field/pallas_call | solution.py:43
  151.3 4.0 %copy-done.5 = bf16[320,64,256]{2,1,0:T(8,128)(2,1)S(1)} copy-done((bf16[320,64,256]{2,1,0:T(8,128)(2,1)S(1)}, bf16[320,64,256]{2,1,0:T(8,128)(2,1)}, u32[]{:S(2)}) %copy-start.5) | copy-done | bytes 10485784
  155.4 4.2 %grad_compress.7 = bf16[80,32,256]{2,1,0:T(8,128)(2,1)S(1)} custom-call(s32[80]{0:T(128)S(1)} %broadcast_select_fusion.1.tbl, s32[1]{0:T(128)} %bitcast.9.blk, bf16[320,64,256]{2,1,0:T(8,128)(2,1)S(1)} %copy-done.5, bf16[80,2048]{1,0:T(8,128)(2,1)S(1)} %convolution_convert_fusion.2.df), custom_call_target="tpu_custom_call" | custom-call | tf_op jit(solution)/shard_map/grad_compressed/grad_compress/pallas_call | solution.py:65
  161.7 4.2 %grad_compress.5 = bf16[80,32,256]{2,1,0:T(8,128)(2,1)S(1)} custom-call(s32[80]{0:T(128)S(1)} %broadcast_select_fusion.1.tbl, s32[1]{0:T(128)} %bitcast.blk, bf16[320,64,256]{2,1,0:T(8,128)(2,1)S(1)} %bitcast.47, bf16[80,2048]{1,0:T(8,128)(2,1)S(1)} %convolution_convert_fusion.4.df), custom_call_target="tpu_custom_call" | custom-call | tf_op jit(solution)/shard_map/grad_compressed/grad_compress/pallas_call | solution.py:65
  167.5 4.2 %grad_compress.6 = bf16[80,32,256]{2,1,0:T(8,128)(2,1)S(1)} custom-call(s32[80]{0:T(128)S(1)} %broadcast_select_fusion.tbl, s32[1]{0:T(128)} %bitcast.12.blk, bf16[320,64,256]{2,1,0:T(8,128)(2,1)S(1)} %bitcast.47, bf16[80,2048]{1,0:T(8,128)(2,1)S(1)} %convolution_convert_fusion.1.df), custom_call_target="tpu_custom_call" | custom-call | tf_op jit(solution)/shard_map/grad_compressed/grad_compress/pallas_call | solution.py:65
  173.1 4.2 %grad_compress.4 = bf16[80,32,256]{2,1,0:T(8,128)(2,1)S(1)} custom-call(s32[80]{0:T(128)S(1)} %broadcast_select_fusion.tbl, s32[1]{0:T(128)} %bitcast.3.blk, bf16[320,64,256]{2,1,0:T(8,128)(2,1)S(1)} %bitcast.47, bf16[80,2048]{1,0:T(8,128)(2,1)S(1)} %convolution_convert_fusion.3.df), custom_call_target="tpu_custom_call" | custom-call | tf_op jit(solution)/shard_map/grad_compressed/grad_compress/pallas_call | solution.py:65
  177.8 12.6 %collective-permute-start.35 = (bf16[40,32,256]{2,1,0:T(8,128)(2,1)S(1)}, bf16[40,32,256]{2,1,0:T(8,128)(2,1)S(1)}, u32[]{:S(2)}, u32[]{:S(2)}) collective-permute-start(bf16[40,32,256]{2,1,0:T(8,128)(2,1)S(1)} %get-tuple-element.27), channel_id=1, source_target_pairs={{0,4},{1,13},{2,6},{3,15},{4,0},{5,9},{6,2},{7,11},{8,12},{9,5},{1... | collective-permute-start | bytes 1966088 | tf_op jit(solution)/shard_map/grad_compressed/ppermute | solution.py:148
  201.6 7.6 %collective-permute-done.14 = bf16[40,32,256]{2,1,0:T(8,128)(2,1)S(1)} collective-permute-done((bf16[40,32,256]{2,1,0:T(8,128)(2,1)S(1)}, bf16[40,32,256]{2,1,0:T(8,128)(2,1)S(1)}, u32[]{:S(2)}, u32[]{:S(2)}) %collective-permute-start.14) | collective-permute-done | bytes 655392 | tf_op jit(solution)/shard_map/grad_compressed/ppermute | solution.py:148
  213.0 4.0 %collective-permute-done.15 = bf16[20,32,256]{2,1,0:T(8,128)(2,1)S(1)} collective-permute-done((bf16[20,32,256]{2,1,0:T(8,128)(2,1)S(1)}, bf16[20,32,256]{2,1,0:T(8,128)(2,1)S(1)}, u32[]{:S(2)}, u32[]{:S(2)}) %collective-permute-start.15) | collective-permute-done | bytes 327712 | tf_op jit(solution)/shard_map/grad_compressed/ppermute | solution.py:148
  236.1 6.2 %collective-permute-start.40 = (bf16[40,32,256]{2,1,0:T(8,128)(2,1)S(1)}, bf16[40,32,256]{2,1,0:T(8,128)(2,1)S(1)}, u32[]{:S(2)}, u32[]{:S(2)}) collective-permute-start(bf16[40,32,256]{2,1,0:T(8,128)(2,1)S(1)} %pad_maximum_fusion.7), channel_id=1, source_target_pairs={{0,4},{1,13},{2,6},{3,15},{4,0},{5,9},{6,2},{7,11},{8,12},{9,5},{1... | collective-permute-start | bytes 1966088 | tf_op jit(solution)/shard_map/grad_compressed/ppermute | solution.py:148
  243.1 6.2 %collective-permute-start.19 = (bf16[40,32,256]{2,1,0:T(8,128)(2,1)S(1)}, bf16[40,32,256]{2,1,0:T(8,128)(2,1)S(1)}, u32[]{:S(2)}, u32[]{:S(2)}) collective-permute-start(bf16[40,32,256]{2,1,0:T(8,128)(2,1)S(1)} %pad_maximum_fusion.5), channel_id=1, source_target_pairs={{0,4},{1,13},{2,6},{3,15},{4,0},{5,9},{6,2},{7,11},{8,12},{9,5},{1... | collective-permute-start | bytes 1966088 | tf_op jit(solution)/shard_map/grad_compressed/ppermute | solution.py:148
  253.7 4.2 %collective-permute-done.19 = bf16[40,32,256]{2,1,0:T(8,128)(2,1)S(1)} collective-permute-done((bf16[40,32,256]{2,1,0:T(8,128)(2,1)S(1)}, bf16[40,32,256]{2,1,0:T(8,128)(2,1)S(1)}, u32[]{:S(2)}, u32[]{:S(2)}) %collective-permute-start.19) | collective-permute-done | bytes 655392 | tf_op jit(solution)/shard_map/grad_compressed/ppermute | solution.py:148
  258.3 8.2 %collective-permute-done.43 = bf16[512,1024]{1,0:T(8,128)(2,1)S(1)} collective-permute-done((bf16[512,1024]{1,0:T(8,128)(2,1)S(1)}, bf16[512,1024]{1,0:T(8,128)(2,1)S(1)}, u32[]{:S(2)}, u32[]{:S(2)}) %collective-permute-start.43) | collective-permute-done | bytes 1048608 | tf_op jit(solution)/shard_map/grad_weight/ppermute | solution.py:156
  287.0 5.1 %grad_tokens.4.gx_in = bf16[320,64,256]{2,1,0:T(8,128)(2,1)} custom-call(s32[80]{0:T(128)S(1)} %broadcast_select_fusion.tbl, s32[1]{0:T(128)} %bitcast.12.blk, bf16[80,2048]{1,0:T(8,128)(2,1)S(1)} %copy-done.17, bf16[80,32,256]{2,1,0:T(8,128)(2,1)S(1)} %copy-done.7, bf16[80,32,256]{2,1,0:T(8,128)(2,1)S(1)} %copy-done.11, ...), custom_call_target="tpu_custom_call" | custom-call | tf_op jit(solution)/shard_map/grad_embeddings/grad_tokens/pallas_call | solution.py:89
  295.3 6.3 %grad_tokens.5.gx_in = bf16[320,64,256]{2,1,0:T(8,128)(2,1)} custom-call(s32[80]{0:T(128)S(1)} %broadcast_select_fusion.1.tbl, s32[1]{0:T(128)} %bitcast.9.blk, bf16[80,2048]{1,0:T(8,128)(2,1)S(1)} %copy-done.19, bf16[80,32,256]{2,1,0:T(8,128)(2,1)} %collective-permute-done.28.comp, ...), custom_call_target="tpu_custom_call", output_to_operand_aliasing={{}: (6, {})} | custom-call | tf_op jit(solution)/shard_map/grad_embeddings/grad_tokens/pallas_call | solution.py:89
  301.6 5.0 %grad_tokens.6.gx_in = bf16[320,64,256]{2,1,0:T(8,128)(2,1)} custom-call(s32[80]{0:T(128)S(1)} %broadcast_select_fusion.tbl, s32[1]{0:T(128)} %bitcast.3.blk, bf16[80,2048]{1,0:T(8,128)(2,1)S(1)} %copy-done.23, bf16[80,32,256]{2,1,0:T(8,128)(2,1)S(1)} %pad_maximum_fusion.comp, bf16[80,32,256]{2,1,0:T(8,128)(2,1)S(1)} %copy-done.9, ...), custom_call_target="tpu_custom_call", output_to_operand_aliasing={{}: (6, {})} | custom-call | tf_op jit(solution)/shard_map/grad_embeddings/grad_tokens/pallas_call | solution.py:89
  306.7 6.3 %grad_tokens.7 = bf16[320,64,256]{2,1,0:T(8,128)(2,1)} custom-call(s32[80]{0:T(128)S(1)} %broadcast_select_fusion.1.tbl, s32[1]{0:T(128)} %bitcast.blk, bf16[80,2048]{1,0:T(8,128)(2,1)S(1)} %copy-done.21, bf16[80,32,256]{2,1,0:T(8,128)(2,1)} %collective-permute-done.7.comp, bf16[80,32,256]{2,1,0:T(8,128)(2,1)S(1)} %copy-done.13, ...), custom_call_target="tpu_custom_call", output_to_operand_aliasing={{}: (6, {})} | custom-call | tf_op jit(solution)/shard_map/grad_embeddings/grad_tokens/pallas_call | solution.py:89
  (261 shorter events, 142.7 us)
Async XLA Ops:
  7.5 12.3 %collective-permute-start.21 = (bf16[80,32,256]{2,1,0:T(8,128)(2,1)S(1)}, bf16[80,32,256]{2,1,0:T(8,128)(2,1)}, u32[]{:S(2)}, u32[]{:S(2)}) collective-permute-start(bf16[80,32,256]{2,1,0:T(8,128)(2,1)S(1)} %compress.7), channel_id=1, source_target_pairs={{0,1},{1,0},{2,3},{3,2},{4,5},{5,4},{6,7},{7,6},{8,9},{9,8},{10,11... | collective-permute-start | bytes 3932168 | tf_op jit(solution)/shard_map/compressed/ppermute | solution.py:148
  13.5 15.4 %collective-permute-start = (bf16[80,32,256]{2,1,0:T(8,128)(2,1)S(1)}, bf16[80,32,256]{2,1,0:T(8,128)(2,1)}, u32[]{:S(2)}, u32[]{:S(2)}) collective-permute-start(bf16[80,32,256]{2,1,0:T(8,128)(2,1)S(1)} %compress.5), channel_id=1, source_target_pairs={{0,1},{1,0},{2,3},{3,2},{4,5},{5,4},{6,7},{7,6},{8,9},{9,8},{10,11... | collective-permute-start | bytes 3932168 | tf_op jit(solution)/shard_map/compressed/ppermute | solution.py:148
  21.7 10.7 %collective-permute-start.22 = (bf16[40,32,256]{2,1,0:T(8,128)(2,1)S(1)}, bf16[40,32,256]{2,1,0:T(8,128)(2,1)S(1)}, u32[]{:S(2)}, u32[]{:S(2)}) collective-permute-start(bf16[40,32,256]{2,1,0:T(8,128)(2,1)S(1)} %get-tuple-element.29), channel_id=1, source_target_pairs={{0,4},{1,13},{2,6},{3,15},{4,0},{5,9},{6,2},{7,11},{8,12},{9,5},{1... | collective-permute-start | bytes 1966088 | tf_op jit(solution)/shard_map/compressed/ppermute | solution.py:148
  30.7 16.3 %collective-permute-start.1 = (bf16[40,32,256]{2,1,0:T(8,128)(2,1)S(1)}, bf16[40,32,256]{2,1,0:T(8,128)(2,1)S(1)}, u32[]{:S(2)}, u32[]{:S(2)}) collective-permute-start(bf16[40,32,256]{2,1,0:T(8,128)(2,1)S(1)} %get-tuple-element.33), channel_id=1, source_target_pairs={{0,4},{1,13},{2,6},{3,15},{4,0},{5,9},{6,2},{7,11},{8,12},{9,5},{1... | collective-permute-start | bytes 1966088 | tf_op jit(solution)/shard_map/compressed/ppermute | solution.py:148
  34.5 8.4 %collective-permute-start.23 = (bf16[20,32,256]{2,1,0:T(8,128)(2,1)S(1)}, bf16[20,32,256]{2,1,0:T(8,128)(2,1)S(1)}, u32[]{:S(2)}, u32[]{:S(2)}) collective-permute-start(bf16[20,32,256]{2,1,0:T(8,128)(2,1)S(1)} %get-tuple-element.37), channel_id=1, source_target_pairs={{0,12},{1,5},{2,14},{3,7},{4,8},{5,1},{6,10},{7,3},{8,4},{9,13},{1... | collective-permute-start | bytes 983048 | tf_op jit(solution)/shard_map/compressed/ppermute | solution.py:148
  43.0 8.7 %collective-permute-start.24 = (bf16[10,32,256]{2,1,0:T(8,128)(2,1)S(1)}, bf16[10,32,256]{2,1,0:T(8,128)(2,1)S(1)}, u32[]{:S(2)}, u32[]{:S(2)}) collective-permute-start(bf16[10,32,256]{2,1,0:T(8,128)(2,1)S(1)} %add_convert_fusion.27), channel_id=1, source_target_pairs={{0,2},{1,3},{2,0},{3,1},{4,6},{5,7},{6,4},{7,5},{8,10},{9,11},{10,... | collective-permute-start | bytes 491528 | tf_op jit(solution)/shard_map/compressed/ppermute | solution.py:148
  47.2 8.4 %collective-permute-start.2 = (bf16[20,32,256]{2,1,0:T(8,128)(2,1)S(1)}, bf16[20,32,256]{2,1,0:T(8,128)(2,1)S(1)}, u32[]{:S(2)}, u32[]{:S(2)}) collective-permute-start(bf16[20,32,256]{2,1,0:T(8,128)(2,1)S(1)} %get-tuple-element.41), channel_id=1, source_target_pairs={{0,12},{1,5},{2,14},{3,7},{4,8},{5,1},{6,10},{7,3},{8,4},{9,13},{1... | collective-permute-start | bytes 983048 | tf_op jit(solution)/shard_map/compressed/ppermute | solution.py:148
  51.8 8.7 %collective-permute-start.25 = (bf16[10,32,256]{2,1,0:T(8,128)(2,1)S(1)}, bf16[10,32,256]{2,1,0:T(8,128)(2,1)S(1)}, u32[]{:S(2)}, u32[]{:S(2)}) collective-permute-start(bf16[10,32,256]{2,1,0:T(8,128)(2,1)S(1)} %add_convert_fusion.26), channel_id=1, source_target_pairs={{0,2},{1,3},{2,0},{3,1},{4,6},{5,7},{6,4},{7,5},{8,10},{9,11},{10,... | collective-permute-start | bytes 491528 | tf_op jit(solution)/shard_map/compressed/ppermute | solution.py:148
  60.5 10.4 %collective-permute-start.26 = (bf16[20,32,256]{2,1,0:T(8,128)(2,1)S(1)}, bf16[20,32,256]{2,1,0:T(8,128)(2,1)S(1)}, u32[]{:S(2)}, u32[]{:S(2)}) collective-permute-start(bf16[20,32,256]{2,1,0:T(8,128)(2,1)S(1)} %pad_maximum_fusion.11), channel_id=1, source_target_pairs={{0,12},{1,5},{2,14},{3,7},{4,8},{5,1},{6,10},{7,3},{8,4},{9,13},{1... | collective-permute-start | bytes 983048 | tf_op jit(solution)/shard_map/compressed/ppermute | solution.py:148
  70.8 10.7 %collective-permute-start.5 = (bf16[20,32,256]{2,1,0:T(8,128)(2,1)S(1)}, bf16[20,32,256]{2,1,0:T(8,128)(2,1)S(1)}, u32[]{:S(2)}, u32[]{:S(2)}) collective-permute-start(bf16[20,32,256]{2,1,0:T(8,128)(2,1)S(1)} %pad_maximum_fusion.9), channel_id=1, source_target_pairs={{0,12},{1,5},{2,14},{3,7},{4,8},{5,1},{6,10},{7,3},{8,4},{9,13},{1... | collective-permute-start | bytes 983048 | tf_op jit(solution)/shard_map/compressed/ppermute | solution.py:148
  71.0 13.3 %collective-permute-start.27 = (bf16[40,32,256]{2,1,0:T(8,128)(2,1)S(1)}, bf16[40,32,256]{2,1,0:T(8,128)(2,1)S(1)}, u32[]{:S(2)}, u32[]{:S(2)}) collective-permute-start(bf16[40,32,256]{2,1,0:T(8,128)(2,1)S(1)} %pad_maximum_fusion.6), channel_id=1, source_target_pairs={{0,4},{1,13},{2,6},{3,15},{4,0},{5,9},{6,2},{7,11},{8,12},{9,5},{1... | collective-permute-start | bytes 1966088 | tf_op jit(solution)/shard_map/compressed/ppermute | solution.py:148
  81.6 11.2 %collective-permute-start.6 = (bf16[40,32,256]{2,1,0:T(8,128)(2,1)S(1)}, bf16[40,32,256]{2,1,0:T(8,128)(2,1)S(1)}, u32[]{:S(2)}, u32[]{:S(2)}) collective-permute-start(bf16[40,32,256]{2,1,0:T(8,128)(2,1)S(1)} %pad_maximum_fusion.4), channel_id=1, source_target_pairs={{0,4},{1,13},{2,6},{3,15},{4,0},{5,9},{6,2},{7,11},{8,12},{9,5},{1... | collective-permute-start | bytes 1966088 | tf_op jit(solution)/shard_map/compressed/ppermute | solution.py:148
  84.4 24.6 %collective-permute-start.28 = (bf16[80,32,256]{2,1,0:T(8,128)(2,1)S(1)}, bf16[80,32,256]{2,1,0:T(8,128)(2,1)}, u32[]{:S(2)}, u32[]{:S(2)}) collective-permute-start(bf16[80,32,256]{2,1,0:T(8,128)(2,1)S(1)} %pad_maximum_fusion.2.comp), channel_id=1, source_target_pairs={{0,1},{1,0},{2,3},{3,2},{4,5},{5,4},{6,7},{7,6},{8,9},{9,8},{10,11... | collective-permute-start | bytes 3932168 | tf_op jit(solution)/shard_map/compressed/ppermute | solution.py:148
  92.9 23.1 %collective-permute-start.7 = (bf16[80,32,256]{2,1,0:T(8,128)(2,1)S(1)}, bf16[80,32,256]{2,1,0:T(8,128)(2,1)}, u32[]{:S(2)}, u32[]{:S(2)}) collective-permute-start(bf16[80,32,256]{2,1,0:T(8,128)(2,1)S(1)} %pad_maximum_fusion.comp), channel_id=1, source_target_pairs={{0,1},{1,0},{2,3},{3,2},{4,5},{5,4},{6,7},{7,6},{8,9},{9,8},{10,11... | collective-permute-start | bytes 3932168 | tf_op jit(solution)/shard_map/compressed/ppermute | solution.py:148
  147.6 12.5 %collective-permute-start.12 = (bf16[80,1024]{1,0:T(8,128)(2,1)S(1)}, bf16[80,1024]{1,0:T(8,128)(2,1)S(1)}, u32[]{:S(2)}, u32[]{:S(2)}) collective-permute-start(bf16[80,1024]{1,0:T(8,128)(2,1)S(1)} %get-tuple-element.23), channel_id=1, source_target_pairs={{0,1},{1,0},{2,3},{3,2},{4,5},{5,4},{6,7},{7,6},{8,9},{9,8},{10,11... | collective-permute-start | bytes 491528 | tf_op jit(solution)/shard_map/pre/ppermute | solution.py:148
  159.6 17.7 %collective-permute-start.34 = (bf16[80,32,256]{2,1,0:T(8,128)(2,1)S(1)}, bf16[80,32,256]{2,1,0:T(8,128)(2,1)S(1)}, u32[]{:S(2)}, u32[]{:S(2)}) collective-permute-start(bf16[80,32,256]{2,1,0:T(8,128)(2,1)S(1)} %grad_compress.7), channel_id=1, source_target_pairs={{0,1},{1,0},{2,3},{3,2},{4,5},{5,4},{6,7},{7,6},{8,9},{9,8},{10,11... | collective-permute-start | bytes 3932168 | tf_op jit(solution)/shard_map/grad_compressed/ppermute | solution.py:148
  165.9 24.5 %collective-permute-start.13 = (bf16[80,32,256]{2,1,0:T(8,128)(2,1)S(1)}, bf16[80,32,256]{2,1,0:T(8,128)(2,1)S(1)}, u32[]{:S(2)}, u32[]{:S(2)}) collective-permute-start(bf16[80,32,256]{2,1,0:T(8,128)(2,1)S(1)} %grad_compress.5), channel_id=1, source_target_pairs={{0,1},{1,0},{2,3},{3,2},{4,5},{5,4},{6,7},{7,6},{8,9},{9,8},{10,11... | collective-permute-start | bytes 3932168 | tf_op jit(solution)/shard_map/grad_compressed/ppermute | solution.py:148
  177.8 21.2 %collective-permute-start.35 = (bf16[40,32,256]{2,1,0:T(8,128)(2,1)S(1)}, bf16[40,32,256]{2,1,0:T(8,128)(2,1)S(1)}, u32[]{:S(2)}, u32[]{:S(2)}) collective-permute-start(bf16[40,32,256]{2,1,0:T(8,128)(2,1)S(1)} %get-tuple-element.27), channel_id=1, source_target_pairs={{0,4},{1,13},{2,6},{3,15},{4,0},{5,9},{6,2},{7,11},{8,12},{9,5},{1... | collective-permute-start | bytes 1966088 | tf_op jit(solution)/shard_map/grad_compressed/ppermute | solution.py:148
  190.9 18.3 %collective-permute-start.14 = (bf16[40,32,256]{2,1,0:T(8,128)(2,1)S(1)}, bf16[40,32,256]{2,1,0:T(8,128)(2,1)S(1)}, u32[]{:S(2)}, u32[]{:S(2)}) collective-permute-start(bf16[40,32,256]{2,1,0:T(8,128)(2,1)S(1)} %get-tuple-element.31), channel_id=1, source_target_pairs={{0,4},{1,13},{2,6},{3,15},{4,0},{5,9},{6,2},{7,11},{8,12},{9,5},{1... | collective-permute-start | bytes 1966088 | tf_op jit(solution)/shard_map/grad_compressed/ppermute | solution.py:148
  193.6 55.7 %collective-permute-start.42 = (bf16[1024,1024]{1,0:T(8,128)(2,1)S(1)}, bf16[1024,1024]{1,0:T(8,128)(2,1)S(1)}, u32[]{:S(2)}, u32[]{:S(2)}) collective-permute-start(bf16[1024,1024]{1,0:T(8,128)(2,1)S(1)} %slice.300), channel_id=1, source_target_pairs={{0,32},{1,97},{2,34},{3,99},{4,36},{5,101},{6,38},{7,103},{8,40},{... | collective-permute-start | bytes 6291464 | tf_op jit(solution)/shard_map/grad_weight/ppermute | solution.py:156
  199.2 12.7 %collective-permute-start.36 = (bf16[20,32,256]{2,1,0:T(8,128)(2,1)S(1)}, bf16[20,32,256]{2,1,0:T(8,128)(2,1)S(1)}, u32[]{:S(2)}, u32[]{:S(2)}) collective-permute-start(bf16[20,32,256]{2,1,0:T(8,128)(2,1)S(1)} %get-tuple-element.35), channel_id=1, source_target_pairs={{0,12},{1,5},{2,14},{3,7},{4,8},{5,1},{6,10},{7,3},{8,4},{9,13},{1... | collective-permute-start | bytes 983048 | tf_op jit(solution)/shard_map/grad_compressed/ppermute | solution.py:148
  212.0 8.0 %collective-permute-start.37 = (bf16[10,32,256]{2,1,0:T(8,128)(2,1)S(1)}, bf16[10,32,256]{2,1,0:T(8,128)(2,1)S(1)}, u32[]{:S(2)}, u32[]{:S(2)}) collective-permute-start(bf16[10,32,256]{2,1,0:T(8,128)(2,1)S(1)} %add_convert_fusion.21), channel_id=1, source_target_pairs={{0,2},{1,3},{2,0},{3,1},{4,6},{5,7},{6,4},{7,5},{8,10},{9,11},{10,... | collective-permute-start | bytes 491528 | tf_op jit(solution)/shard_map/grad_compressed/ppermute | solution.py:148
  220.1 8.6 %collective-permute-start.38 = (bf16[10,32,256]{2,1,0:T(8,128)(2,1)S(1)}, bf16[10,32,256]{2,1,0:T(8,128)(2,1)S(1)}, u32[]{:S(2)}, u32[]{:S(2)}) collective-permute-start(bf16[10,32,256]{2,1,0:T(8,128)(2,1)S(1)} %add_convert_fusion.20), channel_id=1, source_target_pairs={{0,2},{1,3},{2,0},{3,1},{4,6},{5,7},{6,4},{7,5},{8,10},{9,11},{10,... | collective-permute-start | bytes 491528 | tf_op jit(solution)/shard_map/grad_compressed/ppermute | solution.py:148
  231.7 11.3 %collective-permute-start.18 = (bf16[20,32,256]{2,1,0:T(8,128)(2,1)S(1)}, bf16[20,32,256]{2,1,0:T(8,128)(2,1)S(1)}, u32[]{:S(2)}, u32[]{:S(2)}) collective-permute-start(bf16[20,32,256]{2,1,0:T(8,128)(2,1)S(1)} %pad_maximum_fusion.10), channel_id=1, source_target_pairs={{0,12},{1,5},{2,14},{3,7},{4,8},{5,1},{6,10},{7,3},{8,4},{9,13},{1... | collective-permute-start | bytes 983048 | tf_op jit(solution)/shard_map/grad_compressed/ppermute | solution.py:148
  236.1 17.3 %collective-permute-start.40 = (bf16[40,32,256]{2,1,0:T(8,128)(2,1)S(1)}, bf16[40,32,256]{2,1,0:T(8,128)(2,1)S(1)}, u32[]{:S(2)}, u32[]{:S(2)}) collective-permute-start(bf16[40,32,256]{2,1,0:T(8,128)(2,1)S(1)} %pad_maximum_fusion.7), channel_id=1, source_target_pairs={{0,4},{1,13},{2,6},{3,15},{4,0},{5,9},{6,2},{7,11},{8,12},{9,5},{1... | collective-permute-start | bytes 1966088 | tf_op jit(solution)/shard_map/grad_compressed/ppermute | solution.py:148
  243.1 14.8 %collective-permute-start.19 = (bf16[40,32,256]{2,1,0:T(8,128)(2,1)S(1)}, bf16[40,32,256]{2,1,0:T(8,128)(2,1)S(1)}, u32[]{:S(2)}, u32[]{:S(2)}) collective-permute-start(bf16[40,32,256]{2,1,0:T(8,128)(2,1)S(1)} %pad_maximum_fusion.5), channel_id=1, source_target_pairs={{0,4},{1,13},{2,6},{3,15},{4,0},{5,9},{6,2},{7,11},{8,12},{9,5},{1... | collective-permute-start | bytes 1966088 | tf_op jit(solution)/shard_map/grad_compressed/ppermute | solution.py:148
  250.4 16.1 %collective-permute-start.43 = (bf16[512,1024]{1,0:T(8,128)(2,1)S(1)}, bf16[512,1024]{1,0:T(8,128)(2,1)S(1)}, u32[]{:S(2)}, u32[]{:S(2)}) collective-permute-start(bf16[512,1024]{1,0:T(8,128)(2,1)S(1)} %get-tuple-element.25), channel_id=1, source_target_pairs={{0,96},{1,33},{2,98},{3,35},{4,100},{5,37},{6,102},{7,39},{8,104},... | collective-permute-start | bytes 3145736 | tf_op jit(solution)/shard_map/grad_weight/ppermute | solution.py:156
  253.6 18.9 %collective-permute-start.41 = (bf16[80,32,256]{2,1,0:T(8,128)(2,1)S(1)}, bf16[80,32,256]{2,1,0:T(8,128)(2,1)S(1)}, u32[]{:S(2)}, u32[]{:S(2)}) collective-permute-start(bf16[80,32,256]{2,1,0:T(8,128)(2,1)S(1)} %pad_maximum_fusion.3.dcomp), channel_id=1, source_target_pairs={{0,1},{1,0},{2,3},{3,2},{4,5},{5,4},{6,7},{7,6},{8,9},{9,8},{10,11... | collective-permute-start | bytes 3932168 | tf_op jit(solution)/shard_map/grad_compressed/ppermute | solution.py:148
  258.1 16.3 %collective-permute-start.20 = (bf16[80,32,256]{2,1,0:T(8,128)(2,1)S(1)}, bf16[80,32,256]{2,1,0:T(8,128)(2,1)S(1)}, u32[]{:S(2)}, u32[]{:S(2)}) collective-permute-start(bf16[80,32,256]{2,1,0:T(8,128)(2,1)S(1)} %pad_maximum_fusion.1.dcomp), channel_id=1, source_target_pairs={{0,1},{1,0},{2,3},{3,2},{4,5},{5,4},{6,7},{7,6},{8,9},{9,8},{10,11... | collective-permute-start | bytes 3932168 | tf_op jit(solution)/shard_map/grad_compressed/ppermute | solution.py:148
  267.6 25.4 %collective-permute-start.44 = (bf16[256,1024]{1,0:T(8,128)(2,1)}, bf16[256,1024]{1,0:T(8,128)(2,1)}, u32[]{:S(2)}, u32[]{:S(2)}) collective-permute-start(bf16[256,1024]{1,0:T(8,128)(2,1)} %add_convert_fusion.10), channel_id=1, source_target_pairs={{0,16},{1,17},{2,18},{3,19},{4,20},{5,21},{6,22},{7,23},{8,24},{9,... | collective-permute-start | bytes 1572872 | tf_op jit(solution)/shard_map/grad_weight/ppermute | solution.py:156
  280.1 11.9 %collective-permute-start.46 = (f32[24,128]{1,0:T(8,128)S(1)}, f32[24,128]{1,0:T(8,128)S(1)}, u32[]{:S(2)}, u32[]{:S(2)}) collective-permute-start(f32[24,128]{1,0:T(8,128)S(1)} %fusion.21), channel_id=1, source_target_pairs={{0,96},{1,33},{2,98},{3,35},{4,100},{5,37},{6,102},{7,39},{8,104},... | collective-permute-start | bytes 36872 | tf_op jit(solution)/shard_map/grad_projection/ppermute | solution.py:156
  292.1 20.9 %collective-permute-start.47 = (f32[24,128]{1,0:T(8,128)S(1)}, f32[24,128]{1,0:T(8,128)S(1)}, u32[]{:S(2)}, u32[]{:S(2)}) collective-permute-start(f32[24,128]{1,0:T(8,128)S(1)} %add.363), channel_id=1, source_target_pairs={{0,16},{1,17},{2,18},{3,19},{4,20},{5,21},{6,22},{7,23},{8,24},{9,... | collective-permute-start | bytes 36872 | tf_op jit(solution)/shard_map/grad_projection/ppermute | solution.py:156
  (67 other events, 462.0 us)

commit v2 on v0

v2 whole, which is shorter than its diff:
```python
import jax
import jax.numpy as jnp
from jax import lax
from jax.experimental import pallas as pl
from jax.experimental.pallas import tpu as pltpu
from jax.sharding import PartitionSpec as P

f32 = jnp.float32
bf = jnp.bfloat16
T, K, D, H = 64, 32, 256, 1024
EB = 16
NCH = 2
ORDERS = (("ABZ", "BAZ"), ("ABZ", "BAZ"))
DP_ORDERS = ("ABZ", "BAZ")
ORDER = (
    1, 1, 1, 0, 0, 0, 1, 0, 1, 0, 1, 0, 1, 0, 1, 0, 1, 1, 1, 0,
    0, 1, 0, 1, 0, 1, 0, 1, 0, 1, 1, 0, 1, 0, 0, 1, 0, 1, "w", 0,
    1, 0, 1, 0, 1, 0, "w", 1, 1, 0, 1, 1, 1, 0, 0, 0, "s", "w", "s", 0,
    "s", 0, "w", "s",
)


class Chain:
    def __init__(self):
        self.last = []


def call(chain, body, name, outs, scratch, smem=(), vmem=(), far=(), alias=None):
    specs = [pl.BlockSpec(memory_space=pltpu.SMEM)] * len(smem)
    specs += [pl.BlockSpec(memory_space=pltpu.VMEM)] * len(vmem)
    specs += [pl.BlockSpec(memory_space=pl.ANY)] * (len(far) + len(chain.last))
    vmem = [pltpu.with_memory_space_constraint(a, pltpu.VMEM) if a.size > 100000 else a for a in vmem]
    far = [pltpu.with_memory_space_constraint(a, pltpu.HBM) for a in far]
    ins, skip = len(smem) + len(vmem) + len(far), len(chain.last)

    def run(*refs):
        body(*refs[:ins], *refs[ins + skip :])

    def place(out):
        return pl.BlockSpec(memory_space=pltpu.VMEM if isinstance(out, jax.ShapeDtypeStruct) else pl.ANY)

    result = pl.pallas_call(
        run,
        out_shape=outs,
        in_specs=specs,
        out_specs=[place(out) for out in outs],
        scratch_shapes=scratch,
        input_output_aliases=alias or {},
        compiler_params=pltpu.CompilerParams(vmem_limit_bytes=8 * 1024 * 1024),
        name=name,
    )(*smem, *vmem, *far, *chain.last)
    chain.last = [result[-1]]
    return result


def shape(*dims, dtype=bf):
    return jax.ShapeDtypeStruct(dims, dtype)


def compress(chain, x, pt4, tbl, blk):
    n = tbl.shape[0]

    def body(tbl, blk, pt4, x, xv, out, sem):
        def copy(i):
            return pltpu.make_async_copy(x.at[pl.ds((blk[0] + i) * EB, EB)], xv.at[pl.ds(i * EB, EB)], sem.at[i])

        for i in range(n // EB):
            copy(i).start()

        @pl.loop(0, n // EB)
        def _(i):
            copy(i).wait()
            for g in range(EB // 4):
                x4 = xv[pl.ds(i * EB + 4 * g, 4)].reshape(4 * T, D)
                r = jnp.dot(pt4[...], x4, preferred_element_type=f32).astype(bf)
                for j in range(4):
                    out[tbl[i * EB + 4 * g + j]] = r[K * j : K * j + K]

    outs = [shape(n, T, D), shape(n, K, D)]
    return call(chain, body, "compress", outs, [pltpu.SemaphoreType.DMA((n // EB,))], [tbl, blk], [pt4], [x])


def field(chain, x, comp, w, tbl, perm):
    n = tbl.shape[0]

    def body(tbl, perm, comp, x, w, flatp, hidden, sc, flat):
        lane = lax.broadcasted_iota(jnp.int32, (EB, 128), 1) // K

        @pl.loop(0, n // EB)
        def _(i):
            for e in range(EB):
                c = comp[tbl[i * EB + e]]
                sc[T * e : T * e + T, :K] = lax.dot_general(
                    x[i * EB + e], c, (((1,), (1,)), ((), ())), preferred_element_type=f32
                )
            rows = pl.ds(pl.multiple_of(i * EB, EB), EB)
            for g in range(T // 4):
                acc = sc[pl.ds(4 * g, EB, stride=T), :]
                for j in range(1, 4):
                    v = pltpu.roll(sc[pl.ds(4 * g + j, EB, stride=T), :], K * j, 1)
                    acc = jnp.where(lane == j, v, acc)
                flat[rows, 128 * g : 128 * g + 128] = acc.astype(bf)
            for j in range(8):
                at = pl.ds(pl.multiple_of(perm[j] * 256, 256), 256)
                flatp[rows, 256 * j : 256 * j + 256] = flat[rows, at]

        for j in range(H // 256):
            at = slice(256 * j, 256 * j + 256)
            hidden[:, at] = jnp.dot(flat[...], w[:, at], preferred_element_type=f32).astype(bf)

    scratch = [pltpu.VMEM((EB * T, 128), f32), pltpu.VMEM((n, T * K), bf)]
    return call(chain, body, "field", [shape(n, T * K), shape(n, H)], scratch, [tbl, perm], [comp, x, w])


def spread(df, rows, sc, tail=None):
    lane = lax.broadcasted_iota(jnp.int32, (EB, 128), 1)
    for g in range(T // 4):
        v = df[rows, 128 * g : 128 * g + 128].astype(f32)
        for j in range(4):
            w = v if j == 0 else pltpu.roll(v, 128 - K * j, 1)
            if tail is not None:
                w = jnp.where(lane < K, w, tail[4 * g + j : 4 * g + j + 1, :])
            sc[pl.ds(4 * g + j, EB, stride=T), :] = w


def silu_grad(value):
    sig = jax.nn.sigmoid(value)
    return sig * (1.0 + value * (1.0 - sig))


def grad_compress(chain, x, pre, up, bias, w, tbl, blk):
    n = tbl.shape[0]

    def body(tbl, blk, pre, up, bias, x, w, gpre, df, out, sc):
        @pl.loop(0, n // EB)
        def _(i):
            rows = pl.ds(pl.multiple_of(i * EB, EB), EB)
            u = up[pl.ds(pl.multiple_of((blk[0] + i) * EB, EB), EB), :].astype(f32)
            gpre[rows, :] = (u * silu_grad(pre[rows, :].astype(f32) + bias[...])).astype(bf)

        for j in range(T * K // 256):
            at = slice(256 * j, 256 * j + 256)
            df[:, at] = lax.dot_general(
                gpre[...], w[at, :], (((1,), (1,)), ((), ())), preferred_element_type=f32
            ).astype(bf)

        @pl.loop(0, n // EB)
        def _(i):
            spread(df, pl.ds(pl.multiple_of(i * EB, EB), EB), sc)
            for e in range(EB):
                s = sc[T * e : T * e + T, :K].astype(bf)
                r = lax.dot_general(s, x[i * EB + e], (((0,), (0,)), ((), ())), preferred_element_type=f32)
                out[tbl[i * EB + e]] = r.astype(bf)

    outs = [shape(n, H), shape(n, T * K), shape(n, K, D)]
    scratch = [pltpu.VMEM((EB * T, 128), f32)]
    return call(chain, body, "grad_compress", outs, scratch, [tbl, blk], [pre, up, bias, x, w])


def grad_weight(chain, flats, gpres):
    m = T * K // 2

    def body(*refs):
        ins, (keep, send, sums) = refs[:-3], refs[-3:]
        flats, gpres = ins[: len(ins) // 2], ins[len(ins) // 2 :]
        g = jnp.concatenate([r[...] for r in gpres], axis=0)
        for j in range(8):
            f = jnp.concatenate([r[:, 256 * j : 256 * j + 256] for r in flats], axis=0)
            r = lax.dot_general(f, g, (((0,), (0,)), ((), ())), preferred_element_type=f32).astype(bf)
            out, at = (keep, 256 * j) if j < 4 else (send, 256 * j - m)
            out[at : at + 256, :] = r
        sums[...] = jnp.zeros_like(sums)
        total = jnp.sum(g.astype(f32), axis=0, keepdims=True)
        for j in range(H // 128):
            sums[K + j : K + j + 1, :] = total[:, 128 * j : 128 * j + 128]

    outs = [shape(m, H), shape(m, H), shape(K + H // 128, 128, dtype=f32)]
    return call(chain, body, "grad_weight", outs, [], [], [*flats, *gpres])


def grad_projection(chain, x, dcomp, sums, tbl):
    n = tbl.shape[0]

    def body(tbl, dcomp, x, sums, out):
        out[...] = sums[...]

        @pl.loop(0, n // EB)
        def _(i):
            acc = out[:K, :T]
            for e in range(EB):
                acc = acc + lax.dot_general(
                    dcomp[tbl[i * EB + e]], x[i * EB + e], (((1,), (1,)), ((), ())), preferred_element_type=f32
                )
            out[:K, :T] = acc

    return call(chain, body, "grad_projection", [shape(*sums.shape, dtype=f32)], [], [tbl], [dcomp, x, sums])[0]


def grad_tokens(chain, df, comp, dcomp, tail, gx, dims, tbl, blk):
    n = tbl.shape[0]
    far = [] if gx is None else [gx]

    def body(tbl, blk, df, comp, dcomp, tail, *rest):
        out, mark, ov, sem, sc = rest[len(far) :]
        mark[...] = jnp.zeros_like(mark)

        def copy(i):
            return pltpu.make_async_copy(ov.at[pl.ds(i * EB, EB)], out.at[pl.ds((blk[0] + i) * EB, EB)], sem.at[i])

        @pl.loop(0, n // EB)
        def _(i):
            spread(df, pl.ds(pl.multiple_of(i * EB, EB), EB), sc, tail)
            for e in range(EB):
                s = sc[T * e : T * e + T, : 2 * K].astype(bf)
                at = tbl[i * EB + e]
                w = jnp.concatenate([comp[at], dcomp[at]], axis=0)
                ov[i * EB + e] = jnp.dot(s, w, preferred_element_type=f32).astype(bf)
            copy(i).start()

        for i in range(n // EB):
            copy(i).wait()

    outs = [pltpu.HBM(dims, bf), shape(8, 128, dtype=f32)]
    scratch = [pltpu.VMEM((n, T, D), bf), pltpu.SemaphoreType.DMA((n // EB,)), pltpu.VMEM((EB * T, 128), f32)]
    alias = {6: 0} if far else None
    return call(chain, body, "grad_tokens", outs, scratch, [tbl, blk], [df, comp, dcomp, tail], far, alias)[0]


def add_rows(chain, a, b, cut=False, dtype=bf):
    n, rest = a.shape[0], a.shape[1:]
    m = n // 2 if cut else n
    step = 10 if len(rest) == 2 else 16 if a.dtype == bf else 8

    def body(a, b, *outs):
        for k, out in enumerate(outs):

            @pl.loop(0, m // step)
            def _(i):
                to = pl.multiple_of(i * step, step)
                at = pl.ds(pl.multiple_of(k * m + i * step, step), step)
                out[pl.ds(to, step)] = (a[at].astype(f32) + b[at].astype(f32)).astype(out.dtype)

    outs = call(chain, body, "add", [shape(m, *rest, dtype=dtype)] * (n // m), [], [], [a, b])
    return outs if cut else outs[0]


def join_rows(chain, a, b):
    n, rest = a.shape[0], a.shape[1:]

    def body(a, b, out):
        @pl.loop(0, n // 10)
        def _(i):
            out[pl.ds(i * 10, 10)] = a[pl.ds(i * 10, 10)]
            out[pl.ds(n + i * 10, 10)] = b[pl.ds(i * 10, 10)]

    return call(chain, body, "join", [shape(2 * n, *rest)], [], [], [a, b])[0]


def tok_bits(i):
    x = i // 4
    g = x ^ (x >> 1)
    return {"A": g & 1, "B": g >> 1, "Z": (i >> 1) & 1}


def tok_flip(i, d):
    x = i // 4
    return {"A": (x ^ 1) * 4 + i % 4, "B": (3 - x) * 4 + i % 4, "Z": i ^ 2, "C": i ^ 1}[d]


def dp_bits(i):
    y = i // 2
    g = y ^ (y >> 1)
    return {"A": g & 1, "B": g >> 1, "Z": i & 1}


def dp_flip(i, d):
    y = i // 2
    return {"A": (y ^ 1) * 2 + i % 2, "B": (3 - y) * 2 + i % 2, "Z": i ^ 1}[d]


def place(bits, order):
    return bits[order[0]] * 4 + bits[order[1]] * 2 + bits[order[2]]


def tok_swap(x, step, orders):
    if step == "C":
        pairs = [(i, tok_flip(i, "C")) for i in range(16)]
    else:
        pairs = [(i, tok_flip(i, orders[i & 1][step])) for i in range(16)]
    return lax.ppermute(x, "tok", pairs)


def dp_swap(x, step):
    pairs = []
    for d in range(8):
        for t in range(16):
            pairs.append((d * 16 + t, dp_flip(d, DP_ORDERS[t & 1][step]) * 16 + t))
    return lax.ppermute(x, ("dp", "tok"), pairs)


def per_device(embeddings, projection, mlp_weight, mlp_bias, upstream):
    half = embeddings.shape[0] // NCH // 2
    part = half // 8
    tok = lax.axis_index("tok")
    core = tok & 1
    bits, dbits = tok_bits(tok), dp_bits(lax.axis_index("dp"))
    own = jnp.where(core == 0, place(dbits, DP_ORDERS[0]), place(dbits, DP_ORDERS[1]))
    owners = []
    for order in DP_ORDERS:
        table = [0] * 8
        for d in range(8):
            table[place(dp_bits(d), order)] = d
        owners.append(table)
    owners = jnp.asarray(owners, jnp.int32)[core]
    perm = owners[own ^ jnp.arange(8)].astype(jnp.int32)

    pt = jnp.tile(projection.T, (4, 4))
    same = (jnp.arange(4 * K)[:, None] // K) == (jnp.arange(4 * T)[None] // T)
    pt4 = jnp.where(same, pt, 0).astype(bf)
    tail = jnp.pad(projection.astype(f32), ((0, 0), (K, 128 - 2 * K)))
    bias = mlp_bias.reshape(1, H)

    e = jnp.arange(half, dtype=jnp.int32)
    tables, blocks = [], []
    for c in range(NCH):
        tabs = [((e // part) ^ place(bits, ORDERS[c][h])) * part + e % part for h in range(2)]
        tables.append((jnp.where(core == 0, tabs[0], tabs[1]), jnp.where(core == 0, tabs[1], tabs[0])))
        first = c * 2 * half // EB
        blocks.append(((first + core * (half // EB)).reshape(1), (first + (1 - core) * (half // EB)).reshape(1)))

    chain = Chain()
    chain.last = [perm, tail, bias, *(a for c in range(NCH) for pair in (tables[c], blocks[c]) for a in pair)]
    done = {}

    def total(swap, mine, got):
        for step in range(3):
            mine, send = add_rows(chain, mine, got, True)
            got = swap(send, step)
            yield
        mine = add_rows(chain, mine, got)
        for step in (2, 1, 0):
            got = swap(mine, step)
            yield
            mine = join_rows(chain, mine, got)
        return mine

    def chunk(c):
        tbl, blk = tables[c], blocks[c]

        def swap(x, step):
            return tok_swap(x, step, ORDERS[c])

        x1, other = compress(chain, embeddings, pt4, tbl[1], blk[1])
        got = swap(other, "C")
        yield
        x0, mine = compress(chain, embeddings, pt4, tbl[0], blk[0])
        yield
        mine = yield from total(swap, mine, got)
        other = swap(mine, "C")
        comp = (mine, other)
        yield
        f0, h0 = field(chain, x0, mine, mlp_weight, tbl[0], perm)
        yield
        f1, h1 = field(chain, x1, other, mlp_weight, tbl[1], perm)
        got = swap(h1, "C")
        yield
        pre = h0
        for step in range(3):
            pre = add_rows(chain, pre, got)
            got = swap(pre, step)
            yield
        pre = add_rows(chain, pre, got)
        got = swap(pre, "C")
        yield
        g1, d1, other = grad_compress(chain, x1, got, upstream, bias, mlp_weight, tbl[1], blk[1])
        got = swap(other, "C")
        yield
        g0, d0, mine = grad_compress(chain, x0, pre, upstream, bias, mlp_weight, tbl[0], blk[0])
        done[c] = ((f0, f1), (g0, g1))
        yield
        mine = yield from total(swap, mine, got)
        other = swap(mine, "C")
        dcomp = (mine, other)
        yield
        done["sums"] = grad_projection(chain, x0, mine, done["sums"], tbl[0])
        yield
        done["sums"] = grad_projection(chain, x1, other, done["sums"], tbl[1])
        yield
        for h, d in ((0, d0), (1, d1)):
            done["gx"] = grad_tokens(
                chain, d, comp[h], dcomp[h], tail, done.get("gx"), embeddings.shape, tbl[h], blk[h]
            )
            yield

    def weight():
        flats = [f for c in range(NCH) for f in done[c][0]]
        gpres = [g for c in range(NCH) for g in done[c][1]]
        keep, send, done["sums"] = grad_weight(chain, flats, gpres)
        got = dp_swap(send, 0)
        yield
        for step in (1, 2):
            keep, send = add_rows(chain, keep, got, True)
            got = dp_swap(send, step)
            yield
        done["w"] = add_rows(chain, keep, got, dtype=f32)
        yield

    def sums():
        x = done["sums"]
        for step in range(3):
            got = dp_swap(x, step)
            yield
            x = add_rows(chain, x, got, dtype=f32)
        done["sums"] = x
        yield

    steps = {c: chunk(c) for c in range(NCH)}
    steps["w"], steps["s"] = weight(), sums()
    for who in ORDER:
        next(steps[who])
    grad_p = done["sums"][:K, :T].T
    grad_b = done["sums"][K:].reshape(H)
    return done["gx"], done["w"], grad_p, grad_b


def solution(mesh):
    in_specs = (P("dp", "tok", None), P("tok", None), P("tok", None), P(), P("dp", None))
    out_specs = (P("dp", "tok", None), P(("tok", "dp"), None), P("tok", None), P())
    return jax.shard_map(
        per_device, mesh=mesh, in_specs=in_specs, out_specs=out_specs, check_vma=False
    )
```

time: 618 us -> 256 us (0.41)
  waiting for transfers between devices: 473 us -> 96.9 us
  Pallas kernels: 0 us -> 79.7 us
  matrix products: 74.3 us -> 0 us
  starting transfers between devices: 0.35 us -> 71.6 us
  blocking collectives: 35.6 us -> 0 us
  between operations: 13.8 us -> 1.36 us
  local copies, waits for them, and re-layouts: 14.6 us -> 6.13 us
    psum x3 -> x0, waiting for transfers between devices: 444 us -> none  [the longest x1 154 us: per_device(): dcomp = lax.psum(dcomp_part.astype(jnp.bfloat16), 'tok')]
    ppermute x0 -> x48, waiting for transfers between devices: none -> 96.9 us  [the longest x42 85.3 us: tok_swap(): return lax.ppermute(x, 'tok', pairs)]
    pallas_call x0 -> x63, Pallas kernels: none -> 79.7 us  [call(): pl.pallas_call(run, out_shape=outs, in_specs=specs, out_specs=[place(out)...]
    dot_general x9 -> x0, matrix products: 74.3 us -> none  [the longest x1 14.6 us: per_device(): jnp.einsum('etk,ekd->etd', dfield, compressed, preferred_element_type=jnp...]
    ppermute x0 -> x48, starting transfers between devices: none -> 71.6 us  [the longest x42 58.1 us: tok_swap(): return lax.ppermute(x, 'tok', pairs)]
    psum x1 -> x0, blocking collectives: 35.6 us -> none  [per_device(): grad_p, grad_b = lax.psum((proj_local, bias_local), 'dp')]
    reduce_scatter x1 -> x0, waiting for transfers between devices: 29.7 us -> none  [per_device(): lax.psum_scatter(lax.dot_general(flat, grad_pre, (((0,), (0,)), ((), ()))...]
    convert_element_type x2 -> x0, local copies, waits for them, and re-layouts: 7.28 us -> none  [the longest x1 5.73 us: per_device(): field = jnp.einsum('etd,ekd->etk', embeddings, compressed, preferred_elem...]
  transfers between devices with their start and end apart: 4 -> 48, of which waited for: 4 -> 28; matrix products, arithmetic and copies ran while one was open for 7% -> 0% of each run, Pallas kernels for 0% -> 24%
where the time goes in v2:
time: 256 us
  waiting for transfers between devices  96.9 us (38%)
  Pallas kernels  79.7 us (31%)
  starting transfers between devices  71.6 us (28%)
  local copies, waits for them, and re-layouts  6.13 us (2%)
    ppermute x42, waiting for transfers between devices, tok_swap(): return lax.ppermute(x, 'tok', pairs)  85.3 us
    pallas_call x63, Pallas kernels, call(): pl.pallas_call(run, out_shape=outs, in_specs=specs, out_specs=[place(out)...  79.7 us
    ppermute x42, starting transfers between devices, tok_swap(): return lax.ppermute(x, 'tok', pairs)  58.1 us
    ppermute x6, starting transfers between devices, dp_swap(): return lax.ppermute(x, ('dp', 'tok'), pairs)  13.5 us
    ppermute x6, waiting for transfers between devices, dp_swap(): return lax.ppermute(x, ('dp', 'tok'), pairs)  11.6 us
  transfers between devices with their start and end apart: 48, of which 28 were waited for; matrix products, arithmetic and copies ran while one was open for 0% of the time, Pallas kernels for 24%

profile of v2, /device:TPU:4, one launch (start us, length us, event | category | flops | bytes accessed | tf_op | source)
XLA Modules:
  0.0 255.9 jit_solution(4750527797861863800)
XLA Ops:
  19.6 5.3 %collective-permute-done.3.refs_1_ = bf16[40,32,256]{2,1,0:T(8,128)(2,1)S(1)} collective-permute-done((bf16[40,32,256]{2,1,0:T(8,128)(2,1)S(1)}, bf16[40,32,256]{2,1,0:T(8,128)(2,1)S(1)}, u32[]{:S(2)}, u32[]{:S(2)}) %collective-permute-start.3) | collective-permute-done | bytes 655392 | tf_op jit(solution)/shard_map/ppermute | solution.py:290
  25.6 9.8 %collective-permute-done.2.refs_1_ = bf16[40,32,256]{2,1,0:T(8,128)(2,1)S(1)} collective-permute-done((bf16[40,32,256]{2,1,0:T(8,128)(2,1)S(1)}, bf16[40,32,256]{2,1,0:T(8,128)(2,1)S(1)}, u32[]{:S(2)}, u32[]{:S(2)}) %collective-permute-start.2) | collective-permute-done | bytes 655392 | tf_op jit(solution)/shard_map/ppermute | solution.py:290
  36.2 4.0 %collective-permute-start.7 = (bf16[10,32,256]{2,1,0:T(8,128)(2,1)S(1)}, bf16[10,32,256]{2,1,0:T(8,128)(2,1)S(1)}, u32[]{:S(2)}, u32[]{:S(2)}) collective-permute-start(bf16[10,32,256]{2,1,0:T(8,128)(2,1)S(1)} %get-tuple-element.83.refs_2_), channel_id=1, source_target_pairs={{0,2},{1,3},{2,0},{3,1},{4,6},{5,7},{6,4},{7,5},{8,10},{9,11},{10,... | collective-permute-start | bytes 491528 | tf_op jit(solution)/shard_map/ppermute | solution.py:290
  42.8 3.9 %collective-permute-start.6 = (bf16[10,32,256]{2,1,0:T(8,128)(2,1)S(1)}, bf16[10,32,256]{2,1,0:T(8,128)(2,1)S(1)}, u32[]{:S(2)}, u32[]{:S(2)}) collective-permute-start(bf16[10,32,256]{2,1,0:T(8,128)(2,1)S(1)} %get-tuple-element.85.refs_2_), channel_id=1, source_target_pairs={{0,2},{1,3},{2,0},{3,1},{4,6},{5,7},{6,4},{7,5},{8,10},{9,11},{10,... | collective-permute-start | bytes 491528 | tf_op jit(solution)/shard_map/ppermute | solution.py:290
  47.7 3.8 %collective-permute-done.6.refs_1_ = bf16[10,32,256]{2,1,0:T(8,128)(2,1)S(1)} collective-permute-done((bf16[10,32,256]{2,1,0:T(8,128)(2,1)S(1)}, bf16[10,32,256]{2,1,0:T(8,128)(2,1)S(1)}, u32[]{:S(2)}, u32[]{:S(2)}) %collective-permute-start.6) | collective-permute-done | bytes 163872 | tf_op jit(solution)/shard_map/ppermute | solution.py:290
  56.1 5.1 %collective-permute-done.8.refs_1_ = bf16[10,32,256]{2,1,0:T(8,128)(2,1)S(1)} collective-permute-done((bf16[10,32,256]{2,1,0:T(8,128)(2,1)S(1)}, bf16[10,32,256]{2,1,0:T(8,128)(2,1)S(1)}, u32[]{:S(2)}, u32[]{:S(2)}) %collective-permute-start.8) | collective-permute-done | bytes 163872 | tf_op jit(solution)/shard_map/ppermute | solution.py:290
  61.3 4.2 %collective-permute-start.13 = (bf16[40,32,256]{2,1,0:T(8,128)(2,1)S(1)}, bf16[40,32,256]{2,1,0:T(8,128)(2,1)S(1)}, u32[]{:S(2)}, u32[]{:S(2)}) collective-permute-start(bf16[40,32,256]{2,1,0:T(8,128)(2,1)S(1)} %join.14.refs_2_.refs_0_), channel_id=1, source_target_pairs={{0,4},{1,13},{2,6},{3,15},{4,0},{5,9},{6,2},{7,11},{8,12},{9,5},{1... | collective-permute-start | bytes 1966088 | tf_op jit(solution)/shard_map/ppermute | solution.py:290
  65.9 6.7 %collective-permute-done.10.refs_1_ = bf16[20,32,256]{2,1,0:T(8,128)(2,1)S(1)} collective-permute-done((bf16[20,32,256]{2,1,0:T(8,128)(2,1)S(1)}, bf16[20,32,256]{2,1,0:T(8,128)(2,1)S(1)}, u32[]{:S(2)}, u32[]{:S(2)}) %collective-permute-start.10) | collective-permute-done | bytes 327712 | tf_op jit(solution)/shard_map/ppermute | solution.py:290
  76.3 4.1 %field.4 = (bf16[80,2048]{1,0:T(8,128)(2,1)S(1)}, bf16[80,1024]{1,0:T(8,128)(2,1)S(1)}) custom-call(s32[80]{0:T(128)S(1)} %get-tuple-element.138.refs_7_.refs_11_.refs_0_, s32[8]{0:T(128)S(1)} %gather_fusion, bf16[80,32,256]{2,1,0:T(8,128)(2,1)S(1)} %join.16.refs_2_.refs_5_.refs_3_, bf16[80,64,256]{2,1,0:T(8,128)(2,1)S(1)} %get-tuple-element.88.refs_3_.refs_5_.refs_2_, ...), custom_call_target="tpu_custom_call" | custom-call | tf_op jit(solution)/shard_map/field/pallas_call | solution.py:42
  80.4 4.1 %field.5 = (bf16[80,2048]{1,0:T(8,128)(2,1)S(1)}, bf16[80,1024]{1,0:T(8,128)(2,1)S(1)}) custom-call(s32[80]{0:T(128)S(1)} %get-tuple-element.139.refs_0_.refs_8_.refs_12_, s32[8]{0:T(128)S(1)} %gather_fusion, bf16[80,32,256]{2,1,0:T(8,128)(2,1)S(1)} %collective-permute-done.14.refs_2_.refs_3_, ...), custom_call_target="tpu_custom_call" | custom-call | tf_op jit(solution)/shard_map/field/pallas_call | solution.py:42
  85.5 4.1 %field.6 = (bf16[80,2048]{1,0:T(8,128)(2,1)S(1)}, bf16[80,1024]{1,0:T(8,128)(2,1)S(1)}) custom-call(s32[80]{0:T(128)S(1)} %get-tuple-element.138.refs_7_.refs_11_.refs_0_, s32[8]{0:T(128)S(1)} %gather_fusion, bf16[80,32,256]{2,1,0:T(8,128)(2,1)S(1)} %join.17.refs_2_.refs_5_.refs_3_, bf16[80,64,256]{2,1,0:T(8,128)(2,1)S(1)} %get-tuple-element.91.refs_3_.refs_5_.refs_2_, ...), custom_call_target="tpu_custom_call" | custom-call | tf_op jit(solution)/shard_map/field/pallas_call | solution.py:42
  91.9 4.1 %field.7 = (bf16[80,2048]{1,0:T(8,128)(2,1)S(1)}, bf16[80,1024]{1,0:T(8,128)(2,1)S(1)}) custom-call(s32[80]{0:T(128)S(1)} %get-tuple-element.139.refs_0_.refs_8_.refs_12_, s32[8]{0:T(128)S(1)} %gather_fusion, bf16[80,32,256]{2,1,0:T(8,128)(2,1)S(1)} %collective-permute-done.15.refs_2_.refs_3_, ...), custom_call_target="tpu_custom_call" | custom-call | tf_op jit(solution)/shard_map/field/pallas_call | solution.py:42
  105.8 4.2 %collective-permute-done.22.refs_1_ = bf16[80,1024]{1,0:T(8,128)(2,1)S(1)} collective-permute-done((bf16[80,1024]{1,0:T(8,128)(2,1)S(1)}, bf16[80,1024]{1,0:T(8,128)(2,1)S(1)}, u32[]{:S(2)}, u32[]{:S(2)}) %collective-permute-start.22) | collective-permute-done | bytes 163872 | tf_op jit(solution)/shard_map/ppermute | solution.py:290
  111.5 4.7 %grad_compress.4 = (bf16[80,1024]{1,0:T(8,128)(2,1)S(1)}, bf16[80,2048]{1,0:T(8,128)(2,1)S(1)}, bf16[80,32,256]{2,1,0:T(8,128)(2,1)S(1)}) custom-call(s32[80]{0:T(128)S(1)} %get-tuple-element.139.refs_0_.refs_8_.refs_12_, s32[1]{0:T(128)} %bitcast.6.refs_1_.refs_14_, bf16[80,1024]{1,0:T(8,128)(2,1)S(1)} %collective-permute-done.24.refs_2_, ...), custom_call_target="tpu_custom_call" | custom-call | tf_op jit(solution)/shard_map/grad_compress/pallas_call | solution.py:42
  119.0 4.7 %grad_compress.5 = (bf16[80,1024]{1,0:T(8,128)(2,1)S(1)}, bf16[80,2048]{1,0:T(8,128)(2,1)S(1)}, bf16[80,32,256]{2,1,0:T(8,128)(2,1)S(1)}) custom-call(s32[80]{0:T(128)S(1)} %get-tuple-element.138.refs_7_.refs_11_.refs_0_, s32[1]{0:T(128)} %bitcast.5.refs_13_.refs_1_, bf16[80,1024]{1,0:T(8,128)(2,1)S(1)} %add.170.refs_2_, bf16[320,1024]{1,0:T(8,128)(2,1)S(1)} %copy-done.1, ...), custom_call_target="tpu_custom_call" | custom-call | tf_op jit(solution)/shard_map/grad_compress/pallas_call | solution.py:42
  126.0 4.7 %grad_compress.6 = (bf16[80,1024]{1,0:T(8,128)(2,1)S(1)}, bf16[80,2048]{1,0:T(8,128)(2,1)S(1)}, bf16[80,32,256]{2,1,0:T(8,128)(2,1)S(1)}) custom-call(s32[80]{0:T(128)S(1)} %get-tuple-element.139.refs_0_.refs_8_.refs_12_, s32[1]{0:T(128)} %bitcast.refs_10_.refs_1_, bf16[80,1024]{1,0:T(8,128)(2,1)S(1)} %collective-permute-done.25.refs_2_, ...), custom_call_target="tpu_custom_call" | custom-call | tf_op jit(solution)/shard_map/grad_compress/pallas_call | solution.py:42
  131.0 3.3 %collective-permute-start.28 = (bf16[40,32,256]{2,1,0:T(8,128)(2,1)S(1)}, bf16[40,32,256]{2,1,0:T(8,128)(2,1)S(1)}, u32[]{:S(2)}, u32[]{:S(2)}) collective-permute-start(bf16[40,32,256]{2,1,0:T(8,128)(2,1)S(1)} %get-tuple-element.97.refs_7_), channel_id=1, source_target_pairs={{0,4},{1,13},{2,6},{3,15},{4,0},{5,9},{6,2},{7,11},{8,12},{9,5},{1... | collective-permute-start | bytes 1966088 | tf_op jit(solution)/shard_map/ppermute | solution.py:290
  134.3 4.7 %grad_compress.7 = (bf16[80,1024]{1,0:T(8,128)(2,1)S(1)}, bf16[80,2048]{1,0:T(8,128)(2,1)S(1)}, bf16[80,32,256]{2,1,0:T(8,128)(2,1)S(1)}) custom-call(s32[80]{0:T(128)S(1)} %get-tuple-element.138.refs_7_.refs_11_.refs_0_, s32[1]{0:T(128)} %bitcast.3.refs_9_.refs_1_, bf16[80,1024]{1,0:T(8,128)(2,1)S(1)} %add.172.refs_2_, bf16[320,1024]{1,0:T(8,128)(2,1)S(1)} %copy-done.1, ...), custom_call_target="tpu_custom_call" | custom-call | tf_op jit(solution)/shard_map/grad_compress/pallas_call | solution.py:42
  139.1 3.8 %collective-permute-done.28.refs_1_ = bf16[40,32,256]{2,1,0:T(8,128)(2,1)S(1)} collective-permute-done((bf16[40,32,256]{2,1,0:T(8,128)(2,1)S(1)}, bf16[40,32,256]{2,1,0:T(8,128)(2,1)S(1)}, u32[]{:S(2)}, u32[]{:S(2)}) %collective-permute-start.28) | collective-permute-done | bytes 655392 | tf_op jit(solution)/shard_map/ppermute | solution.py:290
  145.1 5.1 %collective-permute-done.30.refs_1_ = bf16[20,32,256]{2,1,0:T(8,128)(2,1)S(1)} collective-permute-done((bf16[20,32,256]{2,1,0:T(8,128)(2,1)S(1)}, bf16[20,32,256]{2,1,0:T(8,128)(2,1)S(1)}, u32[]{:S(2)}, u32[]{:S(2)}) %collective-permute-start.30) | collective-permute-done | bytes 327712 | tf_op jit(solution)/shard_map/ppermute | solution.py:290
  159.1 7.0 %collective-permute-done.29.refs_1_ = bf16[40,32,256]{2,1,0:T(8,128)(2,1)S(1)} collective-permute-done((bf16[40,32,256]{2,1,0:T(8,128)(2,1)S(1)}, bf16[40,32,256]{2,1,0:T(8,128)(2,1)S(1)}, u32[]{:S(2)}, u32[]{:S(2)}) %collective-permute-start.29) | collective-permute-done | bytes 655392 | tf_op jit(solution)/shard_map/ppermute | solution.py:290
  169.7 3.7 %collective-permute-done.31.refs_1_ = bf16[20,32,256]{2,1,0:T(8,128)(2,1)S(1)} collective-permute-done((bf16[20,32,256]{2,1,0:T(8,128)(2,1)S(1)}, bf16[20,32,256]{2,1,0:T(8,128)(2,1)S(1)}, u32[]{:S(2)}, u32[]{:S(2)}) %collective-permute-start.31) | collective-permute-done | bytes 327712 | tf_op jit(solution)/shard_map/ppermute | solution.py:290
  178.7 5.3 %collective-permute-done.33.refs_1_ = bf16[10,32,256]{2,1,0:T(8,128)(2,1)S(1)} collective-permute-done((bf16[10,32,256]{2,1,0:T(8,128)(2,1)S(1)}, bf16[10,32,256]{2,1,0:T(8,128)(2,1)S(1)}, u32[]{:S(2)}, u32[]{:S(2)}) %collective-permute-start.33) | collective-permute-done | bytes 163872 | tf_op jit(solution)/shard_map/ppermute | solution.py:290
  187.7 5.3 %collective-permute-done.35.refs_1_ = bf16[10,32,256]{2,1,0:T(8,128)(2,1)S(1)} collective-permute-done((bf16[10,32,256]{2,1,0:T(8,128)(2,1)S(1)}, bf16[10,32,256]{2,1,0:T(8,128)(2,1)S(1)}, u32[]{:S(2)}, u32[]{:S(2)}) %collective-permute-start.35) | collective-permute-done | bytes 163872 | tf_op jit(solution)/shard_map/ppermute | solution.py:290
  198.1 4.0 %collective-permute-done.37.refs_1_ = bf16[20,32,256]{2,1,0:T(8,128)(2,1)S(1)} collective-permute-done((bf16[20,32,256]{2,1,0:T(8,128)(2,1)S(1)}, bf16[20,32,256]{2,1,0:T(8,128)(2,1)S(1)}, u32[]{:S(2)}, u32[]{:S(2)}) %collective-permute-start.37) | collective-permute-done | bytes 327712 | tf_op jit(solution)/shard_map/ppermute | solution.py:290
  207.3 4.3 %grad_tokens.4 = (bf16[320,64,256]{2,1,0:T(8,128)(2,1)}, f32[8,128]{1,0:T(8,128)S(1)}) custom-call(s32[80]{0:T(128)S(1)} %get-tuple-element.138.refs_7_.refs_11_.refs_0_, s32[1]{0:T(128)} %bitcast.5.refs_13_.refs_1_, bf16[80,2048]{1,0:T(8,128)(2,1)S(1)} %get-tuple-element.125.refs_2_, bf16[80,32,256]{2,1,0:T(8,128)(2,1)S(1)} %join.16.refs_2_.refs_5_.refs_3_, ...), custom_call_target="tpu_custom_call" | custom-call | tf_op jit(solution)/shard_map/grad_tokens/pallas_call | solution.py:42
  211.6 4.3 %grad_tokens.5 = (bf16[320,64,256]{2,1,0:T(8,128)(2,1)}, f32[8,128]{1,0:T(8,128)S(1)}) custom-call(s32[80]{0:T(128)S(1)} %get-tuple-element.139.refs_0_.refs_8_.refs_12_, s32[1]{0:T(128)} %bitcast.6.refs_1_.refs_14_, bf16[80,2048]{1,0:T(8,128)(2,1)S(1)} %get-tuple-element.124.refs_2_, ...), custom_call_target="tpu_custom_call", output_to_operand_aliasing={{0}: (6, {})} | custom-call | tf_op jit(solution)/shard_map/grad_tokens/pallas_call | solution.py:42
  216.1 5.1 %collective-permute-start.44 = (bf16[512,1024]{1,0:T(8,128)(2,1)S(1)}, bf16[512,1024]{1,0:T(8,128)(2,1)S(1)}, u32[]{:S(2)}, u32[]{:S(2)}) collective-permute-start(bf16[512,1024]{1,0:T(8,128)(2,1)S(1)} %get-tuple-element.123.refs_2_), channel_id=1, source_target_pairs={{0,96},{1,33},{2,98},{3,35},{4,100},{5,37},{6,102},{7,39},{8,104},... | collective-permute-start | bytes 3145736 | tf_op jit(solution)/shard_map/ppermute | solution.py:298
  224.9 9.0 %collective-permute-done.44.refs_1_ = bf16[512,1024]{1,0:T(8,128)(2,1)S(1)} collective-permute-done((bf16[512,1024]{1,0:T(8,128)(2,1)S(1)}, bf16[512,1024]{1,0:T(8,128)(2,1)S(1)}, u32[]{:S(2)}, u32[]{:S(2)}) %collective-permute-start.44) | collective-permute-done | bytes 1048608 | tf_op jit(solution)/shard_map/ppermute | solution.py:298
  239.3 3.3 %collective-permute-start.45 = (f32[40,128]{1,0:T(8,128)S(1)}, f32[40,128]{1,0:T(8,128)S(1)}, u32[]{:S(2)}, u32[]{:S(2)}) collective-permute-start(f32[40,128]{1,0:T(8,128)S(1)} %add.183.refs_7_.refs_0_), channel_id=1, source_target_pairs={{0,96},{1,33},{2,98},{3,35},{4,100},{5,37},{6,102},{7,39},{8,104},... | collective-permute-start | bytes 61448 | tf_op jit(solution)/shard_map/ppermute | solution.py:298
  242.6 4.3 %grad_tokens.6 = (bf16[320,64,256]{2,1,0:T(8,128)(2,1)}, f32[8,128]{1,0:T(8,128)S(1)}) custom-call(s32[80]{0:T(128)S(1)} %get-tuple-element.138.refs_7_.refs_11_.refs_0_, s32[1]{0:T(128)} %bitcast.3.refs_9_.refs_1_, bf16[80,2048]{1,0:T(8,128)(2,1)S(1)} %get-tuple-element.129.refs_2_, ...), custom_call_target="tpu_custom_call", output_to_operand_aliasing={{0}: (6, {})} | custom-call | tf_op jit(solution)/shard_map/grad_tokens/pallas_call | solution.py:42
  248.0 4.3 %grad_tokens.7 = (bf16[320,64,256]{2,1,0:T(8,128)(2,1)}, f32[8,128]{1,0:T(8,128)S(1)}) custom-call(s32[80]{0:T(128)S(1)} %get-tuple-element.139.refs_0_.refs_8_.refs_12_, s32[1]{0:T(128)} %bitcast.refs_10_.refs_1_, bf16[80,2048]{1,0:T(8,128)(2,1)S(1)} %get-tuple-element.98.refs_2_, ...), custom_call_target="tpu_custom_call", output_to_operand_aliasing={{0}: (6, {})} | custom-call | tf_op jit(solution)/shard_map/grad_tokens/pallas_call | solution.py:42
  (151 shorter events, 100.3 us)
Async XLA Ops:
  14.3 10.6 %collective-permute-start.3 = (bf16[40,32,256]{2,1,0:T(8,128)(2,1)S(1)}, bf16[40,32,256]{2,1,0:T(8,128)(2,1)S(1)}, u32[]{:S(2)}, u32[]{:S(2)}) collective-permute-start(bf16[40,32,256]{2,1,0:T(8,128)(2,1)S(1)} %get-tuple-element.73.refs_4_), channel_id=1, source_target_pairs={{0,4},{1,13},{2,6},{3,15},{4,0},{5,9},{6,2},{7,11},{8,12},{9,5},{1... | collective-permute-start | bytes 1966088 | tf_op jit(solution)/shard_map/ppermute | solution.py:290
  18.7 16.7 %collective-permute-start.2 = (bf16[40,32,256]{2,1,0:T(8,128)(2,1)S(1)}, bf16[40,32,256]{2,1,0:T(8,128)(2,1)S(1)}, u32[]{:S(2)}, u32[]{:S(2)}) collective-permute-start(bf16[40,32,256]{2,1,0:T(8,128)(2,1)S(1)} %get-tuple-element.77.refs_2_), channel_id=1, source_target_pairs={{0,4},{1,13},{2,6},{3,15},{4,0},{5,9},{6,2},{7,11},{8,12},{9,5},{1... | collective-permute-start | bytes 1966088 | tf_op jit(solution)/shard_map/ppermute | solution.py:290
  25.0 11.1 %collective-permute-start.5 = (bf16[20,32,256]{2,1,0:T(8,128)(2,1)S(1)}, bf16[20,32,256]{2,1,0:T(8,128)(2,1)S(1)}, u32[]{:S(2)}, u32[]{:S(2)}) collective-permute-start(bf16[20,32,256]{2,1,0:T(8,128)(2,1)S(1)} %get-tuple-element.79.refs_2_), channel_id=1, source_target_pairs={{0,12},{1,5},{2,14},{3,7},{4,8},{5,1},{6,10},{7,3},{8,4},{9,13},{1... | collective-permute-start | bytes 983048 | tf_op jit(solution)/shard_map/ppermute | solution.py:290
  35.6 7.2 %collective-permute-start.4 = (bf16[20,32,256]{2,1,0:T(8,128)(2,1)S(1)}, bf16[20,32,256]{2,1,0:T(8,128)(2,1)S(1)}, u32[]{:S(2)}, u32[]{:S(2)}) collective-permute-start(bf16[20,32,256]{2,1,0:T(8,128)(2,1)S(1)} %get-tuple-element.81.refs_2_), channel_id=1, source_target_pairs={{0,12},{1,5},{2,14},{3,7},{4,8},{5,1},{6,10},{7,3},{8,4},{9,13},{1... | collective-permute-start | bytes 983048 | tf_op jit(solution)/shard_map/ppermute | solution.py:290
  36.2 10.5 %collective-permute-start.7 = (bf16[10,32,256]{2,1,0:T(8,128)(2,1)S(1)}, bf16[10,32,256]{2,1,0:T(8,128)(2,1)S(1)}, u32[]{:S(2)}, u32[]{:S(2)}) collective-permute-start(bf16[10,32,256]{2,1,0:T(8,128)(2,1)S(1)} %get-tuple-element.83.refs_2_), channel_id=1, source_target_pairs={{0,2},{1,3},{2,0},{3,1},{4,6},{5,7},{6,4},{7,5},{8,10},{9,11},{10,... | collective-permute-start | bytes 491528 | tf_op jit(solution)/shard_map/ppermute | solution.py:290
  42.8 8.7 %collective-permute-start.6 = (bf16[10,32,256]{2,1,0:T(8,128)(2,1)S(1)}, bf16[10,32,256]{2,1,0:T(8,128)(2,1)S(1)}, u32[]{:S(2)}, u32[]{:S(2)}) collective-permute-start(bf16[10,32,256]{2,1,0:T(8,128)(2,1)S(1)} %get-tuple-element.85.refs_2_), channel_id=1, source_target_pairs={{0,2},{1,3},{2,0},{3,1},{4,6},{5,7},{6,4},{7,5},{8,10},{9,11},{10,... | collective-permute-start | bytes 491528 | tf_op jit(solution)/shard_map/ppermute | solution.py:290
  46.8 6.9 %collective-permute-start.9 = (bf16[10,32,256]{2,1,0:T(8,128)(2,1)S(1)}, bf16[10,32,256]{2,1,0:T(8,128)(2,1)S(1)}, u32[]{:S(2)}, u32[]{:S(2)}) collective-permute-start(bf16[10,32,256]{2,1,0:T(8,128)(2,1)S(1)} %add.163.refs_2_.refs_0_), channel_id=1, source_target_pairs={{0,2},{1,3},{2,0},{3,1},{4,6},{5,7},{6,4},{7,5},{8,10},{9,11},{10,... | collective-permute-start | bytes 491528 | tf_op jit(solution)/shard_map/ppermute | solution.py:290
  53.7 7.5 %collective-permute-start.11 = (bf16[20,32,256]{2,1,0:T(8,128)(2,1)S(1)}, bf16[20,32,256]{2,1,0:T(8,128)(2,1)S(1)}, u32[]{:S(2)}, u32[]{:S(2)}) collective-permute-start(bf16[20,32,256]{2,1,0:T(8,128)(2,1)S(1)} %join.12.refs_2_.refs_0_), channel_id=1, source_target_pairs={{0,12},{1,5},{2,14},{3,7},{4,8},{5,1},{6,10},{7,3},{8,4},{9,13},{1... | collective-permute-start | bytes 983048 | tf_op jit(solution)/shard_map/ppermute | solution.py:290
  61.3 12.7 %collective-permute-start.13 = (bf16[40,32,256]{2,1,0:T(8,128)(2,1)S(1)}, bf16[40,32,256]{2,1,0:T(8,128)(2,1)S(1)}, u32[]{:S(2)}, u32[]{:S(2)}) collective-permute-start(bf16[40,32,256]{2,1,0:T(8,128)(2,1)S(1)} %join.14.refs_2_.refs_0_), channel_id=1, source_target_pairs={{0,4},{1,13},{2,6},{3,15},{4,0},{5,9},{6,2},{7,11},{8,12},{9,5},{1... | collective-permute-start | bytes 1966088 | tf_op jit(solution)/shard_map/ppermute | solution.py:290
  65.4 7.1 %collective-permute-start.10 = (bf16[20,32,256]{2,1,0:T(8,128)(2,1)S(1)}, bf16[20,32,256]{2,1,0:T(8,128)(2,1)S(1)}, u32[]{:S(2)}, u32[]{:S(2)}) collective-permute-start(bf16[20,32,256]{2,1,0:T(8,128)(2,1)S(1)} %join.13.refs_2_.refs_0_), channel_id=1, source_target_pairs={{0,12},{1,5},{2,14},{3,7},{4,8},{5,1},{6,10},{7,3},{8,4},{9,13},{1... | collective-permute-start | bytes 983048 | tf_op jit(solution)/shard_map/ppermute | solution.py:290
  74.2 10.7 %collective-permute-start.12 = (bf16[40,32,256]{2,1,0:T(8,128)(2,1)S(1)}, bf16[40,32,256]{2,1,0:T(8,128)(2,1)S(1)}, u32[]{:S(2)}, u32[]{:S(2)}) collective-permute-start(bf16[40,32,256]{2,1,0:T(8,128)(2,1)S(1)} %join.15.refs_2_.refs_0_), channel_id=1, source_target_pairs={{0,4},{1,13},{2,6},{3,15},{4,0},{5,9},{6,2},{7,11},{8,12},{9,5},{1... | collective-permute-start | bytes 1966088 | tf_op jit(solution)/shard_map/ppermute | solution.py:290
  85.0 6.9 %collective-permute-start.15 = (bf16[80,32,256]{2,1,0:T(8,128)(2,1)S(1)}, bf16[80,32,256]{2,1,0:T(8,128)(2,1)S(1)}, u32[]{:S(2)}, u32[]{:S(2)}) collective-permute-start(bf16[80,32,256]{2,1,0:T(8,128)(2,1)S(1)} %join.17.refs_2_.refs_5_.refs_3_), channel_id=1, source_target_pairs={{0,1},{1,0},{2,3},{3,2},{4,5},{5,4},{6,7},{7,6},{8,9},{9,8},{10,11... | collective-permute-start | bytes 3932168 | tf_op jit(solution)/shard_map/ppermute | solution.py:290
  97.5 8.1 %collective-permute-start.19 = (bf16[80,1024]{1,0:T(8,128)(2,1)S(1)}, bf16[80,1024]{1,0:T(8,128)(2,1)S(1)}, u32[]{:S(2)}, u32[]{:S(2)}) collective-permute-start(bf16[80,1024]{1,0:T(8,128)(2,1)S(1)} %add.167.refs_2_.refs_0_), channel_id=1, source_target_pairs={{0,4},{1,13},{2,6},{3,15},{4,0},{5,9},{6,2},{7,11},{8,12},{9,5},{1... | collective-permute-start | bytes 491528 | tf_op jit(solution)/shard_map/ppermute | solution.py:290
  116.3 8.4 %collective-permute-start.26 = (bf16[80,32,256]{2,1,0:T(8,128)(2,1)S(1)}, bf16[80,32,256]{2,1,0:T(8,128)(2,1)S(1)}, u32[]{:S(2)}, u32[]{:S(2)}) collective-permute-start(bf16[80,32,256]{2,1,0:T(8,128)(2,1)S(1)} %get-tuple-element.95.refs_7_), channel_id=1, source_target_pairs={{0,1},{1,0},{2,3},{3,2},{4,5},{5,4},{6,7},{7,6},{8,9},{9,8},{10,11... | collective-permute-start | bytes 3932168 | tf_op jit(solution)/shard_map/ppermute | solution.py:290
  116.5 8.0 %collective-permute-start.23 = (bf16[80,1024]{1,0:T(8,128)(2,1)S(1)}, bf16[80,1024]{1,0:T(8,128)(2,1)S(1)}, u32[]{:S(2)}, u32[]{:S(2)}) collective-permute-start(bf16[80,1024]{1,0:T(8,128)(2,1)S(1)} %add.171.refs_7_.refs_0_), channel_id=1, source_target_pairs={{0,2},{1,3},{2,0},{3,1},{4,6},{5,7},{6,4},{7,5},{8,10},{9,11},{10,... | collective-permute-start | bytes 491528 | tf_op jit(solution)/shard_map/ppermute | solution.py:290
  130.8 14.0 %collective-permute-start.27 = (bf16[80,32,256]{2,1,0:T(8,128)(2,1)S(1)}, bf16[80,32,256]{2,1,0:T(8,128)(2,1)S(1)}, u32[]{:S(2)}, u32[]{:S(2)}) collective-permute-start(bf16[80,32,256]{2,1,0:T(8,128)(2,1)S(1)} %get-tuple-element.99.refs_7_), channel_id=1, source_target_pairs={{0,1},{1,0},{2,3},{3,2},{4,5},{5,4},{6,7},{7,6},{8,9},{9,8},{10,11... | collective-permute-start | bytes 3932168 | tf_op jit(solution)/shard_map/ppermute | solution.py:290
  131.0 11.9 %collective-permute-start.28 = (bf16[40,32,256]{2,1,0:T(8,128)(2,1)S(1)}, bf16[40,32,256]{2,1,0:T(8,128)(2,1)S(1)}, u32[]{:S(2)}, u32[]{:S(2)}) collective-permute-start(bf16[40,32,256]{2,1,0:T(8,128)(2,1)S(1)} %get-tuple-element.97.refs_7_), channel_id=1, source_target_pairs={{0,4},{1,13},{2,6},{3,15},{4,0},{5,9},{6,2},{7,11},{8,12},{9,5},{1... | collective-permute-start | bytes 1966088 | tf_op jit(solution)/shard_map/ppermute | solution.py:290
  143.0 7.2 %collective-permute-start.30 = (bf16[20,32,256]{2,1,0:T(8,128)(2,1)S(1)}, bf16[20,32,256]{2,1,0:T(8,128)(2,1)S(1)}, u32[]{:S(2)}, u32[]{:S(2)}) collective-permute-start(bf16[20,32,256]{2,1,0:T(8,128)(2,1)S(1)} %get-tuple-element.102.refs_2_), channel_id=1, source_target_pairs={{0,12},{1,5},{2,14},{3,7},{4,8},{5,1},{6,10},{7,3},{8,4},{9,13},{1... | collective-permute-start | bytes 983048 | tf_op jit(solution)/shard_map/ppermute | solution.py:290
  152.7 40.3 %collective-permute-start.39 = (bf16[1024,1024]{1,0:T(8,128)(2,1)S(1)}, bf16[1024,1024]{1,0:T(8,128)(2,1)S(1)}, u32[]{:S(2)}, u32[]{:S(2)}) collective-permute-start(bf16[1024,1024]{1,0:T(8,128)(2,1)S(1)} %get-tuple-element.122), channel_id=1, source_target_pairs={{0,32},{1,97},{2,34},{3,99},{4,36},{5,101},{6,38},{7,103},{8,40},{... | collective-permute-start | bytes 6291464 | tf_op jit(solution)/shard_map/ppermute | solution.py:298
  154.3 11.8 %collective-permute-start.29 = (bf16[40,32,256]{2,1,0:T(8,128)(2,1)S(1)}, bf16[40,32,256]{2,1,0:T(8,128)(2,1)S(1)}, u32[]{:S(2)}, u32[]{:S(2)}) collective-permute-start(bf16[40,32,256]{2,1,0:T(8,128)(2,1)S(1)} %get-tuple-element.104.refs_2_), channel_id=1, source_target_pairs={{0,4},{1,13},{2,6},{3,15},{4,0},{5,9},{6,2},{7,11},{8,12},{9,5},{1... | collective-permute-start | bytes 1966088 | tf_op jit(solution)/shard_map/ppermute | solution.py:290
  157.5 10.5 %collective-permute-start.32 = (bf16[10,32,256]{2,1,0:T(8,128)(2,1)S(1)}, bf16[10,32,256]{2,1,0:T(8,128)(2,1)S(1)}, u32[]{:S(2)}, u32[]{:S(2)}) collective-permute-start(bf16[10,32,256]{2,1,0:T(8,128)(2,1)S(1)} %get-tuple-element.114.refs_8_), channel_id=1, source_target_pairs={{0,2},{1,3},{2,0},{3,1},{4,6},{5,7},{6,4},{7,5},{8,10},{9,11},{10,... | collective-permute-start | bytes 491528 | tf_op jit(solution)/shard_map/ppermute | solution.py:290
  166.3 7.2 %collective-permute-start.31 = (bf16[20,32,256]{2,1,0:T(8,128)(2,1)S(1)}, bf16[20,32,256]{2,1,0:T(8,128)(2,1)S(1)}, u32[]{:S(2)}, u32[]{:S(2)}) collective-permute-start(bf16[20,32,256]{2,1,0:T(8,128)(2,1)S(1)} %get-tuple-element.117.refs_2_), channel_id=1, source_target_pairs={{0,12},{1,5},{2,14},{3,7},{4,8},{5,1},{6,10},{7,3},{8,4},{9,13},{1... | collective-permute-start | bytes 983048 | tf_op jit(solution)/shard_map/ppermute | solution.py:290
  168.1 7.4 %collective-permute-start.34 = (bf16[10,32,256]{2,1,0:T(8,128)(2,1)S(1)}, bf16[10,32,256]{2,1,0:T(8,128)(2,1)S(1)}, u32[]{:S(2)}, u32[]{:S(2)}) collective-permute-start(bf16[10,32,256]{2,1,0:T(8,128)(2,1)S(1)} %add.178.refs_2_.refs_0_), channel_id=1, source_target_pairs={{0,2},{1,3},{2,0},{3,1},{4,6},{5,7},{6,4},{7,5},{8,10},{9,11},{10,... | collective-permute-start | bytes 491528 | tf_op jit(solution)/shard_map/ppermute | solution.py:290
  175.5 8.5 %collective-permute-start.36 = (bf16[20,32,256]{2,1,0:T(8,128)(2,1)S(1)}, bf16[20,32,256]{2,1,0:T(8,128)(2,1)S(1)}, u32[]{:S(2)}, u32[]{:S(2)}) collective-permute-start(bf16[20,32,256]{2,1,0:T(8,128)(2,1)S(1)} %join.18.refs_2_.refs_0_), channel_id=1, source_target_pairs={{0,12},{1,5},{2,14},{3,7},{4,8},{5,1},{6,10},{7,3},{8,4},{9,13},{1... | collective-permute-start | bytes 983048 | tf_op jit(solution)/shard_map/ppermute | solution.py:290
  184.1 10.7 %collective-permute-start.38 = (bf16[40,32,256]{2,1,0:T(8,128)(2,1)S(1)}, bf16[40,32,256]{2,1,0:T(8,128)(2,1)S(1)}, u32[]{:S(2)}, u32[]{:S(2)}) collective-permute-start(bf16[40,32,256]{2,1,0:T(8,128)(2,1)S(1)} %join.19.refs_2_.refs_0_), channel_id=1, source_target_pairs={{0,4},{1,13},{2,6},{3,15},{4,0},{5,9},{6,2},{7,11},{8,12},{9,5},{1... | collective-permute-start | bytes 1966088 | tf_op jit(solution)/shard_map/ppermute | solution.py:290
  194.8 10.6 %collective-permute-start.41 = (bf16[80,32,256]{2,1,0:T(8,128)(2,1)S(1)}, bf16[80,32,256]{2,1,0:T(8,128)(2,1)S(1)}, u32[]{:S(2)}, u32[]{:S(2)}) collective-permute-start(bf16[80,32,256]{2,1,0:T(8,128)(2,1)S(1)} %join.21.refs_1_.refs_4_), channel_id=1, source_target_pairs={{0,1},{1,0},{2,3},{3,2},{4,5},{5,4},{6,7},{7,6},{8,9},{9,8},{10,11... | collective-permute-start | bytes 3932168 | tf_op jit(solution)/shard_map/ppermute | solution.py:290
  194.9 7.2 %collective-permute-start.37 = (bf16[20,32,256]{2,1,0:T(8,128)(2,1)S(1)}, bf16[20,32,256]{2,1,0:T(8,128)(2,1)S(1)}, u32[]{:S(2)}, u32[]{:S(2)}) collective-permute-start(bf16[20,32,256]{2,1,0:T(8,128)(2,1)S(1)} %join.20.refs_2_.refs_0_), channel_id=1, source_target_pairs={{0,12},{1,5},{2,14},{3,7},{4,8},{5,1},{6,10},{7,3},{8,4},{9,13},{1... | collective-permute-start | bytes 983048 | tf_op jit(solution)/shard_map/ppermute | solution.py:290
  202.1 13.7 %collective-permute-start.40 = (bf16[40,32,256]{2,1,0:T(8,128)(2,1)S(1)}, bf16[40,32,256]{2,1,0:T(8,128)(2,1)S(1)}, u32[]{:S(2)}, u32[]{:S(2)}) collective-permute-start(bf16[40,32,256]{2,1,0:T(8,128)(2,1)S(1)} %join.22.refs_4_.refs_0_), channel_id=1, source_target_pairs={{0,4},{1,13},{2,6},{3,15},{4,0},{5,9},{6,2},{7,11},{8,12},{9,5},{1... | collective-permute-start | bytes 1966088 | tf_op jit(solution)/shard_map/ppermute | solution.py:290
  216.0 7.1 %collective-permute-start.42 = (bf16[80,32,256]{2,1,0:T(8,128)(2,1)S(1)}, bf16[80,32,256]{2,1,0:T(8,128)(2,1)S(1)}, u32[]{:S(2)}, u32[]{:S(2)}) collective-permute-start(bf16[80,32,256]{2,1,0:T(8,128)(2,1)S(1)} %join.23.refs_1_.refs_4_), channel_id=1, source_target_pairs={{0,1},{1,0},{2,3},{3,2},{4,5},{5,4},{6,7},{7,6},{8,9},{9,8},{10,11... | collective-permute-start | bytes 3932168 | tf_op jit(solution)/shard_map/ppermute | solution.py:290
  216.1 17.9 %collective-permute-start.44 = (bf16[512,1024]{1,0:T(8,128)(2,1)S(1)}, bf16[512,1024]{1,0:T(8,128)(2,1)S(1)}, u32[]{:S(2)}, u32[]{:S(2)}) collective-permute-start(bf16[512,1024]{1,0:T(8,128)(2,1)S(1)} %get-tuple-element.123.refs_2_), channel_id=1, source_target_pairs={{0,96},{1,33},{2,98},{3,35},{4,100},{5,37},{6,102},{7,39},{8,104},... | collective-permute-start | bytes 3145736 | tf_op jit(solution)/shard_map/ppermute | solution.py:298
  234.4 17.9 %collective-permute-start.46 = (bf16[256,1024]{1,0:T(8,128)(2,1)S(1)}, bf16[256,1024]{1,0:T(8,128)(2,1)S(1)}, u32[]{:S(2)}, u32[]{:S(2)}) collective-permute-start(bf16[256,1024]{1,0:T(8,128)(2,1)S(1)} %get-tuple-element.132.refs_2_), channel_id=1, source_target_pairs={{0,16},{1,17},{2,18},{3,19},{4,20},{5,21},{6,22},{7,23},{8,24},{9,... | collective-permute-start | bytes 1572872 | tf_op jit(solution)/shard_map/ppermute | solution.py:298
  239.3 7.6 %collective-permute-start.45 = (f32[40,128]{1,0:T(8,128)S(1)}, f32[40,128]{1,0:T(8,128)S(1)}, u32[]{:S(2)}, u32[]{:S(2)}) collective-permute-start(f32[40,128]{1,0:T(8,128)S(1)} %add.183.refs_7_.refs_0_), channel_id=1, source_target_pairs={{0,96},{1,33},{2,98},{3,35},{4,100},{5,37},{6,102},{7,39},{8,104},... | collective-permute-start | bytes 61448 | tf_op jit(solution)/shard_map/ppermute | solution.py:298
  (21 other events, 113.0 us)

commit v3 on v2

--- a/solution.py
+++ b/solution.py
@@ -9,14 +9,15 @@
 bf = jnp.bfloat16
 T, K, D, H = 64, 32, 256, 1024
 EB = 16
+PITCH = T + 1
 NCH = 2
 ORDERS = (("ABZ", "BAZ"), ("ABZ", "BAZ"))
 DP_ORDERS = ("ABZ", "BAZ")
 ORDER = (
-    1, 1, 1, 0, 0, 0, 1, 0, 1, 0, 1, 0, 1, 0, 1, 0, 1, 1, 1, 0,
-    0, 1, 0, 1, 0, 1, 0, 1, 0, 1, 1, 0, 1, 0, 0, 1, 0, 1, "w", 0,
-    1, 0, 1, 0, 1, 0, "w", 1, 1, 0, 1, 1, 1, 0, 0, 0, "s", "w", "s", 0,
-    "s", 0, "w", "s",
+    0, 0, 0, 1, 1, 1, 0, 1, 0, 1, 0, 1, 0, 1, 0, 1, 0, 0, 0, 1,
+    0, 1, 1, 0, 1, 0, 1, 0, 1, 0, 0, 1, 0, 1, 1, 1, "w", 0, 1, 0,
+    1, 0, 1, 0, "w", 1, 0, 1, 0, 0, "w", 0, 1, 0, 1, 1, "s", 1, "w", "s",
+    0, "s", 1, "s",
 )
 
 
@@ -47,6 +48,7 @@
         scratch_shapes=scratch,
         input_output_aliases=alias or {},
         compiler_params=pltpu.CompilerParams(vmem_limit_bytes=8 * 1024 * 1024),
+        cost_estimate=pl.CostEstimate(flops=int(2e10), bytes_accessed=1000, transcendentals=0),
         name=name,
     )(*smem, *vmem, *far, *chain.last)
     chain.last = [result[-1]]
@@ -90,14 +92,14 @@
         def _(i):
             for e in range(EB):
                 c = comp[tbl[i * EB + e]]
-                sc[T * e : T * e + T, :K] = lax.dot_general(
+                sc[PITCH * e : PITCH * e + T, :K] = lax.dot_general(
                     x[i * EB + e], c, (((1,), (1,)), ((), ())), preferred_element_type=f32
                 )
             rows = pl.ds(pl.multiple_of(i * EB, EB), EB)
             for g in range(T // 4):
-                acc = sc[pl.ds(4 * g, EB, stride=T), :]
+                acc = sc[pl.ds(4 * g, EB, stride=PITCH), :]
                 for j in range(1, 4):
-                    v = pltpu.roll(sc[pl.ds(4 * g + j, EB, stride=T), :], K * j, 1)
+                    v = pltpu.roll(sc[pl.ds(4 * g + j, EB, stride=PITCH), :], K * j, 1)
                     acc = jnp.where(lane == j, v, acc)
                 flat[rows, 128 * g : 128 * g + 128] = acc.astype(bf)
             for j in range(8):
@@ -108,7 +110,7 @@
             at = slice(256 * j, 256 * j + 256)
             hidden[:, at] = jnp.dot(flat[...], w[:, at], preferred_element_type=f32).astype(bf)
 
-    scratch = [pltpu.VMEM((EB * T, 128), f32), pltpu.VMEM((n, T * K), bf)]
+    scratch = [pltpu.VMEM((EB * PITCH, 128), f32), pltpu.VMEM((n, T * K), bf)]
     return call(chain, body, "field", [shape(n, T * K), shape(n, H)], scratch, [tbl, perm], [comp, x, w])
 
 
@@ -120,7 +122,7 @@
             w = v if j == 0 else pltpu.roll(v, 128 - K * j, 1)
             if tail is not None:
                 w = jnp.where(lane < K, w, tail[4 * g + j : 4 * g + j + 1, :])
-            sc[pl.ds(4 * g + j, EB, stride=T), :] = w
+            sc[pl.ds(4 * g + j, EB, stride=PITCH), :] = w
 
 
 def silu_grad(value):
@@ -148,12 +150,12 @@
         def _(i):
             spread(df, pl.ds(pl.multiple_of(i * EB, EB), EB), sc)
             for e in range(EB):
-                s = sc[T * e : T * e + T, :K].astype(bf)
+                s = sc[PITCH * e : PITCH * e + T, :K].astype(bf)
                 r = lax.dot_general(s, x[i * EB + e], (((0,), (0,)), ((), ())), preferred_element_type=f32)
                 out[tbl[i * EB + e]] = r.astype(bf)
 
     outs = [shape(n, H), shape(n, T * K), shape(n, K, D)]
-    scratch = [pltpu.VMEM((EB * T, 128), f32)]
+    scratch = [pltpu.VMEM((EB * PITCH, 128), f32)]
     return call(chain, body, "grad_compress", outs, scratch, [tbl, blk], [pre, up, bias, x, w])
 
 
@@ -211,7 +213,7 @@
         def _(i):
             spread(df, pl.ds(pl.multiple_of(i * EB, EB), EB), sc, tail)
             for e in range(EB):
-                s = sc[T * e : T * e + T, : 2 * K].astype(bf)
+                s = sc[PITCH * e : PITCH * e + T, : 2 * K].astype(bf)
                 at = tbl[i * EB + e]
                 w = jnp.concatenate([comp[at], dcomp[at]], axis=0)
                 ov[i * EB + e] = jnp.dot(s, w, preferred_element_type=f32).astype(bf)
@@ -221,7 +223,7 @@
             copy(i).wait()
 
     outs = [pltpu.HBM(dims, bf), shape(8, 128, dtype=f32)]
-    scratch = [pltpu.VMEM((n, T, D), bf), pltpu.SemaphoreType.DMA((n // EB,)), pltpu.VMEM((EB * T, 128), f32)]
+    scratch = [pltpu.VMEM((n, T, D), bf), pltpu.SemaphoreType.DMA((n // EB,)), pltpu.VMEM((EB * PITCH, 128), f32)]
     alias = {6: 0} if far else None
     return call(chain, body, "grad_tokens", outs, scratch, [tbl, blk], [df, comp, dcomp, tail], far, alias)[0]
 
@@ -242,6 +244,15 @@
 
     outs = call(chain, body, "add", [shape(m, *rest, dtype=dtype)] * (n // m), [], [], [a, b])
     return outs if cut else outs[0]
+
+
+def split_sums(chain, a, b):
+    def body(a, b, gp, gb):
+        gp[...] = (a[:K, :T] + b[:K, :T]).T
+        gb[...] = a[K:, :] + b[K:, :]
+
+    outs = [shape(T, K, dtype=f32), shape(H // 128, 128, dtype=f32)]
+    return call(chain, body, "add", outs, [], [], [a, b])
 
 
 def join_rows(chain, a, b):
@@ -304,19 +315,18 @@
     tok = lax.axis_index("tok")
     core = tok & 1
     bits, dbits = tok_bits(tok), dp_bits(lax.axis_index("dp"))
-    own = jnp.where(core == 0, place(dbits, DP_ORDERS[0]), place(dbits, DP_ORDERS[1]))
-    owners = []
+    own = jnp.where(core == 0, place(dbits, DP_ORDERS[0]), place(dbits, DP_ORDERS[1])) ^ jnp.arange(8, dtype=jnp.int32)
+    digits = (own >> 2, (own >> 1) & 1, own & 1)
+    blocks = []
     for order in DP_ORDERS:
-        table = [0] * 8
-        for d in range(8):
-            table[place(dp_bits(d), order)] = d
-        owners.append(table)
-    owners = jnp.asarray(owners, jnp.int32)[core]
-    perm = owners[own ^ jnp.arange(8)].astype(jnp.int32)
-
-    pt = jnp.tile(projection.T, (4, 4))
-    same = (jnp.arange(4 * K)[:, None] // K) == (jnp.arange(4 * T)[None] // T)
-    pt4 = jnp.where(same, pt, 0).astype(bf)
+        at = dict(zip(order, digits))
+        g = at["A"] + 2 * at["B"]
+        blocks.append((g ^ (g >> 1)) * 2 + at["Z"])
+    perm = jnp.where(core == 0, blocks[0], blocks[1])
+
+    pt4 = sum(
+        jnp.pad(projection.T.astype(f32), ((K * j, 3 * K - K * j), (T * j, 3 * T - T * j))) for j in range(4)
+    ).astype(bf)
     tail = jnp.pad(projection.astype(f32), ((0, 0), (K, 128 - 2 * K)))
     bias = mlp_bias.reshape(1, H)
 
@@ -410,17 +420,17 @@
         for step in range(3):
             got = dp_swap(x, step)
             yield
-            x = add_rows(chain, x, got, dtype=f32)
-        done["sums"] = x
+            if step < 2:
+                x = add_rows(chain, x, got, dtype=f32)
+        done["sums"] = split_sums(chain, x, got)
         yield
 
     steps = {c: chunk(c) for c in range(NCH)}
     steps["w"], steps["s"] = weight(), sums()
     for who in ORDER:
         next(steps[who])
-    grad_p = done["sums"][:K, :T].T
-    grad_b = done["sums"][K:].reshape(H)
-    return done["gx"], done["w"], grad_p, grad_b
+    grad_p, grad_b = done["sums"]
+    return done["gx"], done["w"], grad_p, grad_b.reshape(H)
 
 
 def solution(mesh):

time: 256 us -> 218 us (0.85); the launches traced: 256 us -> 214 us
  waiting for transfers between devices: 96.9 us -> 62.3 us
  Pallas kernels: 79.7 us -> 70.3 us
  starting transfers between devices: 71.6 us -> 75 us
    ppermute x42, waiting for transfers between devices: 85.3 us -> 62.3 us  [tok_swap(): return lax.ppermute(x, 'tok', pairs)]
    ppermute x6, waiting for transfers between devices: 11.6 us -> 0.03 us  [dp_swap(): return lax.ppermute(x, ('dp', 'tok'), pairs)]
    pallas_call x63, Pallas kernels: 79.7 us -> 70.3 us  [call(): pl.pallas_call(run, out_shape=outs, in_specs=specs, out_specs=[place(out)...]
    ppermute x42, starting transfers between devices: 58.1 us -> 64.6 us  [tok_swap(): return lax.ppermute(x, 'tok', pairs)]
    ppermute x6, starting transfers between devices: 13.5 us -> 10.3 us  [dp_swap(): return lax.ppermute(x, ('dp', 'tok'), pairs)]
  transfers between devices with their start and end apart: 48 -> 48, of which waited for: 28 -> 23; matrix products, arithmetic and copies ran while one was open for 0% -> 0% of each run, Pallas kernels for 24% -> 31%
where the time goes in v3:
time: 218 us; the launch traced here: 214 us
  starting transfers between devices  75 us (34%)
  Pallas kernels  70.3 us (32%)
  waiting for transfers between devices  62.3 us (29%)
  local copies, waits for them, and re-layouts  4.02 us (2%)
    pallas_call x63, Pallas kernels, call(): pl.pallas_call(run, out_shape=outs, in_specs=specs, out_specs=[place(out)...  70.3 us
    ppermute x42, starting transfers between devices, tok_swap(): return lax.ppermute(x, 'tok', pairs)  64.6 us
    ppermute x42, waiting for transfers between devices, tok_swap(): return lax.ppermute(x, 'tok', pairs)  62.3 us
    ppermute x6, starting transfers between devices, dp_swap(): return lax.ppermute(x, ('dp', 'tok'), pairs)  10.3 us
  transfers between devices with their start and end apart: 48, of which 23 were waited for; matrix products, arithmetic and copies ran while one was open for 0% of the time, Pallas kernels for 31%

profile of v3, /device:TPU:4, one launch (start us, length us, event | category | flops | bytes accessed | tf_op | source)
XLA Modules:
  0.0 214.0 jit_solution(11550518136930489650)
XLA Ops:
  3.1 2.9 %compress.4 = (bf16[80,64,256]{2,1,0:T(8,128)(2,1)S(1)}, bf16[80,32,256]{2,1,0:T(8,128)(2,1)S(1)}) custom-call(s32[80]{0:T(128)S(1)} %get-tuple-element.147.refs_0_.refs_8_.refs_12_, s32[1]{0:T(128)} %bitcast.4.refs_1_.refs_10_, bf16[128,256]{1,0:T(8,128)(2,1)S(1)} %add_convert_fusion.refs_2_, bf16[320,64,256]{2,1,0:T(8,128)(2,1)} %refs_3_.11, ...), custom_call_target="tpu_custom_call" | custom-call | flops 20000000000 | bytes 1000 | tf_op jit(solution)/shard_map/compress/pallas_call | solution.py:43
  6.1 2.9 %compress.5 = (bf16[80,64,256]{2,1,0:T(8,128)(2,1)S(1)}, bf16[80,32,256]{2,1,0:T(8,128)(2,1)S(1)}) custom-call(s32[80]{0:T(128)S(1)} %get-tuple-element.146.refs_7_.refs_11_.refs_0_, s32[1]{0:T(128)} %bitcast.3.refs_9_.refs_1_, bf16[128,256]{1,0:T(8,128)(2,1)S(1)} %add_convert_fusion.refs_2_, bf16[320,64,256]{2,1,0:T(8,128)(2,1)} %refs_3_.11, ...), custom_call_target="tpu_custom_call" | custom-call | flops 20000000000 | bytes 1000 | tf_op jit(solution)/shard_map/compress/pallas_call | solution.py:43
  10.7 2.9 %compress.6 = (bf16[80,64,256]{2,1,0:T(8,128)(2,1)S(1)}, bf16[80,32,256]{2,1,0:T(8,128)(2,1)S(1)}) custom-call(s32[80]{0:T(128)S(1)} %get-tuple-element.147.refs_0_.refs_8_.refs_12_, s32[1]{0:T(128)} %bitcast.refs_14_.refs_1_, bf16[128,256]{1,0:T(8,128)(2,1)S(1)} %add_convert_fusion.refs_2_, bf16[320,64,256]{2,1,0:T(8,128)(2,1)} %refs_3_.11, ...), custom_call_target="tpu_custom_call" | custom-call | flops 20000000000 | bytes 1000 | tf_op jit(solution)/shard_map/compress/pallas_call | solution.py:43
  20.9 10.3 %collective-permute-done.2.refs_1_ = bf16[40,32,256]{2,1,0:T(8,128)(2,1)S(1)} collective-permute-done((bf16[40,32,256]{2,1,0:T(8,128)(2,1)S(1)}, bf16[40,32,256]{2,1,0:T(8,128)(2,1)S(1)}, u32[]{:S(2)}, u32[]{:S(2)}) %collective-permute-start.2) | collective-permute-done | bytes 655392 | tf_op jit(solution)/shard_map/ppermute | solution.py:301
  32.3 4.0 %collective-permute-start.7 = (bf16[10,32,256]{2,1,0:T(8,128)(2,1)S(1)}, bf16[10,32,256]{2,1,0:T(8,128)(2,1)S(1)}, u32[]{:S(2)}, u32[]{:S(2)}) collective-permute-start(bf16[10,32,256]{2,1,0:T(8,128)(2,1)S(1)} %get-tuple-element.85.refs_2_), channel_id=1, source_target_pairs={{0,2},{1,3},{2,0},{3,1},{4,6},{5,7},{6,4},{7,5},{8,10},{9,11},{10,... | collective-permute-start | bytes 491528 | tf_op jit(solution)/shard_map/ppermute | solution.py:301
  38.6 3.9 %collective-permute-start.6 = (bf16[10,32,256]{2,1,0:T(8,128)(2,1)S(1)}, bf16[10,32,256]{2,1,0:T(8,128)(2,1)S(1)}, u32[]{:S(2)}, u32[]{:S(2)}) collective-permute-start(bf16[10,32,256]{2,1,0:T(8,128)(2,1)S(1)} %get-tuple-element.87.refs_2_), channel_id=1, source_target_pairs={{0,2},{1,3},{2,0},{3,1},{4,6},{5,7},{6,4},{7,5},{8,10},{9,11},{10,... | collective-permute-start | bytes 491528 | tf_op jit(solution)/shard_map/ppermute | solution.py:301
  43.7 3.3 %collective-permute-done.6.refs_1_ = bf16[10,32,256]{2,1,0:T(8,128)(2,1)S(1)} collective-permute-done((bf16[10,32,256]{2,1,0:T(8,128)(2,1)S(1)}, bf16[10,32,256]{2,1,0:T(8,128)(2,1)S(1)}, u32[]{:S(2)}, u32[]{:S(2)}) %collective-permute-start.6) | collective-permute-done | bytes 163872 | tf_op jit(solution)/shard_map/ppermute | solution.py:301
  47.0 3.3 %collective-permute-start.8 = (bf16[10,32,256]{2,1,0:T(8,128)(2,1)S(1)}, bf16[10,32,256]{2,1,0:T(8,128)(2,1)S(1)}, u32[]{:S(2)}, u32[]{:S(2)}) collective-permute-start(bf16[10,32,256]{2,1,0:T(8,128)(2,1)S(1)} %add.181.refs_2_.refs_0_), channel_id=1, source_target_pairs={{0,2},{1,3},{2,0},{3,1},{4,6},{5,7},{6,4},{7,5},{8,10},{9,11},{10,... | collective-permute-start | bytes 491528 | tf_op jit(solution)/shard_map/ppermute | solution.py:301
  54.7 5.0 %collective-permute-done.11.refs_1_ = bf16[20,32,256]{2,1,0:T(8,128)(2,1)S(1)} collective-permute-done((bf16[20,32,256]{2,1,0:T(8,128)(2,1)S(1)}, bf16[20,32,256]{2,1,0:T(8,128)(2,1)S(1)}, u32[]{:S(2)}, u32[]{:S(2)}) %collective-permute-start.11) | collective-permute-done | bytes 327712 | tf_op jit(solution)/shard_map/ppermute | solution.py:301
  59.8 3.7 %collective-permute-start.13 = (bf16[40,32,256]{2,1,0:T(8,128)(2,1)S(1)}, bf16[40,32,256]{2,1,0:T(8,128)(2,1)S(1)}, u32[]{:S(2)}, u32[]{:S(2)}) collective-permute-start(bf16[40,32,256]{2,1,0:T(8,128)(2,1)S(1)} %join.14.refs_2_.refs_0_), channel_id=1, source_target_pairs={{0,4},{1,13},{2,6},{3,15},{4,0},{5,9},{6,2},{7,11},{8,12},{9,5},{1... | collective-permute-start | bytes 1966088 | tf_op jit(solution)/shard_map/ppermute | solution.py:301
  63.4 3.3 %collective-permute-done.10.refs_1_ = bf16[20,32,256]{2,1,0:T(8,128)(2,1)S(1)} collective-permute-done((bf16[20,32,256]{2,1,0:T(8,128)(2,1)S(1)}, bf16[20,32,256]{2,1,0:T(8,128)(2,1)S(1)}, u32[]{:S(2)}, u32[]{:S(2)}) %collective-permute-start.10) | collective-permute-done | bytes 327712 | tf_op jit(solution)/shard_map/ppermute | solution.py:301
  66.8 3.7 %collective-permute-start.12 = (bf16[40,32,256]{2,1,0:T(8,128)(2,1)S(1)}, bf16[40,32,256]{2,1,0:T(8,128)(2,1)S(1)}, u32[]{:S(2)}, u32[]{:S(2)}) collective-permute-start(bf16[40,32,256]{2,1,0:T(8,128)(2,1)S(1)} %join.15.refs_2_.refs_0_), channel_id=1, source_target_pairs={{0,4},{1,13},{2,6},{3,15},{4,0},{5,9},{6,2},{7,11},{8,12},{9,5},{1... | collective-permute-start | bytes 1966088 | tf_op jit(solution)/shard_map/ppermute | solution.py:301
  72.2 3.4 %field.4 = (bf16[80,2048]{1,0:T(8,128)(2,1)S(1)}, bf16[80,1024]{1,0:T(8,128)(2,1)S(1)}) custom-call(s32[80]{0:T(128)S(1)} %copy-done.5, s32[8]{0:T(128)S(1)} %copy-done.21, bf16[80,32,256]{2,1,0:T(8,128)(2,1)S(1)} %join.16.refs_2_.refs_5_.refs_3_, bf16[80,64,256]{2,1,0:T(8,128)(2,1)S(1)} %get-tuple-element.90.refs_3_.refs_5_.refs_2_, ...), custom_call_target="tpu_custom_call" | custom-call | flops 20000000000 | bytes 1000 | tf_op jit(solution)/shard_map/field/pallas_call | solution.py:43
  75.7 3.4 %field.5 = (bf16[80,2048]{1,0:T(8,128)(2,1)S(1)}, bf16[80,1024]{1,0:T(8,128)(2,1)S(1)}) custom-call(s32[80]{0:T(128)S(1)} %copy-done.3, s32[8]{0:T(128)S(1)} %copy-done.21, bf16[80,32,256]{2,1,0:T(8,128)(2,1)S(1)} %collective-permute-done.14.refs_2_.refs_3_, bf16[80,64,256]{2,1,0:T(8,128)(2,1)S(1)} %get-tuple-element.89.refs_3_.refs_5_.refs_2_, ...), custom_call_target="tpu_custom_call" | custom-call | flops 20000000000 | bytes 1000 | tf_op jit(solution)/shard_map/field/pallas_call | solution.py:43
  82.9 3.4 %field.6 = (bf16[80,2048]{1,0:T(8,128)(2,1)S(1)}, bf16[80,1024]{1,0:T(8,128)(2,1)S(1)}) custom-call(s32[80]{0:T(128)S(1)} %copy-done.5, s32[8]{0:T(128)S(1)} %copy-done.21, bf16[80,32,256]{2,1,0:T(8,128)(2,1)S(1)} %join.17.refs_2_.refs_3_, bf16[80,64,256]{2,1,0:T(8,128)(2,1)S(1)} %get-tuple-element.93.refs_3_.refs_5_.refs_2_, ...), custom_call_target="tpu_custom_call" | custom-call | flops 20000000000 | bytes 1000 | tf_op jit(solution)/shard_map/field/pallas_call | solution.py:43
  86.3 3.4 %field.7 = (bf16[80,2048]{1,0:T(8,128)(2,1)S(1)}, bf16[80,1024]{1,0:T(8,128)(2,1)S(1)}) custom-call(s32[80]{0:T(128)S(1)} %copy-done.3, s32[8]{0:T(128)S(1)} %copy-done.21, bf16[80,32,256]{2,1,0:T(8,128)(2,1)S(1)} %collective-permute-done.16.refs_2_.refs_3_, bf16[80,64,256]{2,1,0:T(8,128)(2,1)S(1)} %get-tuple-element.95.refs_3_.refs_5_.refs_2_, ...), custom_call_target="tpu_custom_call" | custom-call | flops 20000000000 | bytes 1000 | tf_op jit(solution)/shard_map/field/pallas_call | solution.py:43
  105.6 3.9 %grad_compress.4 = (bf16[80,1024]{1,0:T(8,128)(2,1)S(1)}, bf16[80,2048]{1,0:T(8,128)(2,1)S(1)}, bf16[80,32,256]{2,1,0:T(8,128)(2,1)S(1)}) custom-call(s32[80]{0:T(128)S(1)} %copy-done.3, s32[1]{0:T(128)} %bitcast.4.refs_1_.refs_10_, bf16[80,1024]{1,0:T(8,128)(2,1)S(1)} %collective-permute-done.24.refs_2_, bf16[320,1024]{1,0:T(8,128)(2,1)S(1)} %copy-done.16, ...), custom_call_target="tpu_custom_call" | custom-call | flops 20000000000 | bytes 1000 | tf_op jit(solution)/shard_map/grad_compress/pallas_call | solution.py:43
  109.7 3.9 %grad_compress.5 = (bf16[80,1024]{1,0:T(8,128)(2,1)S(1)}, bf16[80,2048]{1,0:T(8,128)(2,1)S(1)}, bf16[80,32,256]{2,1,0:T(8,128)(2,1)S(1)}) custom-call(s32[80]{0:T(128)S(1)} %copy-done.6, s32[1]{0:T(128)} %bitcast.3.refs_9_.refs_1_, bf16[80,1024]{1,0:T(8,128)(2,1)S(1)} %add.187.refs_2_, bf16[320,1024]{1,0:T(8,128)(2,1)S(1)} %copy-done.16, ...), custom_call_target="tpu_custom_call" | custom-call | flops 20000000000 | bytes 1000 | tf_op jit(solution)/shard_map/grad_compress/pallas_call | solution.py:43
  114.6 5.3 %collective-permute-start.29 = (bf16[40,32,256]{2,1,0:T(8,128)(2,1)S(1)}, bf16[40,32,256]{2,1,0:T(8,128)(2,1)S(1)}, u32[]{:S(2)}, u32[]{:S(2)}) collective-permute-start(bf16[40,32,256]{2,1,0:T(8,128)(2,1)S(1)} %get-tuple-element.99.refs_7_), channel_id=1, source_target_pairs={{0,4},{1,13},{2,6},{3,15},{4,0},{5,9},{6,2},{7,11},{8,12},{9,5},{1... | collective-permute-start | bytes 1966088 | tf_op jit(solution)/shard_map/ppermute | solution.py:301
  119.9 3.9 %grad_compress.6 = (bf16[80,1024]{1,0:T(8,128)(2,1)S(1)}, bf16[80,2048]{1,0:T(8,128)(2,1)S(1)}, bf16[80,32,256]{2,1,0:T(8,128)(2,1)S(1)}) custom-call(s32[80]{0:T(128)S(1)} %copy-done.3, s32[1]{0:T(128)} %bitcast.refs_14_.refs_1_, bf16[80,1024]{1,0:T(8,128)(2,1)S(1)} %collective-permute-done.25.refs_2_, bf16[320,1024]{1,0:T(8,128)(2,1)S(1)} %copy-done.16, ...), custom_call_target="tpu_custom_call" | custom-call | flops 20000000000 | bytes 1000 | tf_op jit(solution)/shard_map/grad_compress/pallas_call | solution.py:43
  124.0 3.9 %grad_compress.7 = (bf16[80,1024]{1,0:T(8,128)(2,1)S(1)}, bf16[80,2048]{1,0:T(8,128)(2,1)S(1)}, bf16[80,32,256]{2,1,0:T(8,128)(2,1)S(1)}) custom-call(s32[80]{0:T(128)S(1)} %copy-done.6, s32[1]{0:T(128)} %bitcast.1.refs_13_.refs_1_, bf16[80,1024]{1,0:T(8,128)(2,1)S(1)} %add.189.refs_2_, bf16[320,1024]{1,0:T(8,128)(2,1)S(1)} %copy-done.16, ...), custom_call_target="tpu_custom_call" | custom-call | flops 20000000000 | bytes 1000 | tf_op jit(solution)/shard_map/grad_compress/pallas_call | solution.py:43
  135.3 7.1 %collective-permute-done.28.refs_1_ = bf16[40,32,256]{2,1,0:T(8,128)(2,1)S(1)} collective-permute-done((bf16[40,32,256]{2,1,0:T(8,128)(2,1)S(1)}, bf16[40,32,256]{2,1,0:T(8,128)(2,1)S(1)}, u32[]{:S(2)}, u32[]{:S(2)}) %collective-permute-start.28) | collective-permute-done | bytes 655392 | tf_op jit(solution)/shard_map/ppermute | solution.py:301
  144.4 5.3 %collective-permute-done.30.refs_1_ = bf16[20,32,256]{2,1,0:T(8,128)(2,1)S(1)} collective-permute-done((bf16[20,32,256]{2,1,0:T(8,128)(2,1)S(1)}, bf16[20,32,256]{2,1,0:T(8,128)(2,1)S(1)}, u32[]{:S(2)}, u32[]{:S(2)}) %collective-permute-start.30) | collective-permute-done | bytes 327712 | tf_op jit(solution)/shard_map/ppermute | solution.py:301
  153.6 3.5 %collective-permute-done.32.refs_1_ = bf16[10,32,256]{2,1,0:T(8,128)(2,1)S(1)} collective-permute-done((bf16[10,32,256]{2,1,0:T(8,128)(2,1)S(1)}, bf16[10,32,256]{2,1,0:T(8,128)(2,1)S(1)}, u32[]{:S(2)}, u32[]{:S(2)}) %collective-permute-start.32) | collective-permute-done | bytes 163872 | tf_op jit(solution)/shard_map/ppermute | solution.py:301
  162.1 3.2 %collective-permute-start.42 = (bf16[512,1024]{1,0:T(8,128)(2,1)S(1)}, bf16[512,1024]{1,0:T(8,128)(2,1)S(1)}, u32[]{:S(2)}, u32[]{:S(2)}) collective-permute-start(bf16[512,1024]{1,0:T(8,128)(2,1)S(1)} %get-tuple-element.125.refs_2_), channel_id=1, source_target_pairs={{0,96},{1,33},{2,98},{3,35},{4,100},{5,37},{6,102},{7,39},{8,104},... | collective-permute-start | bytes 3145736 | tf_op jit(solution)/shard_map/ppermute | solution.py:309
  167.6 4.9 %collective-permute-start.40 = (bf16[40,32,256]{2,1,0:T(8,128)(2,1)S(1)}, bf16[40,32,256]{2,1,0:T(8,128)(2,1)S(1)}, u32[]{:S(2)}, u32[]{:S(2)}) collective-permute-start(bf16[40,32,256]{2,1,0:T(8,128)(2,1)S(1)} %join.20.refs_2_.refs_0_), channel_id=1, source_target_pairs={{0,4},{1,13},{2,6},{3,15},{4,0},{5,9},{6,2},{7,11},{8,12},{9,5},{1... | collective-permute-start | bytes 1966088 | tf_op jit(solution)/shard_map/ppermute | solution.py:301
  172.5 3.6 %collective-permute-done.37.refs_1_ = bf16[20,32,256]{2,1,0:T(8,128)(2,1)S(1)} collective-permute-done((bf16[20,32,256]{2,1,0:T(8,128)(2,1)S(1)}, bf16[20,32,256]{2,1,0:T(8,128)(2,1)S(1)}, u32[]{:S(2)}, u32[]{:S(2)}) %collective-permute-start.37) | collective-permute-done | bytes 327712 | tf_op jit(solution)/shard_map/ppermute | solution.py:301
  176.1 4.3 %collective-permute-start.39 = (bf16[40,32,256]{2,1,0:T(8,128)(2,1)S(1)}, bf16[40,32,256]{2,1,0:T(8,128)(2,1)S(1)}, u32[]{:S(2)}, u32[]{:S(2)}) collective-permute-start(bf16[40,32,256]{2,1,0:T(8,128)(2,1)S(1)} %join.21.refs_2_.refs_0_), channel_id=1, source_target_pairs={{0,4},{1,13},{2,6},{3,15},{4,0},{5,9},{6,2},{7,11},{8,12},{9,5},{1... | collective-permute-start | bytes 1966088 | tf_op jit(solution)/shard_map/ppermute | solution.py:301
  189.2 3.2 %grad_tokens.4 = (bf16[320,64,256]{2,1,0:T(8,128)(2,1)}, f32[8,128]{1,0:T(8,128)S(1)}) custom-call(s32[80]{0:T(128)S(1)} %copy-done.6, s32[1]{0:T(128)} %bitcast.3.refs_9_.refs_1_, bf16[80,2048]{1,0:T(8,128)(2,1)S(1)} %get-tuple-element.130.refs_2_, bf16[80,32,256]{2,1,0:T(8,128)(2,1)S(1)} %copy-done.13, bf16[80,32,256]{2,1,0:T(8,128)(2,1)S(1)} %join.22.refs_1_.refs_4_, ...), custom_call_target="tpu_custom_call" | custom-call | flops 20000000000 | bytes 1000 | tf_op jit(solution)/shard_map/grad_tokens/pallas_call | solution.py:43
  196.9 3.3 %grad_tokens.5 = (bf16[320,64,256]{2,1,0:T(8,128)(2,1)}, f32[8,128]{1,0:T(8,128)S(1)}) custom-call(s32[80]{0:T(128)S(1)} %copy-done.6, s32[1]{0:T(128)} %bitcast.1.refs_13_.refs_1_, bf16[80,2048]{1,0:T(8,128)(2,1)S(1)} %get-tuple-element.129.refs_2_, bf16[80,32,256]{2,1,0:T(8,128)(2,1)S(1)} %copy-done.15, ...), custom_call_target="tpu_custom_call", output_to_operand_aliasing={{0}: (6, {})} | custom-call | flops 20000000000 | bytes 1000 | tf_op jit(solution)/shard_map/grad_tokens/pallas_call | solution.py:43
  204.9 3.2 %grad_tokens.6 = (bf16[320,64,256]{2,1,0:T(8,128)(2,1)}, f32[8,128]{1,0:T(8,128)S(1)}) custom-call(s32[80]{0:T(128)S(1)} %copy-done.3, s32[1]{0:T(128)} %bitcast.4.refs_1_.refs_10_, bf16[80,2048]{1,0:T(8,128)(2,1)S(1)} %get-tuple-element.128.refs_2_, bf16[80,32,256]{2,1,0:T(8,128)(2,1)S(1)} %copy-done.9, ...), custom_call_target="tpu_custom_call", output_to_operand_aliasing={{0}: (6, {})} | custom-call | flops 20000000000 | bytes 1000 | tf_op jit(solution)/shard_map/grad_tokens/pallas_call | solution.py:43
  209.5 3.2 %grad_tokens.7 = (bf16[320,64,256]{2,1,0:T(8,128)(2,1)}, f32[8,128]{1,0:T(8,128)S(1)}) custom-call(s32[80]{0:T(128)S(1)} %copy-done.3, s32[1]{0:T(128)} %bitcast.refs_14_.refs_1_, bf16[80,2048]{1,0:T(8,128)(2,1)S(1)} %get-tuple-element.100.refs_2_, bf16[80,32,256]{2,1,0:T(8,128)(2,1)S(1)} %copy-done.11, ...), custom_call_target="tpu_custom_call", output_to_operand_aliasing={{0}: (6, {})} | custom-call | flops 20000000000 | bytes 1000 | tf_op jit(solution)/shard_map/grad_tokens/pallas_call | solution.py:43
  (188 shorter events, 83.9 us)
Async XLA Ops:
  9.4 10.7 %collective-permute-start.3 = (bf16[40,32,256]{2,1,0:T(8,128)(2,1)S(1)}, bf16[40,32,256]{2,1,0:T(8,128)(2,1)S(1)}, u32[]{:S(2)}, u32[]{:S(2)}) collective-permute-start(bf16[40,32,256]{2,1,0:T(8,128)(2,1)S(1)} %get-tuple-element.75.refs_4_), channel_id=1, source_target_pairs={{0,4},{1,13},{2,6},{3,15},{4,0},{5,9},{6,2},{7,11},{8,12},{9,5},{1... | collective-permute-start | bytes 1966088 | tf_op jit(solution)/shard_map/ppermute | solution.py:301
  17.0 14.2 %collective-permute-start.2 = (bf16[40,32,256]{2,1,0:T(8,128)(2,1)S(1)}, bf16[40,32,256]{2,1,0:T(8,128)(2,1)S(1)}, u32[]{:S(2)}, u32[]{:S(2)}) collective-permute-start(bf16[40,32,256]{2,1,0:T(8,128)(2,1)S(1)} %get-tuple-element.79.refs_2_), channel_id=1, source_target_pairs={{0,4},{1,13},{2,6},{3,15},{4,0},{5,9},{6,2},{7,11},{8,12},{9,5},{1... | collective-permute-start | bytes 1966088 | tf_op jit(solution)/shard_map/ppermute | solution.py:301
  20.2 12.0 %collective-permute-start.5 = (bf16[20,32,256]{2,1,0:T(8,128)(2,1)S(1)}, bf16[20,32,256]{2,1,0:T(8,128)(2,1)S(1)}, u32[]{:S(2)}, u32[]{:S(2)}) collective-permute-start(bf16[20,32,256]{2,1,0:T(8,128)(2,1)S(1)} %get-tuple-element.81.refs_2_), channel_id=1, source_target_pairs={{0,12},{1,5},{2,14},{3,7},{4,8},{5,1},{6,10},{7,3},{8,4},{9,13},{1... | collective-permute-start | bytes 983048 | tf_op jit(solution)/shard_map/ppermute | solution.py:301
  31.4 7.2 %collective-permute-start.4 = (bf16[20,32,256]{2,1,0:T(8,128)(2,1)S(1)}, bf16[20,32,256]{2,1,0:T(8,128)(2,1)S(1)}, u32[]{:S(2)}, u32[]{:S(2)}) collective-permute-start(bf16[20,32,256]{2,1,0:T(8,128)(2,1)S(1)} %get-tuple-element.83.refs_2_), channel_id=1, source_target_pairs={{0,12},{1,5},{2,14},{3,7},{4,8},{5,1},{6,10},{7,3},{8,4},{9,13},{1... | collective-permute-start | bytes 983048 | tf_op jit(solution)/shard_map/ppermute | solution.py:301
  32.3 10.3 %collective-permute-start.7 = (bf16[10,32,256]{2,1,0:T(8,128)(2,1)S(1)}, bf16[10,32,256]{2,1,0:T(8,128)(2,1)S(1)}, u32[]{:S(2)}, u32[]{:S(2)}) collective-permute-start(bf16[10,32,256]{2,1,0:T(8,128)(2,1)S(1)} %get-tuple-element.85.refs_2_), channel_id=1, source_target_pairs={{0,2},{1,3},{2,0},{3,1},{4,6},{5,7},{6,4},{7,5},{8,10},{9,11},{10,... | collective-permute-start | bytes 491528 | tf_op jit(solution)/shard_map/ppermute | solution.py:301
  38.6 8.4 %collective-permute-start.6 = (bf16[10,32,256]{2,1,0:T(8,128)(2,1)S(1)}, bf16[10,32,256]{2,1,0:T(8,128)(2,1)S(1)}, u32[]{:S(2)}, u32[]{:S(2)}) collective-permute-start(bf16[10,32,256]{2,1,0:T(8,128)(2,1)S(1)} %get-tuple-element.87.refs_2_), channel_id=1, source_target_pairs={{0,2},{1,3},{2,0},{3,1},{4,6},{5,7},{6,4},{7,5},{8,10},{9,11},{10,... | collective-permute-start | bytes 491528 | tf_op jit(solution)/shard_map/ppermute | solution.py:301
  42.6 8.5 %collective-permute-start.9 = (bf16[10,32,256]{2,1,0:T(8,128)(2,1)S(1)}, bf16[10,32,256]{2,1,0:T(8,128)(2,1)S(1)}, u32[]{:S(2)}, u32[]{:S(2)}) collective-permute-start(bf16[10,32,256]{2,1,0:T(8,128)(2,1)S(1)} %add.180.refs_2_.refs_0_), channel_id=1, source_target_pairs={{0,2},{1,3},{2,0},{3,1},{4,6},{5,7},{6,4},{7,5},{8,10},{9,11},{10,... | collective-permute-start | bytes 491528 | tf_op jit(solution)/shard_map/ppermute | solution.py:301
  47.0 6.9 %collective-permute-start.8 = (bf16[10,32,256]{2,1,0:T(8,128)(2,1)S(1)}, bf16[10,32,256]{2,1,0:T(8,128)(2,1)S(1)}, u32[]{:S(2)}, u32[]{:S(2)}) collective-permute-start(bf16[10,32,256]{2,1,0:T(8,128)(2,1)S(1)} %add.181.refs_2_.refs_0_), channel_id=1, source_target_pairs={{0,2},{1,3},{2,0},{3,1},{4,6},{5,7},{6,4},{7,5},{8,10},{9,11},{10,... | collective-permute-start | bytes 491528 | tf_op jit(solution)/shard_map/ppermute | solution.py:301
  51.1 8.6 %collective-permute-start.11 = (bf16[20,32,256]{2,1,0:T(8,128)(2,1)S(1)}, bf16[20,32,256]{2,1,0:T(8,128)(2,1)S(1)}, u32[]{:S(2)}, u32[]{:S(2)}) collective-permute-start(bf16[20,32,256]{2,1,0:T(8,128)(2,1)S(1)} %join.12.refs_2_.refs_0_), channel_id=1, source_target_pairs={{0,12},{1,5},{2,14},{3,7},{4,8},{5,1},{6,10},{7,3},{8,4},{9,13},{1... | collective-permute-start | bytes 983048 | tf_op jit(solution)/shard_map/ppermute | solution.py:301
  54.0 12.8 %collective-permute-start.10 = (bf16[20,32,256]{2,1,0:T(8,128)(2,1)S(1)}, bf16[20,32,256]{2,1,0:T(8,128)(2,1)S(1)}, u32[]{:S(2)}, u32[]{:S(2)}) collective-permute-start(bf16[20,32,256]{2,1,0:T(8,128)(2,1)S(1)} %join.13.refs_2_.refs_0_), channel_id=1, source_target_pairs={{0,12},{1,5},{2,14},{3,7},{4,8},{5,1},{6,10},{7,3},{8,4},{9,13},{1... | collective-permute-start | bytes 983048 | tf_op jit(solution)/shard_map/ppermute | solution.py:301
  59.8 12.2 %collective-permute-start.13 = (bf16[40,32,256]{2,1,0:T(8,128)(2,1)S(1)}, bf16[40,32,256]{2,1,0:T(8,128)(2,1)S(1)}, u32[]{:S(2)}, u32[]{:S(2)}) collective-permute-start(bf16[40,32,256]{2,1,0:T(8,128)(2,1)S(1)} %join.14.refs_2_.refs_0_), channel_id=1, source_target_pairs={{0,4},{1,13},{2,6},{3,15},{4,0},{5,9},{6,2},{7,11},{8,12},{9,5},{1... | collective-permute-start | bytes 1966088 | tf_op jit(solution)/shard_map/ppermute | solution.py:301
  66.8 12.8 %collective-permute-start.12 = (bf16[40,32,256]{2,1,0:T(8,128)(2,1)S(1)}, bf16[40,32,256]{2,1,0:T(8,128)(2,1)S(1)}, u32[]{:S(2)}, u32[]{:S(2)}) collective-permute-start(bf16[40,32,256]{2,1,0:T(8,128)(2,1)S(1)} %join.15.refs_2_.refs_0_), channel_id=1, source_target_pairs={{0,4},{1,13},{2,6},{3,15},{4,0},{5,9},{6,2},{7,11},{8,12},{9,5},{1... | collective-permute-start | bytes 1966088 | tf_op jit(solution)/shard_map/ppermute | solution.py:301
  79.8 6.5 %collective-permute-start.16 = (bf16[80,32,256]{2,1,0:T(8,128)(2,1)S(1)}, bf16[80,32,256]{2,1,0:T(8,128)(2,1)S(1)}, u32[]{:S(2)}, u32[]{:S(2)}) collective-permute-start(bf16[80,32,256]{2,1,0:T(8,128)(2,1)S(1)} %join.17.refs_2_.refs_3_), channel_id=1, source_target_pairs={{0,1},{1,0},{2,3},{3,2},{4,5},{5,4},{6,7},{7,6},{8,9},{9,8},{10,11... | collective-permute-start | bytes 3932168 | tf_op jit(solution)/shard_map/ppermute | solution.py:301
  80.8 9.1 %collective-permute-start.18 = (bf16[80,1024]{1,0:T(8,128)(2,1)S(1)}, bf16[80,1024]{1,0:T(8,128)(2,1)S(1)}, u32[]{:S(2)}, u32[]{:S(2)}) collective-permute-start(bf16[80,1024]{1,0:T(8,128)(2,1)S(1)} %add.182.refs_5_.refs_0_), channel_id=1, source_target_pairs={{0,4},{1,13},{2,6},{3,15},{4,0},{5,9},{6,2},{7,11},{8,12},{9,5},{1... | collective-permute-start | bytes 491528 | tf_op jit(solution)/shard_map/ppermute | solution.py:301
  95.9 7.0 %collective-permute-start.22 = (bf16[80,1024]{1,0:T(8,128)(2,1)S(1)}, bf16[80,1024]{1,0:T(8,128)(2,1)S(1)}, u32[]{:S(2)}, u32[]{:S(2)}) collective-permute-start(bf16[80,1024]{1,0:T(8,128)(2,1)S(1)} %add.185.refs_2_.refs_0_), channel_id=1, source_target_pairs={{0,2},{1,3},{2,0},{3,1},{4,6},{5,7},{6,4},{7,5},{8,10},{9,11},{10,... | collective-permute-start | bytes 491528 | tf_op jit(solution)/shard_map/ppermute | solution.py:301
  103.5 10.1 %collective-permute-start.23 = (bf16[80,1024]{1,0:T(8,128)(2,1)S(1)}, bf16[80,1024]{1,0:T(8,128)(2,1)S(1)}, u32[]{:S(2)}, u32[]{:S(2)}) collective-permute-start(bf16[80,1024]{1,0:T(8,128)(2,1)S(1)} %add.188.refs_7_.refs_0_), channel_id=1, source_target_pairs={{0,2},{1,3},{2,0},{3,1},{4,6},{5,7},{6,4},{7,5},{8,10},{9,11},{10,... | collective-permute-start | bytes 491528 | tf_op jit(solution)/shard_map/ppermute | solution.py:301
  113.7 6.2 %collective-permute-start.25 = (bf16[80,1024]{1,0:T(8,128)(2,1)S(1)}, bf16[80,1024]{1,0:T(8,128)(2,1)S(1)}, u32[]{:S(2)}, u32[]{:S(2)}) collective-permute-start(bf16[80,1024]{1,0:T(8,128)(2,1)S(1)} %add.189.refs_2_), channel_id=1, source_target_pairs={{0,1},{1,0},{2,3},{3,2},{4,5},{5,4},{6,7},{7,6},{8,9},{9,8},{10,11... | collective-permute-start | bytes 491528 | tf_op jit(solution)/shard_map/ppermute | solution.py:301
  114.6 17.0 %collective-permute-start.29 = (bf16[40,32,256]{2,1,0:T(8,128)(2,1)S(1)}, bf16[40,32,256]{2,1,0:T(8,128)(2,1)S(1)}, u32[]{:S(2)}, u32[]{:S(2)}) collective-permute-start(bf16[40,32,256]{2,1,0:T(8,128)(2,1)S(1)} %get-tuple-element.99.refs_7_), channel_id=1, source_target_pairs={{0,4},{1,13},{2,6},{3,15},{4,0},{5,9},{6,2},{7,11},{8,12},{9,5},{1... | collective-permute-start | bytes 1966088 | tf_op jit(solution)/shard_map/ppermute | solution.py:301
  128.2 14.2 %collective-permute-start.28 = (bf16[40,32,256]{2,1,0:T(8,128)(2,1)S(1)}, bf16[40,32,256]{2,1,0:T(8,128)(2,1)S(1)}, u32[]{:S(2)}, u32[]{:S(2)}) collective-permute-start(bf16[40,32,256]{2,1,0:T(8,128)(2,1)S(1)} %get-tuple-element.104.refs_8_), channel_id=1, source_target_pairs={{0,4},{1,13},{2,6},{3,15},{4,0},{5,9},{6,2},{7,11},{8,12},{9,5},{1... | collective-permute-start | bytes 1966088 | tf_op jit(solution)/shard_map/ppermute | solution.py:301
  132.3 10.4 %collective-permute-start.31 = (bf16[20,32,256]{2,1,0:T(8,128)(2,1)S(1)}, bf16[20,32,256]{2,1,0:T(8,128)(2,1)S(1)}, u32[]{:S(2)}, u32[]{:S(2)}) collective-permute-start(bf16[20,32,256]{2,1,0:T(8,128)(2,1)S(1)} %get-tuple-element.115.refs_2_), channel_id=1, source_target_pairs={{0,12},{1,5},{2,14},{3,7},{4,8},{5,1},{6,10},{7,3},{8,4},{9,13},{1... | collective-permute-start | bytes 983048 | tf_op jit(solution)/shard_map/ppermute | solution.py:301
  133.7 27.6 %collective-permute-start.35 = (bf16[1024,1024]{1,0:T(8,128)(2,1)S(1)}, bf16[1024,1024]{1,0:T(8,128)(2,1)S(1)}, u32[]{:S(2)}, u32[]{:S(2)}) collective-permute-start(bf16[1024,1024]{1,0:T(8,128)(2,1)S(1)} %get-tuple-element.124), channel_id=1, source_target_pairs={{0,32},{1,97},{2,34},{3,99},{4,36},{5,101},{6,38},{7,103},{8,40},{... | collective-permute-start | bytes 6291464 | tf_op jit(solution)/shard_map/ppermute | solution.py:309
  142.6 7.2 %collective-permute-start.30 = (bf16[20,32,256]{2,1,0:T(8,128)(2,1)S(1)}, bf16[20,32,256]{2,1,0:T(8,128)(2,1)S(1)}, u32[]{:S(2)}, u32[]{:S(2)}) collective-permute-start(bf16[20,32,256]{2,1,0:T(8,128)(2,1)S(1)} %get-tuple-element.117.refs_2_), channel_id=1, source_target_pairs={{0,12},{1,5},{2,14},{3,7},{4,8},{5,1},{6,10},{7,3},{8,4},{9,13},{1... | collective-permute-start | bytes 983048 | tf_op jit(solution)/shard_map/ppermute | solution.py:301
  142.8 8.6 %collective-permute-start.33 = (bf16[10,32,256]{2,1,0:T(8,128)(2,1)S(1)}, bf16[10,32,256]{2,1,0:T(8,128)(2,1)S(1)}, u32[]{:S(2)}, u32[]{:S(2)}) collective-permute-start(bf16[10,32,256]{2,1,0:T(8,128)(2,1)S(1)} %get-tuple-element.119.refs_2_), channel_id=1, source_target_pairs={{0,2},{1,3},{2,0},{3,1},{4,6},{5,7},{6,4},{7,5},{8,10},{9,11},{10,... | collective-permute-start | bytes 491528 | tf_op jit(solution)/shard_map/ppermute | solution.py:301
  149.8 7.2 %collective-permute-start.32 = (bf16[10,32,256]{2,1,0:T(8,128)(2,1)S(1)}, bf16[10,32,256]{2,1,0:T(8,128)(2,1)S(1)}, u32[]{:S(2)}, u32[]{:S(2)}) collective-permute-start(bf16[10,32,256]{2,1,0:T(8,128)(2,1)S(1)} %get-tuple-element.121.refs_2_), channel_id=1, source_target_pairs={{0,2},{1,3},{2,0},{3,1},{4,6},{5,7},{6,4},{7,5},{8,10},{9,11},{10,... | collective-permute-start | bytes 491528 | tf_op jit(solution)/shard_map/ppermute | solution.py:301
  151.4 8.5 %collective-permute-start.36 = (bf16[10,32,256]{2,1,0:T(8,128)(2,1)S(1)}, bf16[10,32,256]{2,1,0:T(8,128)(2,1)S(1)}, u32[]{:S(2)}, u32[]{:S(2)}) collective-permute-start(bf16[10,32,256]{2,1,0:T(8,128)(2,1)S(1)} %add.196.refs_2_.refs_0_), channel_id=1, source_target_pairs={{0,2},{1,3},{2,0},{3,1},{4,6},{5,7},{6,4},{7,5},{8,10},{9,11},{10,... | collective-permute-start | bytes 491528 | tf_op jit(solution)/shard_map/ppermute | solution.py:301
  157.1 8.2 %collective-permute-start.34 = (bf16[10,32,256]{2,1,0:T(8,128)(2,1)S(1)}, bf16[10,32,256]{2,1,0:T(8,128)(2,1)S(1)}, u32[]{:S(2)}, u32[]{:S(2)}) collective-permute-start(bf16[10,32,256]{2,1,0:T(8,128)(2,1)S(1)} %add.197.refs_2_.refs_0_), channel_id=1, source_target_pairs={{0,2},{1,3},{2,0},{3,1},{4,6},{5,7},{6,4},{7,5},{8,10},{9,11},{10,... | collective-permute-start | bytes 491528 | tf_op jit(solution)/shard_map/ppermute | solution.py:301
  160.0 7.6 %collective-permute-start.38 = (bf16[20,32,256]{2,1,0:T(8,128)(2,1)S(1)}, bf16[20,32,256]{2,1,0:T(8,128)(2,1)S(1)}, u32[]{:S(2)}, u32[]{:S(2)}) collective-permute-start(bf16[20,32,256]{2,1,0:T(8,128)(2,1)S(1)} %join.18.refs_2_.refs_0_), channel_id=1, source_target_pairs={{0,12},{1,5},{2,14},{3,7},{4,8},{5,1},{6,10},{7,3},{8,4},{9,13},{1... | collective-permute-start | bytes 983048 | tf_op jit(solution)/shard_map/ppermute | solution.py:301
  162.1 21.2 %collective-permute-start.42 = (bf16[512,1024]{1,0:T(8,128)(2,1)S(1)}, bf16[512,1024]{1,0:T(8,128)(2,1)S(1)}, u32[]{:S(2)}, u32[]{:S(2)}) collective-permute-start(bf16[512,1024]{1,0:T(8,128)(2,1)S(1)} %get-tuple-element.125.refs_2_), channel_id=1, source_target_pairs={{0,96},{1,33},{2,98},{3,35},{4,100},{5,37},{6,102},{7,39},{8,104},... | collective-permute-start | bytes 3145736 | tf_op jit(solution)/shard_map/ppermute | solution.py:309
  165.3 10.7 %collective-permute-start.37 = (bf16[20,32,256]{2,1,0:T(8,128)(2,1)S(1)}, bf16[20,32,256]{2,1,0:T(8,128)(2,1)S(1)}, u32[]{:S(2)}, u32[]{:S(2)}) collective-permute-start(bf16[20,32,256]{2,1,0:T(8,128)(2,1)S(1)} %join.19.refs_2_.refs_0_), channel_id=1, source_target_pairs={{0,12},{1,5},{2,14},{3,7},{4,8},{5,1},{6,10},{7,3},{8,4},{9,13},{1... | collective-permute-start | bytes 983048 | tf_op jit(solution)/shard_map/ppermute | solution.py:301
  167.6 13.4 %collective-permute-start.40 = (bf16[40,32,256]{2,1,0:T(8,128)(2,1)S(1)}, bf16[40,32,256]{2,1,0:T(8,128)(2,1)S(1)}, u32[]{:S(2)}, u32[]{:S(2)}) collective-permute-start(bf16[40,32,256]{2,1,0:T(8,128)(2,1)S(1)} %join.20.refs_2_.refs_0_), channel_id=1, source_target_pairs={{0,4},{1,13},{2,6},{3,15},{4,0},{5,9},{6,2},{7,11},{8,12},{9,5},{1... | collective-permute-start | bytes 1966088 | tf_op jit(solution)/shard_map/ppermute | solution.py:301
  176.1 12.8 %collective-permute-start.39 = (bf16[40,32,256]{2,1,0:T(8,128)(2,1)S(1)}, bf16[40,32,256]{2,1,0:T(8,128)(2,1)S(1)}, u32[]{:S(2)}, u32[]{:S(2)}) collective-permute-start(bf16[40,32,256]{2,1,0:T(8,128)(2,1)S(1)} %join.21.refs_2_.refs_0_), channel_id=1, source_target_pairs={{0,4},{1,13},{2,6},{3,15},{4,0},{5,9},{6,2},{7,11},{8,12},{9,5},{1... | collective-permute-start | bytes 1966088 | tf_op jit(solution)/shard_map/ppermute | solution.py:301
  183.8 16.4 %collective-permute-start.45 = (bf16[256,1024]{1,0:T(8,128)(2,1)S(1)}, bf16[256,1024]{1,0:T(8,128)(2,1)S(1)}, u32[]{:S(2)}, u32[]{:S(2)}) collective-permute-start(bf16[256,1024]{1,0:T(8,128)(2,1)S(1)} %get-tuple-element.127.refs_4_), channel_id=1, source_target_pairs={{0,16},{1,17},{2,18},{3,19},{4,20},{5,21},{6,22},{7,23},{8,24},{9,... | collective-permute-start | bytes 1572872 | tf_op jit(solution)/shard_map/ppermute | solution.py:309
  (43 other events, 237.1 us)

commit v4 on v3

--- a/solution.py
+++ b/solution.py
@@ -11,7 +11,7 @@
 EB = 16
 PITCH = T + 1
 NCH = 2
-ORDERS = (("ABZ", "BAZ"), ("ABZ", "BAZ"))
+ORDERS = (("AZB", "BZA"), ("AZB", "BZA"))
 DP_ORDERS = ("ABZ", "BAZ")
 ORDER = (
     0, 0, 0, 1, 1, 1, 0, 1, 0, 1, 0, 1, 0, 1, 0, 1, 0, 0, 0, 1,
@@ -59,15 +59,20 @@
     return jax.ShapeDtypeStruct(dims, dtype)
 
 
-def compress(chain, x, pt4, tbl, blk):
+def compress(chain, x, pt, tbl, blk):
     n = tbl.shape[0]
 
-    def body(tbl, blk, pt4, x, xv, out, sem):
+    def body(tbl, blk, pt, x, xv, out, sem, pt4):
         def copy(i):
             return pltpu.make_async_copy(x.at[pl.ds((blk[0] + i) * EB, EB)], xv.at[pl.ds(i * EB, EB)], sem.at[i])
 
         for i in range(n // EB):
             copy(i).start()
+
+        wide = jnp.concatenate([pt[...].astype(f32)] * 4, axis=1)
+        lane = lax.broadcasted_iota(jnp.int32, (K, 4 * T), 1) // T
+        for j in range(4):
+            pt4[K * j : K * j + K, :] = jnp.where(lane == j, wide, 0.0).astype(bf)
 
         @pl.loop(0, n // EB)
         def _(i):
@@ -79,7 +84,8 @@
                     out[tbl[i * EB + 4 * g + j]] = r[K * j : K * j + K]
 
     outs = [shape(n, T, D), shape(n, K, D)]
-    return call(chain, body, "compress", outs, [pltpu.SemaphoreType.DMA((n // EB,))], [tbl, blk], [pt4], [x])
+    scratch = [pltpu.SemaphoreType.DMA((n // EB,)), pltpu.VMEM((4 * K, 4 * T), bf)]
+    return call(chain, body, "compress", outs, scratch, [tbl, blk], [pt], [x])
 
 
 def field(chain, x, comp, w, tbl, perm):
@@ -198,12 +204,14 @@
     return call(chain, body, "grad_projection", [shape(*sums.shape, dtype=f32)], [], [tbl], [dcomp, x, sums])[0]
 
 
-def grad_tokens(chain, df, comp, dcomp, tail, gx, dims, tbl, blk):
+def grad_tokens(chain, df, comp, dcomp, pt, gx, dims, tbl, blk):
     n = tbl.shape[0]
     far = [] if gx is None else [gx]
 
-    def body(tbl, blk, df, comp, dcomp, tail, *rest):
-        out, mark, ov, sem, sc = rest[len(far) :]
+    def body(tbl, blk, df, comp, dcomp, pt, *rest):
+        out, mark, ov, sem, sc, tail = rest[len(far) :]
+        p = pt[...].astype(f32).T
+        tail[:, : 2 * K] = jnp.concatenate([p, p], axis=1)
         mark[...] = jnp.zeros_like(mark)
 
         def copy(i):
@@ -224,8 +232,9 @@
 
     outs = [pltpu.HBM(dims, bf), shape(8, 128, dtype=f32)]
     scratch = [pltpu.VMEM((n, T, D), bf), pltpu.SemaphoreType.DMA((n // EB,)), pltpu.VMEM((EB * PITCH, 128), f32)]
+    scratch += [pltpu.VMEM((T, 128), f32)]
     alias = {6: 0} if far else None
-    return call(chain, body, "grad_tokens", outs, scratch, [tbl, blk], [df, comp, dcomp, tail], far, alias)[0]
+    return call(chain, body, "grad_tokens", outs, scratch, [tbl, blk], [df, comp, dcomp, pt], far, alias)[0]
 
 
 def add_rows(chain, a, b, cut=False, dtype=bf):
@@ -246,12 +255,31 @@
     return outs if cut else outs[0]
 
 
+def add_out(chain, a, b):
+    n, m, step = a.shape[0], a.shape[1], 64
+
+    def body(a, b, out, mark, ov, sem):
+        mark[...] = jnp.zeros_like(mark)
+        copies = []
+        for i in range(n // step):
+            at = pl.ds(i * step, step)
+            ov[at] = a[at].astype(f32) + b[at].astype(f32)
+            copies.append(pltpu.make_async_copy(ov.at[at], out.at[at], sem.at[i]))
+            copies[-1].start()
+        for copy in copies:
+            copy.wait()
+
+    outs = [pltpu.HBM((n, m), f32), shape(8, 128, dtype=f32)]
+    scratch = [pltpu.VMEM((n, m), f32), pltpu.SemaphoreType.DMA((n // step,))]
+    return call(chain, body, "add", outs, scratch, [], [a, b])[0]
+
+
 def split_sums(chain, a, b):
     def body(a, b, gp, gb):
-        gp[...] = (a[:K, :T] + b[:K, :T]).T
+        gp[...] = a[:K, :T] + b[:K, :T]
         gb[...] = a[K:, :] + b[K:, :]
 
-    outs = [shape(T, K, dtype=f32), shape(H // 128, 128, dtype=f32)]
+    outs = [shape(K, T, dtype=f32), shape(H // 128, 128, dtype=f32)]
     return call(chain, body, "add", outs, [], [], [a, b])
 
 
@@ -324,10 +352,7 @@
         blocks.append((g ^ (g >> 1)) * 2 + at["Z"])
     perm = jnp.where(core == 0, blocks[0], blocks[1])
 
-    pt4 = sum(
-        jnp.pad(projection.T.astype(f32), ((K * j, 3 * K - K * j), (T * j, 3 * T - T * j))) for j in range(4)
-    ).astype(bf)
-    tail = jnp.pad(projection.astype(f32), ((0, 0), (K, 128 - 2 * K)))
+    pt = projection.T
     bias = mlp_bias.reshape(1, H)
 
     e = jnp.arange(half, dtype=jnp.int32)
@@ -339,7 +364,7 @@
         blocks.append(((first + core * (half // EB)).reshape(1), (first + (1 - core) * (half // EB)).reshape(1)))
 
     chain = Chain()
-    chain.last = [perm, tail, bias, *(a for c in range(NCH) for pair in (tables[c], blocks[c]) for a in pair)]
+    chain.last = [perm, bias, *(a for c in range(NCH) for pair in (tables[c], blocks[c]) for a in pair)]
     done = {}
 
     def total(swap, mine, got):
@@ -360,10 +385,10 @@
         def swap(x, step):
             return tok_swap(x, step, ORDERS[c])
 
-        x1, other = compress(chain, embeddings, pt4, tbl[1], blk[1])
+        x1, other = compress(chain, embeddings, pt, tbl[1], blk[1])
         got = swap(other, "C")
         yield
-        x0, mine = compress(chain, embeddings, pt4, tbl[0], blk[0])
+        x0, mine = compress(chain, embeddings, pt, tbl[0], blk[0])
         yield
         mine = yield from total(swap, mine, got)
         other = swap(mine, "C")
@@ -398,7 +423,7 @@
         yield
         for h, d in ((0, d0), (1, d1)):
             done["gx"] = grad_tokens(
-                chain, d, comp[h], dcomp[h], tail, done.get("gx"), embeddings.shape, tbl[h], blk[h]
+                chain, d, comp[h], dcomp[h], pt, done.get("gx"), embeddings.shape, tbl[h], blk[h]
             )
             yield
 
@@ -412,7 +437,7 @@
             keep, send = add_rows(chain, keep, got, True)
             got = dp_swap(send, step)
             yield
-        done["w"] = add_rows(chain, keep, got, dtype=f32)
+        done["w"] = add_out(chain, keep, got)
         yield
 
     def sums():
@@ -430,7 +455,7 @@
     for who in ORDER:
         next(steps[who])
     grad_p, grad_b = done["sums"]
-    return done["gx"], done["w"], grad_p, grad_b.reshape(H)
+    return done["gx"], done["w"], grad_p.T, grad_b.reshape(H)
 
 
 def solution(mesh):

time: 218 us -> 213 us (0.977)
  waiting for transfers between devices: 62.3 us -> 59.1 us
    ppermute x42, waiting for transfers between devices: 62.3 us -> 58.4 us  [tok_swap(): return lax.ppermute(x, 'tok', pairs)]
  transfers between devices with their start and end apart: 48 -> 48, of which waited for: 23 -> 25; matrix products, arithmetic and copies ran while one was open for 0% -> 0% of each run, Pallas kernels for 31% -> 32%
where the time goes in v4:
time: 213 us; the launch traced here: 209 us
  starting transfers between devices  75.5 us (35%)
  Pallas kernels  70.8 us (33%)
  waiting for transfers between devices  59.1 us (28%)
    pallas_call x63, Pallas kernels, call(): pl.pallas_call(run, out_shape=outs, in_specs=specs, out_specs=[place(out)...  70.8 us
    ppermute x42, starting transfers between devices, tok_swap(): return lax.ppermute(x, 'tok', pairs)  64.6 us
    ppermute x42, waiting for transfers between devices, tok_swap(): return lax.ppermute(x, 'tok', pairs)  58.4 us
    ppermute x6, starting transfers between devices, dp_swap(): return lax.ppermute(x, ('dp', 'tok'), pairs)  10.9 us
  transfers between devices with their start and end apart: 48, of which 25 were waited for; matrix products, arithmetic and copies ran while one was open for 0% of the time, Pallas kernels for 32%

profile of v4, /device:TPU:4, one launch (start us, length us, event | category | flops | bytes accessed | tf_op | source)
XLA Modules:
  0.0 209.1 jit_solution(4855536784926250319)
XLA Ops:
  19.3 4.0 %collective-permute-start.5 = (bf16[20,32,256]{2,1,0:T(8,128)(2,1)S(1)}, bf16[20,32,256]{2,1,0:T(8,128)(2,1)S(1)}, u32[]{:S(2)}, u32[]{:S(2)}) collective-permute-start(bf16[20,32,256]{2,1,0:T(8,128)(2,1)S(1)} %get-tuple-element.83.refs_2_), channel_id=1, source_target_pairs={{0,2},{1,3},{2,0},{3,1},{4,6},{5,7},{6,4},{7,5},{8,10},{9,11},{10,... | collective-permute-start | bytes 983048 | tf_op jit(solution)/shard_map/ppermute | solution.py:329
  23.2 3.5 %collective-permute-done.2.refs_1_ = bf16[40,32,256]{2,1,0:T(8,128)(2,1)S(1)} collective-permute-done((bf16[40,32,256]{2,1,0:T(8,128)(2,1)S(1)}, bf16[40,32,256]{2,1,0:T(8,128)(2,1)S(1)}, u32[]{:S(2)}, u32[]{:S(2)}) %collective-permute-start.2) | collective-permute-done | bytes 655392 | tf_op jit(solution)/shard_map/ppermute | solution.py:329
  26.9 4.0 %collective-permute-start.4 = (bf16[20,32,256]{2,1,0:T(8,128)(2,1)S(1)}, bf16[20,32,256]{2,1,0:T(8,128)(2,1)S(1)}, u32[]{:S(2)}, u32[]{:S(2)}) collective-permute-start(bf16[20,32,256]{2,1,0:T(8,128)(2,1)S(1)} %get-tuple-element.85.refs_2_), channel_id=1, source_target_pairs={{0,2},{1,3},{2,0},{3,1},{4,6},{5,7},{6,4},{7,5},{8,10},{9,11},{10,... | collective-permute-start | bytes 983048 | tf_op jit(solution)/shard_map/ppermute | solution.py:329
  31.8 6.5 %collective-permute-done.4.refs_1_ = bf16[20,32,256]{2,1,0:T(8,128)(2,1)S(1)} collective-permute-done((bf16[20,32,256]{2,1,0:T(8,128)(2,1)S(1)}, bf16[20,32,256]{2,1,0:T(8,128)(2,1)S(1)}, u32[]{:S(2)}, u32[]{:S(2)}) %collective-permute-start.4) | collective-permute-done | bytes 327712 | tf_op jit(solution)/shard_map/ppermute | solution.py:329
  40.6 3.2 %collective-permute-done.6.refs_1_ = bf16[10,32,256]{2,1,0:T(8,128)(2,1)S(1)} collective-permute-done((bf16[10,32,256]{2,1,0:T(8,128)(2,1)S(1)}, bf16[10,32,256]{2,1,0:T(8,128)(2,1)S(1)}, u32[]{:S(2)}, u32[]{:S(2)}) %collective-permute-start.6) | collective-permute-done | bytes 163872 | tf_op jit(solution)/shard_map/ppermute | solution.py:329
  45.5 3.3 %collective-permute-start.11 = (bf16[20,32,256]{2,1,0:T(8,128)(2,1)S(1)}, bf16[20,32,256]{2,1,0:T(8,128)(2,1)S(1)}, u32[]{:S(2)}, u32[]{:S(2)}) collective-permute-start(bf16[20,32,256]{2,1,0:T(8,128)(2,1)S(1)} %join.12.refs_2_.refs_0_), channel_id=1, source_target_pairs={{0,2},{1,3},{2,0},{3,1},{4,6},{5,7},{6,4},{7,5},{8,10},{9,11},{10,... | collective-permute-start | bytes 983048 | tf_op jit(solution)/shard_map/ppermute | solution.py:329
  49.2 3.3 %collective-permute-start.10 = (bf16[20,32,256]{2,1,0:T(8,128)(2,1)S(1)}, bf16[20,32,256]{2,1,0:T(8,128)(2,1)S(1)}, u32[]{:S(2)}, u32[]{:S(2)}) collective-permute-start(bf16[20,32,256]{2,1,0:T(8,128)(2,1)S(1)} %join.13.refs_2_.refs_0_), channel_id=1, source_target_pairs={{0,2},{1,3},{2,0},{3,1},{4,6},{5,7},{6,4},{7,5},{8,10},{9,11},{10,... | collective-permute-start | bytes 983048 | tf_op jit(solution)/shard_map/ppermute | solution.py:329
  52.5 5.2 %collective-permute-done.11.refs_1_ = bf16[20,32,256]{2,1,0:T(8,128)(2,1)S(1)} collective-permute-done((bf16[20,32,256]{2,1,0:T(8,128)(2,1)S(1)}, bf16[20,32,256]{2,1,0:T(8,128)(2,1)S(1)}, u32[]{:S(2)}, u32[]{:S(2)}) %collective-permute-start.11) | collective-permute-done | bytes 327712 | tf_op jit(solution)/shard_map/ppermute | solution.py:329
  57.8 3.5 %collective-permute-start.13 = (bf16[40,32,256]{2,1,0:T(8,128)(2,1)S(1)}, bf16[40,32,256]{2,1,0:T(8,128)(2,1)S(1)}, u32[]{:S(2)}, u32[]{:S(2)}) collective-permute-start(bf16[40,32,256]{2,1,0:T(8,128)(2,1)S(1)} %join.14.refs_2_.refs_0_), channel_id=1, source_target_pairs={{0,4},{1,13},{2,6},{3,15},{4,0},{5,9},{6,2},{7,11},{8,12},{9,5},{1... | collective-permute-start | bytes 1966088 | tf_op jit(solution)/shard_map/ppermute | solution.py:329
  64.9 5.0 %collective-permute-done.13.refs_1_ = bf16[40,32,256]{2,1,0:T(8,128)(2,1)S(1)} collective-permute-done((bf16[40,32,256]{2,1,0:T(8,128)(2,1)S(1)}, bf16[40,32,256]{2,1,0:T(8,128)(2,1)S(1)}, u32[]{:S(2)}, u32[]{:S(2)}) %collective-permute-start.13) | collective-permute-done | bytes 655392 | tf_op jit(solution)/shard_map/ppermute | solution.py:329
  70.1 3.4 %field.4 = (bf16[80,2048]{1,0:T(8,128)(2,1)S(1)}, bf16[80,1024]{1,0:T(8,128)(2,1)S(1)}) custom-call(s32[80]{0:T(128)S(1)} %copy-done.3, s32[8]{0:T(128)S(1)} %copy-done.21, bf16[80,32,256]{2,1,0:T(8,128)(2,1)S(1)} %join.16.refs_2_.refs_5_.refs_3_, bf16[80,64,256]{2,1,0:T(8,128)(2,1)S(1)} %get-tuple-element.92.refs_3_.refs_5_.refs_2_, ...), custom_call_target="tpu_custom_call" | custom-call | flops 20000000000 | bytes 1000 | tf_op jit(solution)/shard_map/field/pallas_call | solution.py:43
  73.6 3.4 %field.5 = (bf16[80,2048]{1,0:T(8,128)(2,1)S(1)}, bf16[80,1024]{1,0:T(8,128)(2,1)S(1)}) custom-call(s32[80]{0:T(128)S(1)} %copy-done.1, s32[8]{0:T(128)S(1)} %copy-done.21, bf16[80,32,256]{2,1,0:T(8,128)(2,1)S(1)} %collective-permute-done.14.refs_2_.refs_3_, bf16[80,64,256]{2,1,0:T(8,128)(2,1)S(1)} %get-tuple-element.91.refs_3_.refs_5_.refs_2_, ...), custom_call_target="tpu_custom_call" | custom-call | flops 20000000000 | bytes 1000 | tf_op jit(solution)/shard_map/field/pallas_call | solution.py:43
  80.8 3.4 %field.6 = (bf16[80,2048]{1,0:T(8,128)(2,1)S(1)}, bf16[80,1024]{1,0:T(8,128)(2,1)S(1)}) custom-call(s32[80]{0:T(128)S(1)} %copy-done.3, s32[8]{0:T(128)S(1)} %copy-done.21, bf16[80,32,256]{2,1,0:T(8,128)(2,1)S(1)} %join.17.refs_2_.refs_3_, bf16[80,64,256]{2,1,0:T(8,128)(2,1)S(1)} %get-tuple-element.95.refs_3_.refs_5_.refs_2_, ...), custom_call_target="tpu_custom_call" | custom-call | flops 20000000000 | bytes 1000 | tf_op jit(solution)/shard_map/field/pallas_call | solution.py:43
  84.2 3.4 %field.7 = (bf16[80,2048]{1,0:T(8,128)(2,1)S(1)}, bf16[80,1024]{1,0:T(8,128)(2,1)S(1)}) custom-call(s32[80]{0:T(128)S(1)} %copy-done.1, s32[8]{0:T(128)S(1)} %copy-done.21, bf16[80,32,256]{2,1,0:T(8,128)(2,1)S(1)} %collective-permute-done.16.refs_2_.refs_3_, bf16[80,64,256]{2,1,0:T(8,128)(2,1)S(1)} %get-tuple-element.97.refs_3_.refs_5_.refs_2_, ...), custom_call_target="tpu_custom_call" | custom-call | flops 20000000000 | bytes 1000 | tf_op jit(solution)/shard_map/field/pallas_call | solution.py:43
  87.8 3.1 %collective-permute-start.20 = (bf16[80,1024]{1,0:T(8,128)(2,1)S(1)}, bf16[80,1024]{1,0:T(8,128)(2,1)S(1)}, u32[]{:S(2)}, u32[]{:S(2)}) collective-permute-start(bf16[80,1024]{1,0:T(8,128)(2,1)S(1)} %add.158.refs_2_.refs_0_), channel_id=1, source_target_pairs={{0,2},{1,3},{2,0},{3,1},{4,6},{5,7},{6,4},{7,5},{8,10},{9,11},{10,... | collective-permute-start | bytes 491528 | tf_op jit(solution)/shard_map/ppermute | solution.py:329
  97.4 3.3 %collective-permute-start.21 = (bf16[80,1024]{1,0:T(8,128)(2,1)S(1)}, bf16[80,1024]{1,0:T(8,128)(2,1)S(1)}, u32[]{:S(2)}, u32[]{:S(2)}) collective-permute-start(bf16[80,1024]{1,0:T(8,128)(2,1)S(1)} %add.161.refs_2_.refs_0_), channel_id=1, source_target_pairs={{0,2},{1,3},{2,0},{3,1},{4,6},{5,7},{6,4},{7,5},{8,10},{9,11},{10,... | collective-permute-start | bytes 491528 | tf_op jit(solution)/shard_map/ppermute | solution.py:329
  105.3 3.9 %grad_compress.4 = (bf16[80,1024]{1,0:T(8,128)(2,1)S(1)}, bf16[80,2048]{1,0:T(8,128)(2,1)S(1)}, bf16[80,32,256]{2,1,0:T(8,128)(2,1)S(1)}) custom-call(s32[80]{0:T(128)S(1)} %copy-done.1, s32[1]{0:T(128)} %bitcast.4.refs_1_.refs_9_, bf16[80,1024]{1,0:T(8,128)(2,1)S(1)} %collective-permute-done.24.refs_2_, bf16[320,1024]{1,0:T(8,128)(2,1)S(1)} %copy-done.14, ...), custom_call_target="tpu_custom_call" | custom-call | flops 20000000000 | bytes 1000 | tf_op jit(solution)/shard_map/grad_compress/pallas_call | solution.py:43
  109.4 3.9 %grad_compress.5 = (bf16[80,1024]{1,0:T(8,128)(2,1)S(1)}, bf16[80,2048]{1,0:T(8,128)(2,1)S(1)}, bf16[80,32,256]{2,1,0:T(8,128)(2,1)S(1)}) custom-call(s32[80]{0:T(128)S(1)} %copy-done.4, s32[1]{0:T(128)} %bitcast.3.refs_8_.refs_1_, bf16[80,1024]{1,0:T(8,128)(2,1)S(1)} %add.162.refs_2_, bf16[320,1024]{1,0:T(8,128)(2,1)S(1)} %copy-done.14, ...), custom_call_target="tpu_custom_call" | custom-call | flops 20000000000 | bytes 1000 | tf_op jit(solution)/shard_map/grad_compress/pallas_call | solution.py:43
  116.9 3.9 %grad_compress.6 = (bf16[80,1024]{1,0:T(8,128)(2,1)S(1)}, bf16[80,2048]{1,0:T(8,128)(2,1)S(1)}, bf16[80,32,256]{2,1,0:T(8,128)(2,1)S(1)}) custom-call(s32[80]{0:T(128)S(1)} %copy-done.1, s32[1]{0:T(128)} %bitcast.refs_13_.refs_1_, bf16[80,1024]{1,0:T(8,128)(2,1)S(1)} %collective-permute-done.25.refs_2_, bf16[320,1024]{1,0:T(8,128)(2,1)S(1)} %copy-done.14, ...), custom_call_target="tpu_custom_call" | custom-call | flops 20000000000 | bytes 1000 | tf_op jit(solution)/shard_map/grad_compress/pallas_call | solution.py:43
  121.0 3.9 %grad_compress.7 = (bf16[80,1024]{1,0:T(8,128)(2,1)S(1)}, bf16[80,2048]{1,0:T(8,128)(2,1)S(1)}, bf16[80,32,256]{2,1,0:T(8,128)(2,1)S(1)}) custom-call(s32[80]{0:T(128)S(1)} %copy-done.4, s32[1]{0:T(128)} %bitcast.1.refs_12_.refs_1_, bf16[80,1024]{1,0:T(8,128)(2,1)S(1)} %add.164.refs_2_, bf16[320,1024]{1,0:T(8,128)(2,1)S(1)} %copy-done.14, ...), custom_call_target="tpu_custom_call" | custom-call | flops 20000000000 | bytes 1000 | tf_op jit(solution)/shard_map/grad_compress/pallas_call | solution.py:43
  129.5 3.1 %collective-permute-start.31 = (bf16[20,32,256]{2,1,0:T(8,128)(2,1)S(1)}, bf16[20,32,256]{2,1,0:T(8,128)(2,1)S(1)}, u32[]{:S(2)}, u32[]{:S(2)}) collective-permute-start(bf16[20,32,256]{2,1,0:T(8,128)(2,1)S(1)} %get-tuple-element.117.refs_2_), channel_id=1, source_target_pairs={{0,2},{1,3},{2,0},{3,1},{4,6},{5,7},{6,4},{7,5},{8,10},{9,11},{10,... | collective-permute-start | bytes 983048 | tf_op jit(solution)/shard_map/ppermute | solution.py:329
  136.1 3.3 %collective-permute-start.30 = (bf16[20,32,256]{2,1,0:T(8,128)(2,1)S(1)}, bf16[20,32,256]{2,1,0:T(8,128)(2,1)S(1)}, u32[]{:S(2)}, u32[]{:S(2)}) collective-permute-start(bf16[20,32,256]{2,1,0:T(8,128)(2,1)S(1)} %get-tuple-element.119.refs_2_), channel_id=1, source_target_pairs={{0,2},{1,3},{2,0},{3,1},{4,6},{5,7},{6,4},{7,5},{8,10},{9,11},{10,... | collective-permute-start | bytes 983048 | tf_op jit(solution)/shard_map/ppermute | solution.py:329
  142.7 4.9 %collective-permute-done.30.refs_1_ = bf16[20,32,256]{2,1,0:T(8,128)(2,1)S(1)} collective-permute-done((bf16[20,32,256]{2,1,0:T(8,128)(2,1)S(1)}, bf16[20,32,256]{2,1,0:T(8,128)(2,1)S(1)}, u32[]{:S(2)}, u32[]{:S(2)}) %collective-permute-start.30) | collective-permute-done | bytes 327712 | tf_op jit(solution)/shard_map/ppermute | solution.py:329
  149.9 3.2 %collective-permute-done.32.refs_1_ = bf16[10,32,256]{2,1,0:T(8,128)(2,1)S(1)} collective-permute-done((bf16[10,32,256]{2,1,0:T(8,128)(2,1)S(1)}, bf16[10,32,256]{2,1,0:T(8,128)(2,1)S(1)}, u32[]{:S(2)}, u32[]{:S(2)}) %collective-permute-start.32) | collective-permute-done | bytes 163872 | tf_op jit(solution)/shard_map/ppermute | solution.py:329
  154.8 3.1 %collective-permute-start.38 = (bf16[20,32,256]{2,1,0:T(8,128)(2,1)S(1)}, bf16[20,32,256]{2,1,0:T(8,128)(2,1)S(1)}, u32[]{:S(2)}, u32[]{:S(2)}) collective-permute-start(bf16[20,32,256]{2,1,0:T(8,128)(2,1)S(1)} %join.18.refs_2_.refs_0_), channel_id=1, source_target_pairs={{0,2},{1,3},{2,0},{3,1},{4,6},{5,7},{6,4},{7,5},{8,10},{9,11},{10,... | collective-permute-start | bytes 983048 | tf_op jit(solution)/shard_map/ppermute | solution.py:329
  159.5 3.2 %collective-permute-start.42 = (bf16[512,1024]{1,0:T(8,128)(2,1)S(1)}, bf16[512,1024]{1,0:T(8,128)(2,1)S(1)}, u32[]{:S(2)}, u32[]{:S(2)}) collective-permute-start(bf16[512,1024]{1,0:T(8,128)(2,1)S(1)} %get-tuple-element.127.refs_2_), channel_id=1, source_target_pairs={{0,96},{1,33},{2,98},{3,35},{4,100},{5,37},{6,102},{7,39},{8,104},... | collective-permute-start | bytes 3145736 | tf_op jit(solution)/shard_map/ppermute | solution.py:337
  166.2 3.1 %collective-permute-start.40 = (bf16[40,32,256]{2,1,0:T(8,128)(2,1)S(1)}, bf16[40,32,256]{2,1,0:T(8,128)(2,1)S(1)}, u32[]{:S(2)}, u32[]{:S(2)}) collective-permute-start(bf16[40,32,256]{2,1,0:T(8,128)(2,1)S(1)} %join.20.refs_2_.refs_0_), channel_id=1, source_target_pairs={{0,4},{1,13},{2,6},{3,15},{4,0},{5,9},{6,2},{7,11},{8,12},{9,5},{1... | collective-permute-start | bytes 1966088 | tf_op jit(solution)/shard_map/ppermute | solution.py:329
  173.8 4.0 %collective-permute-done.40.refs_1_ = bf16[40,32,256]{2,1,0:T(8,128)(2,1)S(1)} collective-permute-done((bf16[40,32,256]{2,1,0:T(8,128)(2,1)S(1)}, bf16[40,32,256]{2,1,0:T(8,128)(2,1)S(1)}, u32[]{:S(2)}, u32[]{:S(2)}) %collective-permute-start.40) | collective-permute-done | bytes 655392 | tf_op jit(solution)/shard_map/ppermute | solution.py:329
  185.1 3.4 %grad_tokens.4 = (bf16[320,64,256]{2,1,0:T(8,128)(2,1)}, f32[8,128]{1,0:T(8,128)S(1)}) custom-call(s32[80]{0:T(128)S(1)} %copy-done.4, s32[1]{0:T(128)} %bitcast.3.refs_8_.refs_1_, bf16[80,2048]{1,0:T(8,128)(2,1)S(1)} %get-tuple-element.132.refs_2_, bf16[80,32,256]{2,1,0:T(8,128)(2,1)S(1)} %copy-done.11, bf16[80,32,256]{2,1,0:T(8,128)(2,1)S(1)} %join.22.refs_1_.refs_4_, ...), custom_call_target="tpu_custom_call" | custom-call | flops 20000000000 | bytes 1000 | tf_op jit(solution)/shard_map/grad_tokens/pallas_call | solution.py:43
  193.8 3.4 %grad_tokens.5 = (bf16[320,64,256]{2,1,0:T(8,128)(2,1)}, f32[8,128]{1,0:T(8,128)S(1)}) custom-call(s32[80]{0:T(128)S(1)} %copy-done.4, s32[1]{0:T(128)} %bitcast.1.refs_12_.refs_1_, bf16[80,2048]{1,0:T(8,128)(2,1)S(1)} %get-tuple-element.131.refs_2_, bf16[80,32,256]{2,1,0:T(8,128)(2,1)S(1)} %copy-done.13, ...), custom_call_target="tpu_custom_call", output_to_operand_aliasing={{0}: (6, {})} | custom-call | flops 20000000000 | bytes 1000 | tf_op jit(solution)/shard_map/grad_tokens/pallas_call | solution.py:43
  200.3 3.4 %grad_tokens.6 = (bf16[320,64,256]{2,1,0:T(8,128)(2,1)}, f32[8,128]{1,0:T(8,128)S(1)}) custom-call(s32[80]{0:T(128)S(1)} %copy-done.1, s32[1]{0:T(128)} %bitcast.4.refs_1_.refs_9_, bf16[80,2048]{1,0:T(8,128)(2,1)S(1)} %get-tuple-element.130.refs_2_, bf16[80,32,256]{2,1,0:T(8,128)(2,1)S(1)} %copy-done.7, ...), custom_call_target="tpu_custom_call", output_to_operand_aliasing={{0}: (6, {})} | custom-call | flops 20000000000 | bytes 1000 | tf_op jit(solution)/shard_map/grad_tokens/pallas_call | solution.py:43
  205.1 3.4 %grad_tokens.7 = (bf16[320,64,256]{2,1,0:T(8,128)(2,1)}, f32[8,128]{1,0:T(8,128)S(1)}) custom-call(s32[80]{0:T(128)S(1)} %copy-done.1, s32[1]{0:T(128)} %bitcast.refs_13_.refs_1_, bf16[80,2048]{1,0:T(8,128)(2,1)S(1)} %get-tuple-element.102.refs_2_, bf16[80,32,256]{2,1,0:T(8,128)(2,1)S(1)} %copy-done.9, ...), custom_call_target="tpu_custom_call", output_to_operand_aliasing={{0}: (6, {})} | custom-call | flops 20000000000 | bytes 1000 | tf_op jit(solution)/shard_map/grad_tokens/pallas_call | solution.py:43
  (183 shorter events, 88.9 us)
Async XLA Ops:
  8.5 10.7 %collective-permute-start.3 = (bf16[40,32,256]{2,1,0:T(8,128)(2,1)S(1)}, bf16[40,32,256]{2,1,0:T(8,128)(2,1)S(1)}, u32[]{:S(2)}, u32[]{:S(2)}) collective-permute-start(bf16[40,32,256]{2,1,0:T(8,128)(2,1)S(1)} %get-tuple-element.77.refs_4_), channel_id=1, source_target_pairs={{0,4},{1,13},{2,6},{3,15},{4,0},{5,9},{6,2},{7,11},{8,12},{9,5},{1... | collective-permute-start | bytes 1966088 | tf_op jit(solution)/shard_map/ppermute | solution.py:329
  16.0 10.7 %collective-permute-start.2 = (bf16[40,32,256]{2,1,0:T(8,128)(2,1)S(1)}, bf16[40,32,256]{2,1,0:T(8,128)(2,1)S(1)}, u32[]{:S(2)}, u32[]{:S(2)}) collective-permute-start(bf16[40,32,256]{2,1,0:T(8,128)(2,1)S(1)} %get-tuple-element.81.refs_2_), channel_id=1, source_target_pairs={{0,4},{1,13},{2,6},{3,15},{4,0},{5,9},{6,2},{7,11},{8,12},{9,5},{1... | collective-permute-start | bytes 1966088 | tf_op jit(solution)/shard_map/ppermute | solution.py:329
  19.3 11.6 %collective-permute-start.5 = (bf16[20,32,256]{2,1,0:T(8,128)(2,1)S(1)}, bf16[20,32,256]{2,1,0:T(8,128)(2,1)S(1)}, u32[]{:S(2)}, u32[]{:S(2)}) collective-permute-start(bf16[20,32,256]{2,1,0:T(8,128)(2,1)S(1)} %get-tuple-element.83.refs_2_), channel_id=1, source_target_pairs={{0,2},{1,3},{2,0},{3,1},{4,6},{5,7},{6,4},{7,5},{8,10},{9,11},{10,... | collective-permute-start | bytes 983048 | tf_op jit(solution)/shard_map/ppermute | solution.py:329
  26.9 11.4 %collective-permute-start.4 = (bf16[20,32,256]{2,1,0:T(8,128)(2,1)S(1)}, bf16[20,32,256]{2,1,0:T(8,128)(2,1)S(1)}, u32[]{:S(2)}, u32[]{:S(2)}) collective-permute-start(bf16[20,32,256]{2,1,0:T(8,128)(2,1)S(1)} %get-tuple-element.85.refs_2_), channel_id=1, source_target_pairs={{0,2},{1,3},{2,0},{3,1},{4,6},{5,7},{6,4},{7,5},{8,10},{9,11},{10,... | collective-permute-start | bytes 983048 | tf_op jit(solution)/shard_map/ppermute | solution.py:329
  30.9 8.0 %collective-permute-start.7 = (bf16[10,32,256]{2,1,0:T(8,128)(2,1)S(1)}, bf16[10,32,256]{2,1,0:T(8,128)(2,1)S(1)}, u32[]{:S(2)}, u32[]{:S(2)}) collective-permute-start(bf16[10,32,256]{2,1,0:T(8,128)(2,1)S(1)} %get-tuple-element.87.refs_2_), channel_id=1, source_target_pairs={{0,12},{1,5},{2,14},{3,7},{4,8},{5,1},{6,10},{7,3},{8,4},{9,13},{1... | collective-permute-start | bytes 491528 | tf_op jit(solution)/shard_map/ppermute | solution.py:329
  39.0 6.5 %collective-permute-start.9 = (bf16[10,32,256]{2,1,0:T(8,128)(2,1)S(1)}, bf16[10,32,256]{2,1,0:T(8,128)(2,1)S(1)}, u32[]{:S(2)}, u32[]{:S(2)}) collective-permute-start(bf16[10,32,256]{2,1,0:T(8,128)(2,1)S(1)} %add.155.refs_2_.refs_0_), channel_id=1, source_target_pairs={{0,12},{1,5},{2,14},{3,7},{4,8},{5,1},{6,10},{7,3},{8,4},{9,13},{1... | collective-permute-start | bytes 491528 | tf_op jit(solution)/shard_map/ppermute | solution.py:329
  45.5 12.2 %collective-permute-start.11 = (bf16[20,32,256]{2,1,0:T(8,128)(2,1)S(1)}, bf16[20,32,256]{2,1,0:T(8,128)(2,1)S(1)}, u32[]{:S(2)}, u32[]{:S(2)}) collective-permute-start(bf16[20,32,256]{2,1,0:T(8,128)(2,1)S(1)} %join.12.refs_2_.refs_0_), channel_id=1, source_target_pairs={{0,2},{1,3},{2,0},{3,1},{4,6},{5,7},{6,4},{7,5},{8,10},{9,11},{10,... | collective-permute-start | bytes 983048 | tf_op jit(solution)/shard_map/ppermute | solution.py:329
  49.2 13.8 %collective-permute-start.10 = (bf16[20,32,256]{2,1,0:T(8,128)(2,1)S(1)}, bf16[20,32,256]{2,1,0:T(8,128)(2,1)S(1)}, u32[]{:S(2)}, u32[]{:S(2)}) collective-permute-start(bf16[20,32,256]{2,1,0:T(8,128)(2,1)S(1)} %join.13.refs_2_.refs_0_), channel_id=1, source_target_pairs={{0,2},{1,3},{2,0},{3,1},{4,6},{5,7},{6,4},{7,5},{8,10},{9,11},{10,... | collective-permute-start | bytes 983048 | tf_op jit(solution)/shard_map/ppermute | solution.py:329
  57.8 12.1 %collective-permute-start.13 = (bf16[40,32,256]{2,1,0:T(8,128)(2,1)S(1)}, bf16[40,32,256]{2,1,0:T(8,128)(2,1)S(1)}, u32[]{:S(2)}, u32[]{:S(2)}) collective-permute-start(bf16[40,32,256]{2,1,0:T(8,128)(2,1)S(1)} %join.14.refs_2_.refs_0_), channel_id=1, source_target_pairs={{0,4},{1,13},{2,6},{3,15},{4,0},{5,9},{6,2},{7,11},{8,12},{9,5},{1... | collective-permute-start | bytes 1966088 | tf_op jit(solution)/shard_map/ppermute | solution.py:329
  63.1 14.5 %collective-permute-start.12 = (bf16[40,32,256]{2,1,0:T(8,128)(2,1)S(1)}, bf16[40,32,256]{2,1,0:T(8,128)(2,1)S(1)}, u32[]{:S(2)}, u32[]{:S(2)}) collective-permute-start(bf16[40,32,256]{2,1,0:T(8,128)(2,1)S(1)} %join.15.refs_2_.refs_0_), channel_id=1, source_target_pairs={{0,4},{1,13},{2,6},{3,15},{4,0},{5,9},{6,2},{7,11},{8,12},{9,5},{1... | collective-permute-start | bytes 1966088 | tf_op jit(solution)/shard_map/ppermute | solution.py:329
  77.7 6.5 %collective-permute-start.16 = (bf16[80,32,256]{2,1,0:T(8,128)(2,1)S(1)}, bf16[80,32,256]{2,1,0:T(8,128)(2,1)S(1)}, u32[]{:S(2)}, u32[]{:S(2)}) collective-permute-start(bf16[80,32,256]{2,1,0:T(8,128)(2,1)S(1)} %join.17.refs_2_.refs_3_), channel_id=1, source_target_pairs={{0,1},{1,0},{2,3},{3,2},{4,5},{5,4},{6,7},{7,6},{8,9},{9,8},{10,11... | collective-permute-start | bytes 3932168 | tf_op jit(solution)/shard_map/ppermute | solution.py:329
  78.7 9.1 %collective-permute-start.18 = (bf16[80,1024]{1,0:T(8,128)(2,1)S(1)}, bf16[80,1024]{1,0:T(8,128)(2,1)S(1)}, u32[]{:S(2)}, u32[]{:S(2)}) collective-permute-start(bf16[80,1024]{1,0:T(8,128)(2,1)S(1)} %add.157.refs_5_.refs_0_), channel_id=1, source_target_pairs={{0,4},{1,13},{2,6},{3,15},{4,0},{5,9},{6,2},{7,11},{8,12},{9,5},{1... | collective-permute-start | bytes 491528 | tf_op jit(solution)/shard_map/ppermute | solution.py:329
  87.8 8.2 %collective-permute-start.20 = (bf16[80,1024]{1,0:T(8,128)(2,1)S(1)}, bf16[80,1024]{1,0:T(8,128)(2,1)S(1)}, u32[]{:S(2)}, u32[]{:S(2)}) collective-permute-start(bf16[80,1024]{1,0:T(8,128)(2,1)S(1)} %add.158.refs_2_.refs_0_), channel_id=1, source_target_pairs={{0,2},{1,3},{2,0},{3,1},{4,6},{5,7},{6,4},{7,5},{8,10},{9,11},{10,... | collective-permute-start | bytes 491528 | tf_op jit(solution)/shard_map/ppermute | solution.py:329
  91.0 6.3 %collective-permute-start.19 = (bf16[80,1024]{1,0:T(8,128)(2,1)S(1)}, bf16[80,1024]{1,0:T(8,128)(2,1)S(1)}, u32[]{:S(2)}, u32[]{:S(2)}) collective-permute-start(bf16[80,1024]{1,0:T(8,128)(2,1)S(1)} %add.159.refs_2_.refs_0_), channel_id=1, source_target_pairs={{0,4},{1,13},{2,6},{3,15},{4,0},{5,9},{6,2},{7,11},{8,12},{9,5},{1... | collective-permute-start | bytes 491528 | tf_op jit(solution)/shard_map/ppermute | solution.py:329
  97.4 6.9 %collective-permute-start.21 = (bf16[80,1024]{1,0:T(8,128)(2,1)S(1)}, bf16[80,1024]{1,0:T(8,128)(2,1)S(1)}, u32[]{:S(2)}, u32[]{:S(2)}) collective-permute-start(bf16[80,1024]{1,0:T(8,128)(2,1)S(1)} %add.161.refs_2_.refs_0_), channel_id=1, source_target_pairs={{0,2},{1,3},{2,0},{3,1},{4,6},{5,7},{6,4},{7,5},{8,10},{9,11},{10,... | collective-permute-start | bytes 491528 | tf_op jit(solution)/shard_map/ppermute | solution.py:329
  104.3 9.0 %collective-permute-start.23 = (bf16[80,1024]{1,0:T(8,128)(2,1)S(1)}, bf16[80,1024]{1,0:T(8,128)(2,1)S(1)}, u32[]{:S(2)}, u32[]{:S(2)}) collective-permute-start(bf16[80,1024]{1,0:T(8,128)(2,1)S(1)} %add.163.refs_7_.refs_0_), channel_id=1, source_target_pairs={{0,12},{1,5},{2,14},{3,7},{4,8},{5,1},{6,10},{7,3},{8,4},{9,13},{1... | collective-permute-start | bytes 491528 | tf_op jit(solution)/shard_map/ppermute | solution.py:329
  114.3 14.7 %collective-permute-start.29 = (bf16[40,32,256]{2,1,0:T(8,128)(2,1)S(1)}, bf16[40,32,256]{2,1,0:T(8,128)(2,1)S(1)}, u32[]{:S(2)}, u32[]{:S(2)}) collective-permute-start(bf16[40,32,256]{2,1,0:T(8,128)(2,1)S(1)} %get-tuple-element.101.refs_7_), channel_id=1, source_target_pairs={{0,4},{1,13},{2,6},{3,15},{4,0},{5,9},{6,2},{7,11},{8,12},{9,5},{1... | collective-permute-start | bytes 1966088 | tf_op jit(solution)/shard_map/ppermute | solution.py:329
  125.3 10.7 %collective-permute-start.28 = (bf16[40,32,256]{2,1,0:T(8,128)(2,1)S(1)}, bf16[40,32,256]{2,1,0:T(8,128)(2,1)S(1)}, u32[]{:S(2)}, u32[]{:S(2)}) collective-permute-start(bf16[40,32,256]{2,1,0:T(8,128)(2,1)S(1)} %get-tuple-element.106.refs_8_), channel_id=1, source_target_pairs={{0,4},{1,13},{2,6},{3,15},{4,0},{5,9},{6,2},{7,11},{8,12},{9,5},{1... | collective-permute-start | bytes 1966088 | tf_op jit(solution)/shard_map/ppermute | solution.py:329
  129.5 11.6 %collective-permute-start.31 = (bf16[20,32,256]{2,1,0:T(8,128)(2,1)S(1)}, bf16[20,32,256]{2,1,0:T(8,128)(2,1)S(1)}, u32[]{:S(2)}, u32[]{:S(2)}) collective-permute-start(bf16[20,32,256]{2,1,0:T(8,128)(2,1)S(1)} %get-tuple-element.117.refs_2_), channel_id=1, source_target_pairs={{0,2},{1,3},{2,0},{3,1},{4,6},{5,7},{6,4},{7,5},{8,10},{9,11},{10,... | collective-permute-start | bytes 983048 | tf_op jit(solution)/shard_map/ppermute | solution.py:329
  132.6 26.0 %collective-permute-start.35 = (bf16[1024,1024]{1,0:T(8,128)(2,1)S(1)}, bf16[1024,1024]{1,0:T(8,128)(2,1)S(1)}, u32[]{:S(2)}, u32[]{:S(2)}) collective-permute-start(bf16[1024,1024]{1,0:T(8,128)(2,1)S(1)} %get-tuple-element.126), channel_id=1, source_target_pairs={{0,32},{1,97},{2,34},{3,99},{4,36},{5,101},{6,38},{7,103},{8,40},{... | collective-permute-start | bytes 6291464 | tf_op jit(solution)/shard_map/ppermute | solution.py:337
  136.1 11.5 %collective-permute-start.30 = (bf16[20,32,256]{2,1,0:T(8,128)(2,1)S(1)}, bf16[20,32,256]{2,1,0:T(8,128)(2,1)S(1)}, u32[]{:S(2)}, u32[]{:S(2)}) collective-permute-start(bf16[20,32,256]{2,1,0:T(8,128)(2,1)S(1)} %get-tuple-element.119.refs_2_), channel_id=1, source_target_pairs={{0,2},{1,3},{2,0},{3,1},{4,6},{5,7},{6,4},{7,5},{8,10},{9,11},{10,... | collective-permute-start | bytes 983048 | tf_op jit(solution)/shard_map/ppermute | solution.py:329
  141.2 7.7 %collective-permute-start.33 = (bf16[10,32,256]{2,1,0:T(8,128)(2,1)S(1)}, bf16[10,32,256]{2,1,0:T(8,128)(2,1)S(1)}, u32[]{:S(2)}, u32[]{:S(2)}) collective-permute-start(bf16[10,32,256]{2,1,0:T(8,128)(2,1)S(1)} %get-tuple-element.121.refs_2_), channel_id=1, source_target_pairs={{0,12},{1,5},{2,14},{3,7},{4,8},{5,1},{6,10},{7,3},{8,4},{9,13},{1... | collective-permute-start | bytes 491528 | tf_op jit(solution)/shard_map/ppermute | solution.py:329
  148.9 5.9 %collective-permute-start.36 = (bf16[10,32,256]{2,1,0:T(8,128)(2,1)S(1)}, bf16[10,32,256]{2,1,0:T(8,128)(2,1)S(1)}, u32[]{:S(2)}, u32[]{:S(2)}) collective-permute-start(bf16[10,32,256]{2,1,0:T(8,128)(2,1)S(1)} %add.171.refs_2_.refs_0_), channel_id=1, source_target_pairs={{0,12},{1,5},{2,14},{3,7},{4,8},{5,1},{6,10},{7,3},{8,4},{9,13},{1... | collective-permute-start | bytes 491528 | tf_op jit(solution)/shard_map/ppermute | solution.py:329
  153.1 9.6 %collective-permute-start.34 = (bf16[10,32,256]{2,1,0:T(8,128)(2,1)S(1)}, bf16[10,32,256]{2,1,0:T(8,128)(2,1)S(1)}, u32[]{:S(2)}, u32[]{:S(2)}) collective-permute-start(bf16[10,32,256]{2,1,0:T(8,128)(2,1)S(1)} %add.172.refs_2_.refs_0_), channel_id=1, source_target_pairs={{0,12},{1,5},{2,14},{3,7},{4,8},{5,1},{6,10},{7,3},{8,4},{9,13},{1... | collective-permute-start | bytes 491528 | tf_op jit(solution)/shard_map/ppermute | solution.py:329
  154.8 11.3 %collective-permute-start.38 = (bf16[20,32,256]{2,1,0:T(8,128)(2,1)S(1)}, bf16[20,32,256]{2,1,0:T(8,128)(2,1)S(1)}, u32[]{:S(2)}, u32[]{:S(2)}) collective-permute-start(bf16[20,32,256]{2,1,0:T(8,128)(2,1)S(1)} %join.18.refs_2_.refs_0_), channel_id=1, source_target_pairs={{0,2},{1,3},{2,0},{3,1},{4,6},{5,7},{6,4},{7,5},{8,10},{9,11},{10,... | collective-permute-start | bytes 983048 | tf_op jit(solution)/shard_map/ppermute | solution.py:329
  159.5 20.6 %collective-permute-start.42 = (bf16[512,1024]{1,0:T(8,128)(2,1)S(1)}, bf16[512,1024]{1,0:T(8,128)(2,1)S(1)}, u32[]{:S(2)}, u32[]{:S(2)}) collective-permute-start(bf16[512,1024]{1,0:T(8,128)(2,1)S(1)} %get-tuple-element.127.refs_2_), channel_id=1, source_target_pairs={{0,96},{1,33},{2,98},{3,35},{4,100},{5,37},{6,102},{7,39},{8,104},... | collective-permute-start | bytes 3145736 | tf_op jit(solution)/shard_map/ppermute | solution.py:337
  162.7 9.1 %collective-permute-start.37 = (bf16[20,32,256]{2,1,0:T(8,128)(2,1)S(1)}, bf16[20,32,256]{2,1,0:T(8,128)(2,1)S(1)}, u32[]{:S(2)}, u32[]{:S(2)}) collective-permute-start(bf16[20,32,256]{2,1,0:T(8,128)(2,1)S(1)} %join.19.refs_2_.refs_0_), channel_id=1, source_target_pairs={{0,2},{1,3},{2,0},{3,1},{4,6},{5,7},{6,4},{7,5},{8,10},{9,11},{10,... | collective-permute-start | bytes 983048 | tf_op jit(solution)/shard_map/ppermute | solution.py:329
  166.2 11.6 %collective-permute-start.40 = (bf16[40,32,256]{2,1,0:T(8,128)(2,1)S(1)}, bf16[40,32,256]{2,1,0:T(8,128)(2,1)S(1)}, u32[]{:S(2)}, u32[]{:S(2)}) collective-permute-start(bf16[40,32,256]{2,1,0:T(8,128)(2,1)S(1)} %join.20.refs_2_.refs_0_), channel_id=1, source_target_pairs={{0,4},{1,13},{2,6},{3,15},{4,0},{5,9},{6,2},{7,11},{8,12},{9,5},{1... | collective-permute-start | bytes 1966088 | tf_op jit(solution)/shard_map/ppermute | solution.py:329
  171.9 12.9 %collective-permute-start.39 = (bf16[40,32,256]{2,1,0:T(8,128)(2,1)S(1)}, bf16[40,32,256]{2,1,0:T(8,128)(2,1)S(1)}, u32[]{:S(2)}, u32[]{:S(2)}) collective-permute-start(bf16[40,32,256]{2,1,0:T(8,128)(2,1)S(1)} %join.21.refs_2_.refs_0_), channel_id=1, source_target_pairs={{0,4},{1,13},{2,6},{3,15},{4,0},{5,9},{6,2},{7,11},{8,12},{9,5},{1... | collective-permute-start | bytes 1966088 | tf_op jit(solution)/shard_map/ppermute | solution.py:329
  180.5 16.7 %collective-permute-start.45 = (bf16[256,1024]{1,0:T(8,128)(2,1)S(1)}, bf16[256,1024]{1,0:T(8,128)(2,1)S(1)}, u32[]{:S(2)}, u32[]{:S(2)}) collective-permute-start(bf16[256,1024]{1,0:T(8,128)(2,1)S(1)} %get-tuple-element.129.refs_4_), channel_id=1, source_target_pairs={{0,16},{1,17},{2,18},{3,19},{4,20},{5,21},{6,22},{7,23},{8,24},{9,... | collective-permute-start | bytes 1572872 | tf_op jit(solution)/shard_map/ppermute | solution.py:337
  184.9 5.5 %collective-permute-start.43 = (bf16[80,32,256]{2,1,0:T(8,128)(2,1)S(1)}, bf16[80,32,256]{2,1,0:T(8,128)(2,1)S(1)}, u32[]{:S(2)}, u32[]{:S(2)}) collective-permute-start(bf16[80,32,256]{2,1,0:T(8,128)(2,1)S(1)} %join.23.refs_6_.refs_1_.refs_4_), channel_id=1, source_target_pairs={{0,1},{1,0},{2,3},{3,2},{4,5},{5,4},{6,7},{7,6},{8,9},{9,8},{10,11... | collective-permute-start | bytes 3932168 | tf_op jit(solution)/shard_map/ppermute | solution.py:329
  192.2 6.0 %collective-permute-start.44 = (f32[40,128]{1,0:T(8,128)S(1)}, f32[40,128]{1,0:T(8,128)S(1)}, u32[]{:S(2)}, u32[]{:S(2)}) collective-permute-start(f32[40,128]{1,0:T(8,128)S(1)} %grad_projection.7.refs_7_.refs_0_), channel_id=1, source_target_pairs={{0,32},{1,97},{2,34},{3,99},{4,36},{5,101},{6,38},{7,103},{8,40},{... | collective-permute-start | bytes 61448 | tf_op jit(solution)/shard_map/ppermute | solution.py:337
  (43 other events, 238.5 us)

commit v5 on v4

--- a/solution.py
+++ b/solution.py
@@ -14,10 +14,10 @@
 ORDERS = (("AZB", "BZA"), ("AZB", "BZA"))
 DP_ORDERS = ("ABZ", "BAZ")
 ORDER = (
-    0, 0, 0, 1, 1, 1, 0, 1, 0, 1, 0, 1, 0, 1, 0, 1, 0, 0, 0, 1,
-    0, 1, 1, 0, 1, 0, 1, 0, 1, 0, 0, 1, 0, 1, 1, 1, "w", 0, 1, 0,
-    1, 0, 1, 0, "w", 1, 0, 1, 0, 0, "w", 0, 1, 0, 1, 1, "s", 1, "w", "s",
-    0, "s", 1, "s",
+    0, 0, 0, 1, 1, 1, 0, 1, 0, 0, 1, 0, 1, 1, 0, 1, 0, 0, 0, 0,
+    1, 1, 0, 1, 1, 0, 1, 0, 0, 1, 0, 1, 0, 1, 1, 1, 0, "w", 1, 0,
+    0, 1, 0, 1, 1, 0, "w", 0, 1, 0, 0, 0, "w", 1, 1, 1, "s", 1, "s", 0,
+    "s", 1, "w", "s",
 )
 
 

time: 213 us -> 244 us (1.15)
  waiting for transfers between devices: 59.1 us -> 88.7 us
    ppermute x42, waiting for transfers between devices: 58.4 us -> 76 us  [tok_swap(): return lax.ppermute(x, 'tok', pairs)]
    ppermute x6, waiting for transfers between devices: 0.71 us -> 12.7 us  [dp_swap(): return lax.ppermute(x, ('dp', 'tok'), pairs)]
  transfers between devices with their start and end apart: 48 -> 48, of which waited for: 25 -> 27; matrix products, arithmetic and copies ran while one was open for 0% -> 0% of each run, Pallas kernels for 32% -> 26%
where the time goes in v5:
time: 244 us; the launch traced here: 239 us
  waiting for transfers between devices  88.7 us (36%)
  starting transfers between devices  74 us (30%)
  Pallas kernels  72.5 us (30%)
    ppermute x42, waiting for transfers between devices, tok_swap(): return lax.ppermute(x, 'tok', pairs)  76 us
    pallas_call x63, Pallas kernels, call(): pl.pallas_call(run, out_shape=outs, in_specs=specs, out_specs=[place(out)...  72.5 us
    ppermute x42, starting transfers between devices, tok_swap(): return lax.ppermute(x, 'tok', pairs)  63.7 us
    ppermute x6, waiting for transfers between devices, dp_swap(): return lax.ppermute(x, ('dp', 'tok'), pairs)  12.7 us
    ppermute x6, starting transfers between devices, dp_swap(): return lax.ppermute(x, ('dp', 'tok'), pairs)  10.3 us
  transfers between devices with their start and end apart: 48, of which 27 were waited for; matrix products, arithmetic and copies ran while one was open for 0% of the time, Pallas kernels for 26%

profile of v5, /device:TPU:4, one launch (start us, length us, event | category | flops | bytes accessed | tf_op | source)
XLA Modules:
  0.0 238.9 jit_solution(14544996250424153353)
XLA Ops:
  19.3 4.0 %collective-permute-start.5 = (bf16[20,32,256]{2,1,0:T(8,128)(2,1)S(1)}, bf16[20,32,256]{2,1,0:T(8,128)(2,1)S(1)}, u32[]{:S(2)}, u32[]{:S(2)}) collective-permute-start(bf16[20,32,256]{2,1,0:T(8,128)(2,1)S(1)} %get-tuple-element.83.refs_2_), channel_id=1, source_target_pairs={{0,2},{1,3},{2,0},{3,1},{4,6},{5,7},{6,4},{7,5},{8,10},{9,11},{10,... | collective-permute-start | bytes 983048 | tf_op jit(solution)/shard_map/ppermute | solution.py:329
  23.2 3.5 %collective-permute-done.2.refs_1_ = bf16[40,32,256]{2,1,0:T(8,128)(2,1)S(1)} collective-permute-done((bf16[40,32,256]{2,1,0:T(8,128)(2,1)S(1)}, bf16[40,32,256]{2,1,0:T(8,128)(2,1)S(1)}, u32[]{:S(2)}, u32[]{:S(2)}) %collective-permute-start.2) | collective-permute-done | bytes 655392 | tf_op jit(solution)/shard_map/ppermute | solution.py:329
  26.9 3.7 %collective-permute-done.5.refs_1_ = bf16[20,32,256]{2,1,0:T(8,128)(2,1)S(1)} collective-permute-done((bf16[20,32,256]{2,1,0:T(8,128)(2,1)S(1)}, bf16[20,32,256]{2,1,0:T(8,128)(2,1)S(1)}, u32[]{:S(2)}, u32[]{:S(2)}) %collective-permute-start.5) | collective-permute-done | bytes 327712 | tf_op jit(solution)/shard_map/ppermute | solution.py:329
  36.8 6.5 %collective-permute-done.4.refs_1_ = bf16[20,32,256]{2,1,0:T(8,128)(2,1)S(1)} collective-permute-done((bf16[20,32,256]{2,1,0:T(8,128)(2,1)S(1)}, bf16[20,32,256]{2,1,0:T(8,128)(2,1)S(1)}, u32[]{:S(2)}, u32[]{:S(2)}) %collective-permute-start.4) | collective-permute-done | bytes 327712 | tf_op jit(solution)/shard_map/ppermute | solution.py:329
  43.6 5.1 %collective-permute-done.7.refs_1_ = bf16[10,32,256]{2,1,0:T(8,128)(2,1)S(1)} collective-permute-done((bf16[10,32,256]{2,1,0:T(8,128)(2,1)S(1)}, bf16[10,32,256]{2,1,0:T(8,128)(2,1)S(1)}, u32[]{:S(2)}, u32[]{:S(2)}) %collective-permute-start.7) | collective-permute-done | bytes 163872 | tf_op jit(solution)/shard_map/ppermute | solution.py:329
  49.0 3.3 %collective-permute-start.11 = (bf16[20,32,256]{2,1,0:T(8,128)(2,1)S(1)}, bf16[20,32,256]{2,1,0:T(8,128)(2,1)S(1)}, u32[]{:S(2)}, u32[]{:S(2)}) collective-permute-start(bf16[20,32,256]{2,1,0:T(8,128)(2,1)S(1)} %join.12.refs_2_.refs_0_), channel_id=1, source_target_pairs={{0,2},{1,3},{2,0},{3,1},{4,6},{5,7},{6,4},{7,5},{8,10},{9,11},{10,... | collective-permute-start | bytes 983048 | tf_op jit(solution)/shard_map/ppermute | solution.py:329
  54.2 3.5 %collective-permute-start.10 = (bf16[20,32,256]{2,1,0:T(8,128)(2,1)S(1)}, bf16[20,32,256]{2,1,0:T(8,128)(2,1)S(1)}, u32[]{:S(2)}, u32[]{:S(2)}) collective-permute-start(bf16[20,32,256]{2,1,0:T(8,128)(2,1)S(1)} %join.13.refs_2_.refs_0_), channel_id=1, source_target_pairs={{0,2},{1,3},{2,0},{3,1},{4,6},{5,7},{6,4},{7,5},{8,10},{9,11},{10,... | collective-permute-start | bytes 983048 | tf_op jit(solution)/shard_map/ppermute | solution.py:329
  57.6 3.5 %collective-permute-done.11.refs_1_ = bf16[20,32,256]{2,1,0:T(8,128)(2,1)S(1)} collective-permute-done((bf16[20,32,256]{2,1,0:T(8,128)(2,1)S(1)}, bf16[20,32,256]{2,1,0:T(8,128)(2,1)S(1)}, u32[]{:S(2)}, u32[]{:S(2)}) %collective-permute-start.11) | collective-permute-done | bytes 327712 | tf_op jit(solution)/shard_map/ppermute | solution.py:329
  66.5 5.8 %collective-permute-done.13.refs_1_ = bf16[40,32,256]{2,1,0:T(8,128)(2,1)S(1)} collective-permute-done((bf16[40,32,256]{2,1,0:T(8,128)(2,1)S(1)}, bf16[40,32,256]{2,1,0:T(8,128)(2,1)S(1)}, u32[]{:S(2)}, u32[]{:S(2)}) %collective-permute-start.13) | collective-permute-done | bytes 655392 | tf_op jit(solution)/shard_map/ppermute | solution.py:329
  72.6 3.4 %field.4 = (bf16[80,2048]{1,0:T(8,128)(2,1)S(1)}, bf16[80,1024]{1,0:T(8,128)(2,1)S(1)}) custom-call(s32[80]{0:T(128)S(1)} %copy-done.4, s32[8]{0:T(128)S(1)} %copy-done.22, bf16[80,32,256]{2,1,0:T(8,128)(2,1)S(1)} %join.16.refs_2_.refs_5_.refs_3_, bf16[80,64,256]{2,1,0:T(8,128)(2,1)S(1)} %get-tuple-element.91.refs_3_.refs_5_.refs_2_, ...), custom_call_target="tpu_custom_call" | custom-call | flops 20000000000 | bytes 1000 | tf_op jit(solution)/shard_map/field/pallas_call | solution.py:43
  76.1 3.4 %field.5 = (bf16[80,2048]{1,0:T(8,128)(2,1)S(1)}, bf16[80,1024]{1,0:T(8,128)(2,1)S(1)}) custom-call(s32[80]{0:T(128)S(1)} %copy-done.1, s32[8]{0:T(128)S(1)} %copy-done.22, bf16[80,32,256]{2,1,0:T(8,128)(2,1)S(1)} %collective-permute-done.14.refs_2_.refs_3_, bf16[80,64,256]{2,1,0:T(8,128)(2,1)S(1)} %get-tuple-element.93.refs_3_.refs_5_.refs_2_, ...), custom_call_target="tpu_custom_call" | custom-call | flops 20000000000 | bytes 1000 | tf_op jit(solution)/shard_map/field/pallas_call | solution.py:43
  83.2 7.4 %collective-permute-done.12.refs_1_ = bf16[40,32,256]{2,1,0:T(8,128)(2,1)S(1)} collective-permute-done((bf16[40,32,256]{2,1,0:T(8,128)(2,1)S(1)}, bf16[40,32,256]{2,1,0:T(8,128)(2,1)S(1)}, u32[]{:S(2)}, u32[]{:S(2)}) %collective-permute-start.12) | collective-permute-done | bytes 655392 | tf_op jit(solution)/shard_map/ppermute | solution.py:329
  90.8 3.4 %field.6 = (bf16[80,2048]{1,0:T(8,128)(2,1)S(1)}, bf16[80,1024]{1,0:T(8,128)(2,1)S(1)}) custom-call(s32[80]{0:T(128)S(1)} %copy-done.4, s32[8]{0:T(128)S(1)} %copy-done.22, bf16[80,32,256]{2,1,0:T(8,128)(2,1)S(1)} %join.17.refs_2_.refs_5_.refs_3_, bf16[80,64,256]{2,1,0:T(8,128)(2,1)S(1)} %get-tuple-element.95.refs_3_.refs_5_.refs_2_, ...), custom_call_target="tpu_custom_call" | custom-call | flops 20000000000 | bytes 1000 | tf_op jit(solution)/shard_map/field/pallas_call | solution.py:43
  94.3 3.4 %field.7 = (bf16[80,2048]{1,0:T(8,128)(2,1)S(1)}, bf16[80,1024]{1,0:T(8,128)(2,1)S(1)}) custom-call(s32[80]{0:T(128)S(1)} %copy-done.1, s32[8]{0:T(128)S(1)} %copy-done.22, bf16[80,32,256]{2,1,0:T(8,128)(2,1)S(1)} %collective-permute-done.16.refs_2_.refs_3_, bf16[80,64,256]{2,1,0:T(8,128)(2,1)S(1)} %get-tuple-element.97.refs_3_.refs_5_.refs_2_, ...), custom_call_target="tpu_custom_call" | custom-call | flops 20000000000 | bytes 1000 | tf_op jit(solution)/shard_map/field/pallas_call | solution.py:43
  98.3 3.3 %collective-permute-start.20 = (bf16[80,1024]{1,0:T(8,128)(2,1)S(1)}, bf16[80,1024]{1,0:T(8,128)(2,1)S(1)}, u32[]{:S(2)}, u32[]{:S(2)}) collective-permute-start(bf16[80,1024]{1,0:T(8,128)(2,1)S(1)} %add.158.refs_5_.refs_0_), channel_id=1, source_target_pairs={{0,2},{1,3},{2,0},{3,1},{4,6},{5,7},{6,4},{7,5},{8,10},{9,11},{10,... | collective-permute-start | bytes 491528 | tf_op jit(solution)/shard_map/ppermute | solution.py:329
  107.1 4.4 %collective-permute-done.22.refs_1_ = bf16[80,1024]{1,0:T(8,128)(2,1)S(1)} collective-permute-done((bf16[80,1024]{1,0:T(8,128)(2,1)S(1)}, bf16[80,1024]{1,0:T(8,128)(2,1)S(1)}, u32[]{:S(2)}, u32[]{:S(2)}) %collective-permute-start.22) | collective-permute-done | bytes 163872 | tf_op jit(solution)/shard_map/ppermute | solution.py:329
  111.7 3.5 %collective-permute-start.21 = (bf16[80,1024]{1,0:T(8,128)(2,1)S(1)}, bf16[80,1024]{1,0:T(8,128)(2,1)S(1)}, u32[]{:S(2)}, u32[]{:S(2)}) collective-permute-start(bf16[80,1024]{1,0:T(8,128)(2,1)S(1)} %add.161.refs_2_.refs_0_), channel_id=1, source_target_pairs={{0,2},{1,3},{2,0},{3,1},{4,6},{5,7},{6,4},{7,5},{8,10},{9,11},{10,... | collective-permute-start | bytes 491528 | tf_op jit(solution)/shard_map/ppermute | solution.py:329
  115.2 3.9 %grad_compress.4 = (bf16[80,1024]{1,0:T(8,128)(2,1)S(1)}, bf16[80,2048]{1,0:T(8,128)(2,1)S(1)}, bf16[80,32,256]{2,1,0:T(8,128)(2,1)S(1)}) custom-call(s32[80]{0:T(128)S(1)} %copy-done.1, s32[1]{0:T(128)} %bitcast.4.refs_1_.refs_9_, bf16[80,1024]{1,0:T(8,128)(2,1)S(1)} %collective-permute-done.23.refs_2_, bf16[320,1024]{1,0:T(8,128)(2,1)S(1)} %copy-done.15, ...), custom_call_target="tpu_custom_call" | custom-call | flops 20000000000 | bytes 1000 | tf_op jit(solution)/shard_map/grad_compress/pallas_call | solution.py:43
  120.1 3.9 %grad_compress.5 = (bf16[80,1024]{1,0:T(8,128)(2,1)S(1)}, bf16[80,2048]{1,0:T(8,128)(2,1)S(1)}, bf16[80,32,256]{2,1,0:T(8,128)(2,1)S(1)}) custom-call(s32[80]{0:T(128)S(1)} %copy-done.5, s32[1]{0:T(128)} %bitcast.3.refs_8_.refs_1_, bf16[80,1024]{1,0:T(8,128)(2,1)S(1)} %add.162.refs_7_.refs_2_, bf16[320,1024]{1,0:T(8,128)(2,1)S(1)} %copy-done.15, ...), custom_call_target="tpu_custom_call" | custom-call | flops 20000000000 | bytes 1000 | tf_op jit(solution)/shard_map/grad_compress/pallas_call | solution.py:43
  130.4 3.9 %grad_compress.6 = (bf16[80,1024]{1,0:T(8,128)(2,1)S(1)}, bf16[80,2048]{1,0:T(8,128)(2,1)S(1)}, bf16[80,32,256]{2,1,0:T(8,128)(2,1)S(1)}) custom-call(s32[80]{0:T(128)S(1)} %copy-done.1, s32[1]{0:T(128)} %bitcast.refs_13_.refs_1_, bf16[80,1024]{1,0:T(8,128)(2,1)S(1)} %collective-permute-done.25.refs_2_, bf16[320,1024]{1,0:T(8,128)(2,1)S(1)} %copy-done.15, ...), custom_call_target="tpu_custom_call" | custom-call | flops 20000000000 | bytes 1000 | tf_op jit(solution)/shard_map/grad_compress/pallas_call | solution.py:43
  134.4 3.9 %grad_compress.7 = (bf16[80,1024]{1,0:T(8,128)(2,1)S(1)}, bf16[80,2048]{1,0:T(8,128)(2,1)S(1)}, bf16[80,32,256]{2,1,0:T(8,128)(2,1)S(1)}) custom-call(s32[80]{0:T(128)S(1)} %copy-done.5, s32[1]{0:T(128)} %bitcast.1.refs_12_.refs_1_, bf16[80,1024]{1,0:T(8,128)(2,1)S(1)} %add.164.refs_2_, bf16[320,1024]{1,0:T(8,128)(2,1)S(1)} %copy-done.15, ...), custom_call_target="tpu_custom_call" | custom-call | flops 20000000000 | bytes 1000 | tf_op jit(solution)/shard_map/grad_compress/pallas_call | solution.py:43
  140.0 3.3 %collective-permute-start.31 = (bf16[20,32,256]{2,1,0:T(8,128)(2,1)S(1)}, bf16[20,32,256]{2,1,0:T(8,128)(2,1)S(1)}, u32[]{:S(2)}, u32[]{:S(2)}) collective-permute-start(bf16[20,32,256]{2,1,0:T(8,128)(2,1)S(1)} %get-tuple-element.116.refs_8_), channel_id=1, source_target_pairs={{0,2},{1,3},{2,0},{3,1},{4,6},{5,7},{6,4},{7,5},{8,10},{9,11},{10,... | collective-permute-start | bytes 983048 | tf_op jit(solution)/shard_map/ppermute | solution.py:329
  145.7 3.6 %collective-permute-done.28.refs_1_ = bf16[40,32,256]{2,1,0:T(8,128)(2,1)S(1)} collective-permute-done((bf16[40,32,256]{2,1,0:T(8,128)(2,1)S(1)}, bf16[40,32,256]{2,1,0:T(8,128)(2,1)S(1)}, u32[]{:S(2)}, u32[]{:S(2)}) %collective-permute-start.28) | collective-permute-done | bytes 655392 | tf_op jit(solution)/shard_map/ppermute | solution.py:329
  158.0 6.4 %collective-permute-done.30.refs_1_ = bf16[20,32,256]{2,1,0:T(8,128)(2,1)S(1)} collective-permute-done((bf16[20,32,256]{2,1,0:T(8,128)(2,1)S(1)}, bf16[20,32,256]{2,1,0:T(8,128)(2,1)S(1)}, u32[]{:S(2)}, u32[]{:S(2)}) %collective-permute-start.30) | collective-permute-done | bytes 327712 | tf_op jit(solution)/shard_map/ppermute | solution.py:329
  165.1 4.8 %collective-permute-done.33.refs_1_ = bf16[10,32,256]{2,1,0:T(8,128)(2,1)S(1)} collective-permute-done((bf16[10,32,256]{2,1,0:T(8,128)(2,1)S(1)}, bf16[10,32,256]{2,1,0:T(8,128)(2,1)S(1)}, u32[]{:S(2)}, u32[]{:S(2)}) %collective-permute-start.33) | collective-permute-done | bytes 163872 | tf_op jit(solution)/shard_map/ppermute | solution.py:329
  175.3 3.3 %collective-permute-start.36 = (bf16[20,32,256]{2,1,0:T(8,128)(2,1)S(1)}, bf16[20,32,256]{2,1,0:T(8,128)(2,1)S(1)}, u32[]{:S(2)}, u32[]{:S(2)}) collective-permute-start(bf16[20,32,256]{2,1,0:T(8,128)(2,1)S(1)} %join.19.refs_2_.refs_0_), channel_id=1, source_target_pairs={{0,2},{1,3},{2,0},{3,1},{4,6},{5,7},{6,4},{7,5},{8,10},{9,11},{10,... | collective-permute-start | bytes 983048 | tf_op jit(solution)/shard_map/ppermute | solution.py:329
  178.7 5.5 %collective-permute-done.37.refs_1_ = bf16[20,32,256]{2,1,0:T(8,128)(2,1)S(1)} collective-permute-done((bf16[20,32,256]{2,1,0:T(8,128)(2,1)S(1)}, bf16[20,32,256]{2,1,0:T(8,128)(2,1)S(1)}, u32[]{:S(2)}, u32[]{:S(2)}) %collective-permute-start.37) | collective-permute-done | bytes 327712 | tf_op jit(solution)/shard_map/ppermute | solution.py:329
  186.6 9.9 %collective-permute-done.39.refs_1_ = bf16[1024,1024]{1,0:T(8,128)(2,1)S(1)} collective-permute-done((bf16[1024,1024]{1,0:T(8,128)(2,1)S(1)}, bf16[1024,1024]{1,0:T(8,128)(2,1)S(1)}, u32[]{:S(2)}, u32[]{:S(2)}) %collective-permute-start.39) | collective-permute-done | bytes 2097184 | tf_op jit(solution)/shard_map/ppermute | solution.py:337
  207.3 3.4 %grad_tokens.4 = (bf16[320,64,256]{2,1,0:T(8,128)(2,1)}, f32[8,128]{1,0:T(8,128)S(1)}) custom-call(s32[80]{0:T(128)S(1)} %copy-done.5, s32[1]{0:T(128)} %bitcast.3.refs_8_.refs_1_, bf16[80,2048]{1,0:T(8,128)(2,1)S(1)} %get-tuple-element.129.refs_2_, bf16[80,32,256]{2,1,0:T(8,128)(2,1)S(1)} %copy-done.14, ...), custom_call_target="tpu_custom_call" | custom-call | flops 20000000000 | bytes 1000 | tf_op jit(solution)/shard_map/grad_tokens/pallas_call | solution.py:43
  221.4 3.4 %grad_tokens.5 = (bf16[320,64,256]{2,1,0:T(8,128)(2,1)}, f32[8,128]{1,0:T(8,128)S(1)}) custom-call(s32[80]{0:T(128)S(1)} %copy-done.5, s32[1]{0:T(128)} %bitcast.1.refs_12_.refs_1_, bf16[80,2048]{1,0:T(8,128)(2,1)S(1)} %get-tuple-element.133.refs_2_, bf16[80,32,256]{2,1,0:T(8,128)(2,1)S(1)} %copy-done.12, ...), custom_call_target="tpu_custom_call", output_to_operand_aliasing={{0}: (6, {})} | custom-call | flops 20000000000 | bytes 1000 | tf_op jit(solution)/shard_map/grad_tokens/pallas_call | solution.py:43
  228.0 3.4 %grad_tokens.6 = (bf16[320,64,256]{2,1,0:T(8,128)(2,1)}, f32[8,128]{1,0:T(8,128)S(1)}) custom-call(s32[80]{0:T(128)S(1)} %copy-done.2, s32[1]{0:T(128)} %bitcast.4.refs_1_.refs_9_, bf16[80,2048]{1,0:T(8,128)(2,1)S(1)} %get-tuple-element.132.refs_2_, bf16[80,32,256]{2,1,0:T(8,128)(2,1)S(1)} %copy-done.8, ...), custom_call_target="tpu_custom_call", output_to_operand_aliasing={{0}: (6, {})} | custom-call | flops 20000000000 | bytes 1000 | tf_op jit(solution)/shard_map/grad_tokens/pallas_call | solution.py:43
  232.8 3.4 %grad_tokens.7 = (bf16[320,64,256]{2,1,0:T(8,128)(2,1)}, f32[8,128]{1,0:T(8,128)S(1)}) custom-call(s32[80]{0:T(128)S(1)} %copy-done.2, s32[1]{0:T(128)} %bitcast.refs_13_.refs_1_, bf16[80,2048]{1,0:T(8,128)(2,1)S(1)} %get-tuple-element.102.refs_2_, bf16[80,32,256]{2,1,0:T(8,128)(2,1)S(1)} %copy-done.10, ...), custom_call_target="tpu_custom_call", output_to_operand_aliasing={{0}: (6, {})} | custom-call | flops 20000000000 | bytes 1000 | tf_op jit(solution)/shard_map/grad_tokens/pallas_call | solution.py:43
  (187 shorter events, 100.2 us)
Async XLA Ops:
  8.4 10.7 %collective-permute-start.3 = (bf16[40,32,256]{2,1,0:T(8,128)(2,1)S(1)}, bf16[40,32,256]{2,1,0:T(8,128)(2,1)S(1)}, u32[]{:S(2)}, u32[]{:S(2)}) collective-permute-start(bf16[40,32,256]{2,1,0:T(8,128)(2,1)S(1)} %get-tuple-element.77.refs_4_), channel_id=1, source_target_pairs={{0,4},{1,13},{2,6},{3,15},{4,0},{5,9},{6,2},{7,11},{8,12},{9,5},{1... | collective-permute-start | bytes 1966088 | tf_op jit(solution)/shard_map/ppermute | solution.py:329
  16.0 10.7 %collective-permute-start.2 = (bf16[40,32,256]{2,1,0:T(8,128)(2,1)S(1)}, bf16[40,32,256]{2,1,0:T(8,128)(2,1)S(1)}, u32[]{:S(2)}, u32[]{:S(2)}) collective-permute-start(bf16[40,32,256]{2,1,0:T(8,128)(2,1)S(1)} %get-tuple-element.81.refs_2_), channel_id=1, source_target_pairs={{0,4},{1,13},{2,6},{3,15},{4,0},{5,9},{6,2},{7,11},{8,12},{9,5},{1... | collective-permute-start | bytes 1966088 | tf_op jit(solution)/shard_map/ppermute | solution.py:329
  19.3 11.3 %collective-permute-start.5 = (bf16[20,32,256]{2,1,0:T(8,128)(2,1)S(1)}, bf16[20,32,256]{2,1,0:T(8,128)(2,1)S(1)}, u32[]{:S(2)}, u32[]{:S(2)}) collective-permute-start(bf16[20,32,256]{2,1,0:T(8,128)(2,1)S(1)} %get-tuple-element.83.refs_2_), channel_id=1, source_target_pairs={{0,2},{1,3},{2,0},{3,1},{4,6},{5,7},{6,4},{7,5},{8,10},{9,11},{10,... | collective-permute-start | bytes 983048 | tf_op jit(solution)/shard_map/ppermute | solution.py:329
  30.7 5.4 %collective-permute-start.6 = (bf16[10,32,256]{2,1,0:T(8,128)(2,1)S(1)}, bf16[10,32,256]{2,1,0:T(8,128)(2,1)S(1)}, u32[]{:S(2)}, u32[]{:S(2)}) collective-permute-start(bf16[10,32,256]{2,1,0:T(8,128)(2,1)S(1)} %get-tuple-element.88.refs_2_), channel_id=1, source_target_pairs={{0,12},{1,5},{2,14},{3,7},{4,8},{5,1},{6,10},{7,3},{8,4},{9,13},{1... | collective-permute-start | bytes 491528 | tf_op jit(solution)/shard_map/ppermute | solution.py:329
  31.3 11.9 %collective-permute-start.4 = (bf16[20,32,256]{2,1,0:T(8,128)(2,1)S(1)}, bf16[20,32,256]{2,1,0:T(8,128)(2,1)S(1)}, u32[]{:S(2)}, u32[]{:S(2)}) collective-permute-start(bf16[20,32,256]{2,1,0:T(8,128)(2,1)S(1)} %get-tuple-element.85.refs_2_), channel_id=1, source_target_pairs={{0,2},{1,3},{2,0},{3,1},{4,6},{5,7},{6,4},{7,5},{8,10},{9,11},{10,... | collective-permute-start | bytes 983048 | tf_op jit(solution)/shard_map/ppermute | solution.py:329
  36.1 7.5 %collective-permute-start.8 = (bf16[10,32,256]{2,1,0:T(8,128)(2,1)S(1)}, bf16[10,32,256]{2,1,0:T(8,128)(2,1)S(1)}, u32[]{:S(2)}, u32[]{:S(2)}) collective-permute-start(bf16[10,32,256]{2,1,0:T(8,128)(2,1)S(1)} %add.154.refs_2_.refs_0_), channel_id=1, source_target_pairs={{0,12},{1,5},{2,14},{3,7},{4,8},{5,1},{6,10},{7,3},{8,4},{9,13},{1... | collective-permute-start | bytes 491528 | tf_op jit(solution)/shard_map/ppermute | solution.py:329
  43.3 5.4 %collective-permute-start.7 = (bf16[10,32,256]{2,1,0:T(8,128)(2,1)S(1)}, bf16[10,32,256]{2,1,0:T(8,128)(2,1)S(1)}, u32[]{:S(2)}, u32[]{:S(2)}) collective-permute-start(bf16[10,32,256]{2,1,0:T(8,128)(2,1)S(1)} %get-tuple-element.90.refs_2_), channel_id=1, source_target_pairs={{0,12},{1,5},{2,14},{3,7},{4,8},{5,1},{6,10},{7,3},{8,4},{9,13},{1... | collective-permute-start | bytes 491528 | tf_op jit(solution)/shard_map/ppermute | solution.py:329
  48.8 5.4 %collective-permute-start.9 = (bf16[10,32,256]{2,1,0:T(8,128)(2,1)S(1)}, bf16[10,32,256]{2,1,0:T(8,128)(2,1)S(1)}, u32[]{:S(2)}, u32[]{:S(2)}) collective-permute-start(bf16[10,32,256]{2,1,0:T(8,128)(2,1)S(1)} %add.156.refs_0_.refs_2_), channel_id=1, source_target_pairs={{0,12},{1,5},{2,14},{3,7},{4,8},{5,1},{6,10},{7,3},{8,4},{9,13},{1... | collective-permute-start | bytes 491528 | tf_op jit(solution)/shard_map/ppermute | solution.py:329
  49.0 12.2 %collective-permute-start.11 = (bf16[20,32,256]{2,1,0:T(8,128)(2,1)S(1)}, bf16[20,32,256]{2,1,0:T(8,128)(2,1)S(1)}, u32[]{:S(2)}, u32[]{:S(2)}) collective-permute-start(bf16[20,32,256]{2,1,0:T(8,128)(2,1)S(1)} %join.12.refs_2_.refs_0_), channel_id=1, source_target_pairs={{0,2},{1,3},{2,0},{3,1},{4,6},{5,7},{6,4},{7,5},{8,10},{9,11},{10,... | collective-permute-start | bytes 983048 | tf_op jit(solution)/shard_map/ppermute | solution.py:329
  54.2 12.3 %collective-permute-start.10 = (bf16[20,32,256]{2,1,0:T(8,128)(2,1)S(1)}, bf16[20,32,256]{2,1,0:T(8,128)(2,1)S(1)}, u32[]{:S(2)}, u32[]{:S(2)}) collective-permute-start(bf16[20,32,256]{2,1,0:T(8,128)(2,1)S(1)} %join.13.refs_2_.refs_0_), channel_id=1, source_target_pairs={{0,2},{1,3},{2,0},{3,1},{4,6},{5,7},{6,4},{7,5},{8,10},{9,11},{10,... | collective-permute-start | bytes 983048 | tf_op jit(solution)/shard_map/ppermute | solution.py:329
  61.2 11.1 %collective-permute-start.13 = (bf16[40,32,256]{2,1,0:T(8,128)(2,1)S(1)}, bf16[40,32,256]{2,1,0:T(8,128)(2,1)S(1)}, u32[]{:S(2)}, u32[]{:S(2)}) collective-permute-start(bf16[40,32,256]{2,1,0:T(8,128)(2,1)S(1)} %join.14.refs_2_.refs_0_), channel_id=1, source_target_pairs={{0,4},{1,13},{2,6},{3,15},{4,0},{5,9},{6,2},{7,11},{8,12},{9,5},{1... | collective-permute-start | bytes 1966088 | tf_op jit(solution)/shard_map/ppermute | solution.py:329
  80.0 10.6 %collective-permute-start.12 = (bf16[40,32,256]{2,1,0:T(8,128)(2,1)S(1)}, bf16[40,32,256]{2,1,0:T(8,128)(2,1)S(1)}, u32[]{:S(2)}, u32[]{:S(2)}) collective-permute-start(bf16[40,32,256]{2,1,0:T(8,128)(2,1)S(1)} %join.15.refs_2_.refs_0_), channel_id=1, source_target_pairs={{0,4},{1,13},{2,6},{3,15},{4,0},{5,9},{6,2},{7,11},{8,12},{9,5},{1... | collective-permute-start | bytes 1966088 | tf_op jit(solution)/shard_map/ppermute | solution.py:329
  82.1 12.1 %collective-permute-start.17 = (bf16[80,1024]{1,0:T(8,128)(2,1)S(1)}, bf16[80,1024]{1,0:T(8,128)(2,1)S(1)}, u32[]{:S(2)}, u32[]{:S(2)}) collective-permute-start(bf16[80,1024]{1,0:T(8,128)(2,1)S(1)} %add.157.refs_2_.refs_0_), channel_id=1, source_target_pairs={{0,4},{1,13},{2,6},{3,15},{4,0},{5,9},{6,2},{7,11},{8,12},{9,5},{1... | collective-permute-start | bytes 491528 | tf_op jit(solution)/shard_map/ppermute | solution.py:329
  98.3 7.7 %collective-permute-start.20 = (bf16[80,1024]{1,0:T(8,128)(2,1)S(1)}, bf16[80,1024]{1,0:T(8,128)(2,1)S(1)}, u32[]{:S(2)}, u32[]{:S(2)}) collective-permute-start(bf16[80,1024]{1,0:T(8,128)(2,1)S(1)} %add.158.refs_5_.refs_0_), channel_id=1, source_target_pairs={{0,2},{1,3},{2,0},{3,1},{4,6},{5,7},{6,4},{7,5},{8,10},{9,11},{10,... | collective-permute-start | bytes 491528 | tf_op jit(solution)/shard_map/ppermute | solution.py:329
  101.7 5.4 %collective-permute-start.19 = (bf16[80,1024]{1,0:T(8,128)(2,1)S(1)}, bf16[80,1024]{1,0:T(8,128)(2,1)S(1)}, u32[]{:S(2)}, u32[]{:S(2)}) collective-permute-start(bf16[80,1024]{1,0:T(8,128)(2,1)S(1)} %add.159.refs_2_.refs_0_), channel_id=1, source_target_pairs={{0,4},{1,13},{2,6},{3,15},{4,0},{5,9},{6,2},{7,11},{8,12},{9,5},{1... | collective-permute-start | bytes 491528 | tf_op jit(solution)/shard_map/ppermute | solution.py:329
  106.1 5.4 %collective-permute-start.22 = (bf16[80,1024]{1,0:T(8,128)(2,1)S(1)}, bf16[80,1024]{1,0:T(8,128)(2,1)S(1)}, u32[]{:S(2)}, u32[]{:S(2)}) collective-permute-start(bf16[80,1024]{1,0:T(8,128)(2,1)S(1)} %add.160.refs_2_.refs_0_), channel_id=1, source_target_pairs={{0,12},{1,5},{2,14},{3,7},{4,8},{5,1},{6,10},{7,3},{8,4},{9,13},{1... | collective-permute-start | bytes 491528 | tf_op jit(solution)/shard_map/ppermute | solution.py:329
  111.7 8.1 %collective-permute-start.21 = (bf16[80,1024]{1,0:T(8,128)(2,1)S(1)}, bf16[80,1024]{1,0:T(8,128)(2,1)S(1)}, u32[]{:S(2)}, u32[]{:S(2)}) collective-permute-start(bf16[80,1024]{1,0:T(8,128)(2,1)S(1)} %add.161.refs_2_.refs_0_), channel_id=1, source_target_pairs={{0,2},{1,3},{2,0},{3,1},{4,6},{5,7},{6,4},{7,5},{8,10},{9,11},{10,... | collective-permute-start | bytes 491528 | tf_op jit(solution)/shard_map/ppermute | solution.py:329
  119.1 7.9 %collective-permute-start.26 = (bf16[80,32,256]{2,1,0:T(8,128)(2,1)S(1)}, bf16[80,32,256]{2,1,0:T(8,128)(2,1)S(1)}, u32[]{:S(2)}, u32[]{:S(2)}) collective-permute-start(bf16[80,32,256]{2,1,0:T(8,128)(2,1)S(1)} %get-tuple-element.99.refs_2_), channel_id=1, source_target_pairs={{0,1},{1,0},{2,3},{3,2},{4,5},{5,4},{6,7},{7,6},{8,9},{9,8},{10,11... | collective-permute-start | bytes 3932168 | tf_op jit(solution)/shard_map/ppermute | solution.py:329
  127.4 12.5 %collective-permute-start.29 = (bf16[40,32,256]{2,1,0:T(8,128)(2,1)S(1)}, bf16[40,32,256]{2,1,0:T(8,128)(2,1)S(1)}, u32[]{:S(2)}, u32[]{:S(2)}) collective-permute-start(bf16[40,32,256]{2,1,0:T(8,128)(2,1)S(1)} %get-tuple-element.101.refs_7_), channel_id=1, source_target_pairs={{0,4},{1,13},{2,6},{3,15},{4,0},{5,9},{6,2},{7,11},{8,12},{9,5},{1... | collective-permute-start | bytes 1966088 | tf_op jit(solution)/shard_map/ppermute | solution.py:329
  138.7 10.7 %collective-permute-start.28 = (bf16[40,32,256]{2,1,0:T(8,128)(2,1)S(1)}, bf16[40,32,256]{2,1,0:T(8,128)(2,1)S(1)}, u32[]{:S(2)}, u32[]{:S(2)}) collective-permute-start(bf16[40,32,256]{2,1,0:T(8,128)(2,1)S(1)} %get-tuple-element.106.refs_2_), channel_id=1, source_target_pairs={{0,4},{1,13},{2,6},{3,15},{4,0},{5,9},{6,2},{7,11},{8,12},{9,5},{1... | collective-permute-start | bytes 1966088 | tf_op jit(solution)/shard_map/ppermute | solution.py:329
  140.0 10.7 %collective-permute-start.31 = (bf16[20,32,256]{2,1,0:T(8,128)(2,1)S(1)}, bf16[20,32,256]{2,1,0:T(8,128)(2,1)S(1)}, u32[]{:S(2)}, u32[]{:S(2)}) collective-permute-start(bf16[20,32,256]{2,1,0:T(8,128)(2,1)S(1)} %get-tuple-element.116.refs_8_), channel_id=1, source_target_pairs={{0,2},{1,3},{2,0},{3,1},{4,6},{5,7},{6,4},{7,5},{8,10},{9,11},{10,... | collective-permute-start | bytes 983048 | tf_op jit(solution)/shard_map/ppermute | solution.py:329
  152.5 11.8 %collective-permute-start.30 = (bf16[20,32,256]{2,1,0:T(8,128)(2,1)S(1)}, bf16[20,32,256]{2,1,0:T(8,128)(2,1)S(1)}, u32[]{:S(2)}, u32[]{:S(2)}) collective-permute-start(bf16[20,32,256]{2,1,0:T(8,128)(2,1)S(1)} %get-tuple-element.119.refs_2_), channel_id=1, source_target_pairs={{0,2},{1,3},{2,0},{3,1},{4,6},{5,7},{6,4},{7,5},{8,10},{9,11},{10,... | collective-permute-start | bytes 983048 | tf_op jit(solution)/shard_map/ppermute | solution.py:329
  156.2 8.8 %collective-permute-start.34 = (bf16[10,32,256]{2,1,0:T(8,128)(2,1)S(1)}, bf16[10,32,256]{2,1,0:T(8,128)(2,1)S(1)}, u32[]{:S(2)}, u32[]{:S(2)}) collective-permute-start(bf16[10,32,256]{2,1,0:T(8,128)(2,1)S(1)} %add.170.refs_2_.refs_0_), channel_id=1, source_target_pairs={{0,12},{1,5},{2,14},{3,7},{4,8},{5,1},{6,10},{7,3},{8,4},{9,13},{1... | collective-permute-start | bytes 491528 | tf_op jit(solution)/shard_map/ppermute | solution.py:329
  170.5 26.0 %collective-permute-start.39 = (bf16[1024,1024]{1,0:T(8,128)(2,1)S(1)}, bf16[1024,1024]{1,0:T(8,128)(2,1)S(1)}, u32[]{:S(2)}, u32[]{:S(2)}) collective-permute-start(bf16[1024,1024]{1,0:T(8,128)(2,1)S(1)} %get-tuple-element.126), channel_id=1, source_target_pairs={{0,32},{1,97},{2,34},{3,99},{4,36},{5,101},{6,38},{7,103},{8,40},{... | collective-permute-start | bytes 6291464 | tf_op jit(solution)/shard_map/ppermute | solution.py:337
  172.0 12.1 %collective-permute-start.37 = (bf16[20,32,256]{2,1,0:T(8,128)(2,1)S(1)}, bf16[20,32,256]{2,1,0:T(8,128)(2,1)S(1)}, u32[]{:S(2)}, u32[]{:S(2)}) collective-permute-start(bf16[20,32,256]{2,1,0:T(8,128)(2,1)S(1)} %join.18.refs_2_.refs_0_), channel_id=1, source_target_pairs={{0,2},{1,3},{2,0},{3,1},{4,6},{5,7},{6,4},{7,5},{8,10},{9,11},{10,... | collective-permute-start | bytes 983048 | tf_op jit(solution)/shard_map/ppermute | solution.py:329
  175.3 25.4 %collective-permute-start.36 = (bf16[20,32,256]{2,1,0:T(8,128)(2,1)S(1)}, bf16[20,32,256]{2,1,0:T(8,128)(2,1)S(1)}, u32[]{:S(2)}, u32[]{:S(2)}) collective-permute-start(bf16[20,32,256]{2,1,0:T(8,128)(2,1)S(1)} %join.19.refs_2_.refs_0_), channel_id=1, source_target_pairs={{0,2},{1,3},{2,0},{3,1},{4,6},{5,7},{6,4},{7,5},{8,10},{9,11},{10,... | collective-permute-start | bytes 983048 | tf_op jit(solution)/shard_map/ppermute | solution.py:329
  184.2 16.3 %collective-permute-start.38 = (bf16[40,32,256]{2,1,0:T(8,128)(2,1)S(1)}, bf16[40,32,256]{2,1,0:T(8,128)(2,1)S(1)}, u32[]{:S(2)}, u32[]{:S(2)}) collective-permute-start(bf16[40,32,256]{2,1,0:T(8,128)(2,1)S(1)} %join.20.refs_2_.refs_0_), channel_id=1, source_target_pairs={{0,4},{1,13},{2,6},{3,15},{4,0},{5,9},{6,2},{7,11},{8,12},{9,5},{1... | collective-permute-start | bytes 1966088 | tf_op jit(solution)/shard_map/ppermute | solution.py:329
  197.3 16.1 %collective-permute-start.41 = (bf16[512,1024]{1,0:T(8,128)(2,1)S(1)}, bf16[512,1024]{1,0:T(8,128)(2,1)S(1)}, u32[]{:S(2)}, u32[]{:S(2)}) collective-permute-start(bf16[512,1024]{1,0:T(8,128)(2,1)S(1)} %get-tuple-element.127.refs_2_), channel_id=1, source_target_pairs={{0,96},{1,33},{2,98},{3,35},{4,100},{5,37},{6,102},{7,39},{8,104},... | collective-permute-start | bytes 3145736 | tf_op jit(solution)/shard_map/ppermute | solution.py:337
  200.8 15.1 %collective-permute-start.40 = (bf16[40,32,256]{2,1,0:T(8,128)(2,1)S(1)}, bf16[40,32,256]{2,1,0:T(8,128)(2,1)S(1)}, u32[]{:S(2)}, u32[]{:S(2)}) collective-permute-start(bf16[40,32,256]{2,1,0:T(8,128)(2,1)S(1)} %join.22.refs_4_.refs_0_), channel_id=1, source_target_pairs={{0,4},{1,13},{2,6},{3,15},{4,0},{5,9},{6,2},{7,11},{8,12},{9,5},{1... | collective-permute-start | bytes 1966088 | tf_op jit(solution)/shard_map/ppermute | solution.py:329
  214.6 21.5 %collective-permute-start.46 = (bf16[256,1024]{1,0:T(8,128)(2,1)}, bf16[256,1024]{1,0:T(8,128)(2,1)}, u32[]{:S(2)}, u32[]{:S(2)}) collective-permute-start(bf16[256,1024]{1,0:T(8,128)(2,1)} %get-tuple-element.131.refs_2_), channel_id=1, source_target_pairs={{0,16},{1,17},{2,18},{3,19},{4,20},{5,21},{6,22},{7,23},{8,24},{9,... | collective-permute-start | bytes 1572872 | tf_op jit(solution)/shard_map/ppermute | solution.py:337
  224.8 6.6 %collective-permute-start.45 = (f32[40,128]{1,0:T(8,128)S(1)}, f32[40,128]{1,0:T(8,128)S(1)}, u32[]{:S(2)}, u32[]{:S(2)}) collective-permute-start(f32[40,128]{1,0:T(8,128)S(1)} %add.175.refs_7_.refs_0_), channel_id=1, source_target_pairs={{0,96},{1,33},{2,98},{3,35},{4,100},{5,37},{6,102},{7,39},{8,104},... | collective-permute-start | bytes 61448 | tf_op jit(solution)/shard_map/ppermute | solution.py:337
  231.5 6.8 %collective-permute-start.47 = (f32[40,128]{1,0:T(8,128)S(1)}, f32[40,128]{1,0:T(8,128)S(1)}, u32[]{:S(2)}, u32[]{:S(2)}) collective-permute-start(f32[40,128]{1,0:T(8,128)S(1)} %add.176.refs_7_.refs_0_), channel_id=1, source_target_pairs={{0,16},{1,17},{2,18},{3,19},{4,20},{5,21},{6,22},{7,23},{8,24},{9,... | collective-permute-start | bytes 61448 | tf_op jit(solution)/shard_map/ppermute | solution.py:337
  (45 other events, 368.3 us)
